TPU v7x, 32 devices: a whole 2x2x4 slice. The times are simulated.
32 devices in a mesh: field: 2 (over x), slab: 16 (over z, y, core).
Axes of the slice: x: 2, y: 2, z: 4, core: 2. Of those that a mesh axis runs over, the one named last changes fastest.
Arguments:
- right_side: float32 [128, 64, 512], P(('field', 'slab')), parts along dimension 0, may hold values from -7.3 to 8
- cond_x: float32 [64, 64, 512], P('slab'), may hold values from 0.2 to 5
- cond_y: float32 [64, 64, 512], P('slab'), may hold values from 0.2 to 5
- cond_z: float32 [64, 64, 512], P('slab'), may hold values from 0.2 to 5
- kappa_sq: float32 [64, 64, 512], P('slab'), may hold values from 0.05 to 2
- shifts: float32 [8], replicated, may hold values from 0.01 to 20
- weights: float32 [8], replicated, may hold values from 0.3 to 3
Outputs:
- matern_field: float32 [128, 64, 512], P(('field', 'slab')), parts along dimension 0
There are 2 independent parts, one for each index of `field`. A program takes and returns all parts, laid end to end along the dimension named above; an argument that names none is the same for every part. Nothing has to cross between parts.
All inputs are finite; a program needn't handle non-finite values.
Results may differ from a plain program's by a relative error of at most 0.0001.
Values sent between devices are 32-bit elements; how exact they have to be, the bound alone decides.
No kernel may reach another device: no remote copies, remote signals or barrier semaphores. Data moves between devices by JAX's collectives and lax.ppermute only.
A program may use at most 64 MiB of HBM per device.

v0:
```python
import jax
import jax.numpy as jnp
from jax import lax
from jax.sharding import PartitionSpec as P

ITERS = 3


def padded_2(cells, sides, width):
    for axis, dim in sides:
        count = lax.axis_size(axis)
        ends = count - 1
        head = lax.slice_in_dim(cells, 0, width, axis=dim)
        tail = lax.slice_in_dim(cells, cells.shape[dim] - width, cells.shape[dim], axis=dim)
        cells = jnp.concatenate(
            [
                lax.ppermute(tail, axis, [(i, (i + 1) % count) for i in range(ends)]),
                cells,
                lax.ppermute(head, axis, [((i + 1) % count, i) for i in range(ends)]),
            ],
            axis=dim,
        )
    return cells


def face_pair(values, axis):
    count = values.shape[axis]
    widths = [(1, 1) if number == axis else (0, 0) for number in range(values.ndim)]
    padded = jnp.pad(values, widths)
    faces = 0.5 * (
        lax.slice_in_dim(padded, 0, count + 1, axis=axis)
        + lax.slice_in_dim(padded, 1, count + 2, axis=axis)
    )
    return (
        lax.slice_in_dim(faces, 0, count, axis=axis),
        lax.slice_in_dim(faces, 1, count + 1, axis=axis),
    )


def neighbours(field, axis, low, high):
    count = field.shape[axis]
    widths = [(1, 1) if number == axis else (0, 0) for number in range(field.ndim)]
    padded = jnp.pad(field, widths)
    return low * lax.slice_in_dim(padded, 0, count, axis=axis) + high * lax.slice_in_dim(
        padded, 2, count + 2, axis=axis
    )


def operate_exchanged(field, shifted_diag, coefficients):
    low_x, high_x, low_z, high_z, low_y, high_y = coefficients
    padded = padded_2(field, (("slab", 1),), 1)
    result = shifted_diag * field - (low_x * padded[:, :-2] + high_x * padded[:, 2:])
    result = result - neighbours(field, 2, low_z, high_z)
    result = result - neighbours(field, 3, low_y, high_y)
    return result


def expand(scalars):
    return scalars[:, None, None, None]


def on_device(right_side, cond_x, cond_y, cond_z, kappa_sq, shifts, weights):
    padded_cond = padded_2(cond_x, (("slab", 0),), 1)
    faces_x = 0.5 * (padded_cond[:-1] + padded_cond[1:])
    low_x, high_x = (faces_x[:-1], faces_x[1:])
    low_z, high_z = face_pair(cond_z, 1)
    low_y, high_y = face_pair(cond_y, 2)
    diagonal = kappa_sq + low_x + high_x + low_z + high_z + low_y + high_y
    coefficients = (low_x, high_x, low_z, high_z, low_y, high_y)

    def inner_sum(first, second):
        return jnp.sum(first * second, axis=(1, 2, 3))

    def precond_total(residual, precond):
        return lax.psum(inner_sum(residual, precond), "slab")

    shifted_diag = diagonal[None] + expand(shifts)
    residual = jnp.broadcast_to(right_side[None], shifted_diag.shape)
    iterate = jnp.zeros_like(shifted_diag)
    precond = residual / shifted_diag
    direction = precond
    norm_now = precond_total(residual, precond)
    for number in range(ITERS):
        image = operate_exchanged(direction, shifted_diag, coefficients)
        product = lax.psum(inner_sum(direction, image), "slab")
        step_size = norm_now / product
        iterate = iterate + expand(step_size) * direction
        residual = residual - expand(step_size) * image
        if number + 1 < ITERS:
            precond = residual / shifted_diag
            norm_next = precond_total(residual, precond)
            direction = precond + expand(norm_next / norm_now) * direction
            norm_now = norm_next
    return jnp.sum(expand(weights) * iterate, axis=0)


def solution(mesh):
    return jax.shard_map(
        on_device,
        mesh=mesh,
        in_specs=(
            P(("field", "slab"), None, None),
            P("slab", None, None),
            P("slab", None, None),
            P("slab", None, None),
            P("slab", None, None),
            P(),
            P(),
        ),
        out_specs=P(("field", "slab"), None, None),
        check_vma=False,
    )
```

profile of v0, /device:TPU:0, one launch (start us, length us, event | category | flops | bytes accessed | tf_op | source)
XLA Modules:
  0.0 287.8 jit_solution(5409053457591726921)
XLA Ops:
  0.0 1.0 fusion.47
  1.0 1.3 collective-permute-start.1
  2.3 3.0 %collective-permute-start = (f32[1,64,512]{2,1,0:T(8,128)S(1)}, f32[1,64,512]{2,1,0:T(8,128)S(1)}, u32[]{:S(2)}, u32[]{:S(2)}) collective-permute-start(f32[1,64,512]{2,1,0:T(8,128)S(1)} %get-tuple-element.26), channel_id=1, source_target_pairs={{0,1},{1,2},{2,3},{3,4},{4,5},{5,6},{6,7},{7,8},{8,9},{9,10},{10,1... | collective-permute-start | bytes 393224 | tf_op jit(solution)/shard_map/ppermute | solution.py:17
  5.4 1.3 add_multiply_fusion.3
  6.7 1.5 fusion.39
  8.3 1.4 fusion.40
  9.6 1.7 fusion.46
  11.4 0.9 add_divide_fusion.2
  12.5 5.5 %collective-permute-start.2 = (f32[8,1,64,512]{3,2,1,0:T(8,128)S(1)}, f32[8,1,64,512]{3,2,1,0:T(8,128)}, u32[]{:S(2)}, u32[]{:S(2)}) collective-permute-start(f32[8,1,64,512]{3,2,1,0:T(8,128)S(1)} %get-tuple-element.16), channel_id=1, source_target_pairs={{0,1},{1,2},{2,3},{3,4},{4,5},{5,6},{6,7},{7,8},{8,9},{9,10},{10,1... | collective-permute-start | bytes 3145736 | tf_op jit(solution)/shard_map/ppermute | solution.py:17
  18.0 1.3 collective-permute-start.3
  19.4 3.7 %collective-permute-done.3 = f32[8,1,64,512]{3,2,1,0:T(8,128)} collective-permute-done((f32[8,1,64,512]{3,2,1,0:T(8,128)S(1)}, f32[8,1,64,512]{3,2,1,0:T(8,128)}, u32[]{:S(2)}, u32[]{:S(2)}) %collective-permute-start.3) | collective-permute-done | bytes 1048608 | tf_op jit(solution)/shard_map/ppermute | solution.py:19
  23.1 8.9 %multiply_reduce_fusion.4 = (f32[8]{0:T(128)S(1)}, f32[8]{0:T(128)S(1)}, f32[8,4,64,512]{3,2,1,0:T(8,128)}) fusion(f32[8]{0:T(128)S(1)} %copy-done.8, f32[4,64,512]{2,1,0:T(8,128)S(1)} %get-tuple-element.19, f32[4,64,512]{2,1,0:T(8,128)S(1)} %copy-done.1, f32[4,64,512]{2,1,0:T(8,128)} %get-tuple-element.21, f32[8,4,64,512]{3,2,1,0:T(8,128)S(1)} %add_divide_fusion.2, ...), kind=kLoop, calls=%fused_computation.70 | loop fusion | flops 22020080 | bytes 14680160 | tf_op jit(solution)/shard_map/reduce_sum | solution.py:72
  31.9 51.0 %all-reduce.8 = (f32[8]{0:T(128)S(1)}, f32[8]{0:T(128)S(1)}) all-reduce(f32[8]{0:T(128)S(1)} %get-tuple-element.6, f32[8]{0:T(128)S(1)} %get-tuple-element.5), channel_id=1, replica_groups=mesh['field'=2,'slab'=16] {'slab'}, use_global_device_ids=true, to_apply=%region_1.2 | all-reduce | flops 16 | bytes 128 | tf_op jit(solution)/shard_map/psum | solution.py:75
  82.9 3.3 %multiply_reduce_fusion.3 = f32[8]{0:T(128)S(1)} fusion(f32[8,4,64,512]{3,2,1,0:T(8,128)} %get-tuple-element.11, f32[8]{0:T(128)S(1)} %div.25, f32[8]{0:T(128)S(1)} %copy-done.8, f32[4,64,512]{2,1,0:T(8,128)S(1)} %get-tuple-element.19, f32[4,64,512]{2,1,0:T(8,128)S(1)} %copy-done.1), kind=kLoop, calls=%fused_computation.68 | loop fusion | flops 6291448 | bytes 5242976 | tf_op jit(solution)/shard_map/reduce_sum | solution.py:72
  86.2 29.5 %psum.44 = f32[8]{0:T(128)S(1)} all-reduce(f32[8]{0:T(128)S(1)} %multiply_reduce_fusion.3), channel_id=1, replica_groups=mesh['field'=2,'slab'=16] {'slab'}, use_global_device_ids=true, to_apply=%region_5.6 | all-reduce | flops 8 | bytes 64 | tf_op jit(solution)/shard_map/psum | solution.py:75
  115.7 3.3 %multiply_add_fusion.1 = f32[8,4,64,512]{3,2,1,0:T(8,128)S(1)} fusion(f32[8,4,64,512]{3,2,1,0:T(8,128)} %get-tuple-element.11, f32[8]{0:T(128)S(1)} %div.27, f32[8]{0:T(128)S(1)} %div.25, f32[8]{0:T(128)S(1)} %copy-done.8, f32[4,64,512]{2,1,0:T(8,128)S(1)} %get-tuple-element.19, f32[4,64,512]{2,1,0:T(8,128)S(1)} %copy-done.1), kind=kLoop, calls=%fused_computation.67 | loop fusion | flops 7340032 | bytes 9437280 | tf_op jit(solution)/shard_map/add | solution.py:92
  119.3 2.9 %collective-permute-start.4 = (f32[8,1,64,512]{3,2,1,0:T(8,128)S(1)}, f32[8,1,64,512]{3,2,1,0:T(8,128)}, u32[]{:S(2)}, u32[]{:S(2)}) collective-permute-start(f32[8,1,64,512]{3,2,1,0:T(8,128)S(1)} %get-tuple-element.14), channel_id=1, source_target_pairs={{0,1},{1,2},{2,3},{3,4},{4,5},{5,6},{6,7},{7,8},{8,9},{9,10},{10,1... | collective-permute-start | bytes 3145736 | tf_op jit(solution)/shard_map/ppermute | solution.py:17
  122.2 1.3 collective-permute-start.5
  123.6 3.2 %collective-permute-done.5 = f32[8,1,64,512]{3,2,1,0:T(8,128)} collective-permute-done((f32[8,1,64,512]{3,2,1,0:T(8,128)S(1)}, f32[8,1,64,512]{3,2,1,0:T(8,128)}, u32[]{:S(2)}, u32[]{:S(2)}) %collective-permute-start.5) | collective-permute-done | bytes 1048608 | tf_op jit(solution)/shard_map/ppermute | solution.py:19
  126.9 8.2 %multiply_reduce_fusion.2 = (f32[8]{0:T(128)S(1)}, f32[8,4,64,512]{3,2,1,0:T(8,128)}) fusion(f32[8,4,64,512]{3,2,1,0:T(8,128)S(1)} %multiply_add_fusion.1, f32[4,64,512]{2,1,0:T(8,128)S(1)} %copy-done.2, f32[4,64,512]{2,1,0:T(8,128)S(1)} %get-tuple-element.20, f32[4,64,512]{2,1,0:T(8,128)} %get-tuple-element.24, f32[4,64,512]{2,1,0:T(8,128)S(1)} %copy-done.4, ...), kind=kLoop, calls=%fused_computation.66 | loop fusion | flops 18874360 | bytes 14155840 | tf_op jit(solution)/shard_map/reduce_sum | solution.py:72
  135.1 46.8 %psum.45 = f32[8]{0:T(128)S(1)} all-reduce(f32[8]{0:T(128)S(1)} %get-tuple-element.9), channel_id=1, replica_groups=mesh['field'=2,'slab'=16] {'slab'}, use_global_device_ids=true, to_apply=%region_7.8 | all-reduce | flops 8 | bytes 64 | tf_op jit(solution)/shard_map/psum | solution.py:85
  181.9 4.9 %multiply_reduce_fusion.1 = f32[8]{0:T(128)S(1)} fusion(f32[8,4,64,512]{3,2,1,0:T(8,128)} %get-tuple-element.10, f32[8]{0:T(128)S(1)} %div.28, f32[8,4,64,512]{3,2,1,0:T(8,128)} %get-tuple-element.11, f32[8]{0:T(128)S(1)} %div.25, f32[8]{0:T(128)S(1)} %copy-done.8, f32[4,64,512]{2,1,0:T(8,128)S(1)} %get-tuple-element.19, f32[4,64,512]{2,1,0:T(8,128)S(1)} %copy-done.1), kind=kLoop, calls=%fused_computation.64 | loop fusion | flops 8388600 | bytes 9437312 | tf_op jit(solution)/shard_map/reduce_sum | solution.py:72
  186.8 29.7 %psum.46 = f32[8]{0:T(128)S(1)} all-reduce(f32[8]{0:T(128)S(1)} %multiply_reduce_fusion.1), channel_id=1, replica_groups=mesh['field'=2,'slab'=16] {'slab'}, use_global_device_ids=true, to_apply=%region_9.10 | all-reduce | flops 8 | bytes 64 | tf_op jit(solution)/shard_map/psum | solution.py:75
  216.4 4.4 %multiply_add_fusion = f32[8,4,64,512]{3,2,1,0:T(8,128)S(1)} fusion(f32[8]{0:T(128)S(1)} %div.30, f32[8,4,64,512]{3,2,1,0:T(8,128)} %get-tuple-element.10, f32[8]{0:T(128)S(1)} %div.28, f32[8,4,64,512]{3,2,1,0:T(8,128)} %get-tuple-element.11, f32[8]{0:T(128)S(1)} %div.25, f32[8]{0:T(128)S(1)} %copy-done.8, f32[4,64,512]{2,1,0:T(8,128)S(1)} %get-tuple-element.19, ...), kind=kLoop, calls=%fused_computation.63 | loop fusion | flops 12582912 | bytes 13631648 | tf_op jit(solution)/shard_map/add | solution.py:92
  220.9 0.3 fusion.43
  221.2 2.1 collective-permute-start.6
  223.3 1.3 collective-permute-start.7
  224.6 0.9 collective-permute-done.6
  225.5 2.5 collective-permute-done.7
  228.0 6.7 %fusion.15 = f32[8]{0:T(128)S(1)} fusion(f32[8,4,64,512]{3,2,1,0:T(8,128)S(1)} %multiply_add_fusion, f32[8,1,64,512]{3,2,1,0:T(8,128)} %collective-permute-done.7, f32[8,1,64,512]{3,2,1,0:T(8,128)S(1)} %collective-permute-done.6, f32[4,64,512]{2,1,0:T(8,128)S(1)} %copy-done.2, f32[4,64,512]{2,1,0:T(8,128)S(1)} %get-tuple-element.20, ...), kind=kLoop, calls=%fused_computation.33 | loop fusion | flops 18874360 | bytes 9961536 | tf_op jit(solution)/shard_map/reduce_sum | solution.py:72
  234.7 47.7 %psum.47 = f32[8]{0:T(128)S(1)} all-reduce(f32[8]{0:T(128)S(1)} %fusion.15), channel_id=1, replica_groups=mesh['field'=2,'slab'=16] {'slab'}, use_global_device_ids=true, to_apply=%region_11.12 | all-reduce | flops 8 | bytes 64 | tf_op jit(solution)/shard_map/psum | solution.py:85
  282.4 5.4 %multiply_reduce_fusion = f32[4,64,512]{2,1,0:T(8,128)} fusion(f32[8,4,64,512]{3,2,1,0:T(8,128)} %copy-done, f32[8]{0:T(128)S(1)} %div.31, f32[8]{0:T(128)S(1)} %div.28, f32[8]{0:T(128)S(1)} %div.25, f32[8]{0:T(128)S(1)} %copy-done.8, f32[4,64,512]{2,1,0:T(8,128)S(1)} %get-tuple-element.19, f32[4,64,512]{2,1,0:T(8,128)S(1)} %copy-done.1, f32[8]{0:T(128)S(1)} %copy-done.9, ...), kind=kLoop, calls=%fused_computation.62 | loop fusion | flops 14548992 | bytes 9961664 | tf_op jit(solution)/shard_map/reduce_sum | solution.py:94
  (31 shorter events, 0.8 us)
Async XLA Ops:
  0.0 9.6 %copy-start.7 = (f32[4,64,512]{2,1,0:T(8,128)S(1)}, f32[4,64,512]{2,1,0:T(8,128)}, u32[]{:S(2)}) copy-start(f32[4,64,512]{2,1,0:T(8,128)} %param.11) | copy-start | bytes 1572868
  1.0 7.2 %collective-permute-start.1 = (f32[1,64,512]{2,1,0:T(8,128)S(1)}, f32[1,64,512]{2,1,0:T(8,128)S(1)}, u32[]{:S(2)}, u32[]{:S(2)}) collective-permute-start(f32[1,64,512]{2,1,0:T(8,128)S(1)} %get-tuple-element.25), channel_id=1, source_target_pairs={{1,0},{2,1},{3,2},{4,3},{5,4},{6,5},{7,6},{8,7},{9,8},{10,9},{11,1... | collective-permute-start | bytes 393224 | tf_op jit(solution)/shard_map/ppermute | solution.py:19
  2.3 5.9 %collective-permute-start = (f32[1,64,512]{2,1,0:T(8,128)S(1)}, f32[1,64,512]{2,1,0:T(8,128)S(1)}, u32[]{:S(2)}, u32[]{:S(2)}) collective-permute-start(f32[1,64,512]{2,1,0:T(8,128)S(1)} %get-tuple-element.26), channel_id=1, source_target_pairs={{0,1},{1,2},{2,3},{3,4},{4,5},{5,6},{6,7},{7,8},{8,9},{9,10},{10,1... | collective-permute-start | bytes 393224 | tf_op jit(solution)/shard_map/ppermute | solution.py:17
  8.2 3.2 %copy-start.1 = (f32[4,64,512]{2,1,0:T(8,128)S(1)}, f32[4,64,512]{2,1,0:T(8,128)}, u32[]{:S(2)}) copy-start(f32[4,64,512]{2,1,0:T(8,128)} %param.7) | copy-start | bytes 1572868
  8.2 3.1 %copy-start.8 = (f32[8]{0:T(128)S(1)}, f32[8]{0:T(128)}, u32[]{:S(2)}) copy-start(f32[8]{0:T(128)} %param.12) | copy-start | bytes 100
  12.5 6.9 %collective-permute-start.2 = (f32[8,1,64,512]{3,2,1,0:T(8,128)S(1)}, f32[8,1,64,512]{3,2,1,0:T(8,128)}, u32[]{:S(2)}, u32[]{:S(2)}) collective-permute-start(f32[8,1,64,512]{3,2,1,0:T(8,128)S(1)} %get-tuple-element.16), channel_id=1, source_target_pairs={{0,1},{1,2},{2,3},{3,4},{4,5},{5,6},{6,7},{7,8},{8,9},{9,10},{10,1... | collective-permute-start | bytes 3145736 | tf_op jit(solution)/shard_map/ppermute | solution.py:17
  18.0 5.1 %collective-permute-start.3 = (f32[8,1,64,512]{3,2,1,0:T(8,128)S(1)}, f32[8,1,64,512]{3,2,1,0:T(8,128)}, u32[]{:S(2)}, u32[]{:S(2)}) collective-permute-start(f32[8,1,64,512]{3,2,1,0:T(8,128)S(1)} %get-tuple-element.17), channel_id=1, source_target_pairs={{1,0},{2,1},{3,2},{4,3},{5,4},{6,5},{7,6},{8,7},{9,8},{10,9},{11,1... | collective-permute-start | bytes 3145736 | tf_op jit(solution)/shard_map/ppermute | solution.py:19
  119.1 7.8 %copy-start.2 = (f32[4,64,512]{2,1,0:T(8,128)S(1)}, f32[4,64,512]{2,1,0:T(8,128)}, u32[]{:S(2)}) copy-start(f32[4,64,512]{2,1,0:T(8,128)} %get-tuple-element.21) | copy-start | bytes 1572868
  119.1 7.8 %copy-start.3 = (f32[4,64,512]{2,1,0:T(8,128)S(1)}, f32[4,64,512]{2,1,0:T(8,128)}, u32[]{:S(2)}) copy-start(f32[4,64,512]{2,1,0:T(8,128)} %get-tuple-element.22) | copy-start | bytes 1572868
  119.1 7.8 %copy-start.4 = (f32[4,64,512]{2,1,0:T(8,128)S(1)}, f32[4,64,512]{2,1,0:T(8,128)}, u32[]{:S(2)}) copy-start(f32[4,64,512]{2,1,0:T(8,128)} %get-tuple-element.23) | copy-start | bytes 1572868
  119.3 4.3 %collective-permute-start.4 = (f32[8,1,64,512]{3,2,1,0:T(8,128)S(1)}, f32[8,1,64,512]{3,2,1,0:T(8,128)}, u32[]{:S(2)}, u32[]{:S(2)}) collective-permute-start(f32[8,1,64,512]{3,2,1,0:T(8,128)S(1)} %get-tuple-element.14), channel_id=1, source_target_pairs={{0,1},{1,2},{2,3},{3,4},{4,5},{5,6},{6,7},{7,8},{8,9},{9,10},{10,1... | collective-permute-start | bytes 3145736 | tf_op jit(solution)/shard_map/ppermute | solution.py:17
  122.2 4.7 %collective-permute-start.5 = (f32[8,1,64,512]{3,2,1,0:T(8,128)S(1)}, f32[8,1,64,512]{3,2,1,0:T(8,128)}, u32[]{:S(2)}, u32[]{:S(2)}) collective-permute-start(f32[8,1,64,512]{3,2,1,0:T(8,128)S(1)} %get-tuple-element.15), channel_id=1, source_target_pairs={{1,0},{2,1},{3,2},{4,3},{5,4},{6,5},{7,6},{8,7},{9,8},{10,9},{11,1... | collective-permute-start | bytes 3145736 | tf_op jit(solution)/shard_map/ppermute | solution.py:19
  220.9 7.1 %copy-start = (f32[8,4,64,512]{3,2,1,0:T(8,128)}, f32[8,4,64,512]{3,2,1,0:T(8,128)S(1)}, u32[]{:S(2)}) copy-start(f32[8,4,64,512]{3,2,1,0:T(8,128)S(1)} %multiply_add_fusion) | copy-start | bytes 12582916
  220.9 7.1 %copy-start.5 = (f32[4,64,512]{2,1,0:T(8,128)S(1)}, f32[4,64,512]{2,1,0:T(8,128)}, u32[]{:S(2)}) copy-start(f32[4,64,512]{2,1,0:T(8,128)} %get-tuple-element.23) | copy-start | bytes 1572868
  220.9 7.1 %copy-start.6 = (f32[4,64,512]{2,1,0:T(8,128)S(1)}, f32[4,64,512]{2,1,0:T(8,128)}, u32[]{:S(2)}) copy-start(f32[4,64,512]{2,1,0:T(8,128)} %get-tuple-element.24) | copy-start | bytes 1572868
  221.2 4.3 %collective-permute-start.6 = (f32[8,1,64,512]{3,2,1,0:T(8,128)S(1)}, f32[8,1,64,512]{3,2,1,0:T(8,128)S(1)}, u32[]{:S(2)}, u32[]{:S(2)}) collective-permute-start(f32[8,1,64,512]{3,2,1,0:T(8,128)S(1)} %get-tuple-element.12), channel_id=1, source_target_pairs={{0,1},{1,2},{2,3},{3,4},{4,5},{5,6},{6,7},{7,8},{8,9},{9,10},{10,1... | collective-permute-start | bytes 3145736 | tf_op jit(solution)/shard_map/ppermute | solution.py:17
  223.3 59.1 %copy-start.9 = (f32[8]{0:T(128)S(1)}, f32[8]{0:T(128)}, u32[]{:S(2)}) copy-start(f32[8]{0:T(128)} %param.13) | copy-start | bytes 100
  223.3 4.7 %collective-permute-start.7 = (f32[8,1,64,512]{3,2,1,0:T(8,128)S(1)}, f32[8,1,64,512]{3,2,1,0:T(8,128)}, u32[]{:S(2)}, u32[]{:S(2)}) collective-permute-start(f32[8,1,64,512]{3,2,1,0:T(8,128)S(1)} %get-tuple-element.13), channel_id=1, source_target_pairs={{1,0},{2,1},{3,2},{4,3},{5,4},{6,5},{7,6},{8,7},{9,8},{10,9},{11,1... | collective-permute-start | bytes 3145736 | tf_op jit(solution)/shard_map/ppermute | solution.py:19
where the time goes:
time: 289 us; the launch traced here: 288 us
  blocking collectives  205 us (71%)
  other arithmetic  52 us (18%)
  starting transfers between devices  18.7 us (6%)
  waiting for transfers between devices  10.5 us (4%)
    psum x3, blocking collectives, precond_total(): return lax.psum(inner_sum(residual, precond), 'slab')  110 us
    psum x2, blocking collectives, on_device(): product = lax.psum(inner_sum(direction, image), 'slab')  94.5 us
    reduce_sum x5, other arithmetic, inner_sum(): return jnp.sum(first * second, axis=(1, 2, 3))  32 us
    ppermute x4, starting transfers between devices, padded_2(): lax.ppermute(tail, axis, [(i, (i + 1) % count) for i in range(ends)])  13.5 us
    ppermute x4, waiting for transfers between devices, padded_2(): lax.ppermute(head, axis, [((i + 1) % count, i) for i in range(ends)])  9.42 us
    add x2, other arithmetic, on_device(): direction = precond + expand(norm_next / norm_now) * direction  7.79 us
  transfers between devices with their start and end apart: 8, of which 6 were waited for; matrix products, arithmetic and copies ran while one was open for 1% of the time, Pallas kernels for 0%

commit v1 on v0

v1 whole, which is shorter than its diff:
```python
import functools
import jax
import jax.numpy as jnp
from jax import lax
from jax.experimental import pallas as pl
from jax.experimental.pallas import tpu as pltpu
from jax.sharding import PartitionSpec as P

LANES = 128
PAD = 8
VMEM_LIMIT = 52 * 1024 * 1024


class Dims:
    def __init__(self, shape):
        self.nl, self.nz, self.ny = shape
        self.nc = self.ny // LANES
        self.plane = self.nc * self.nz
        self.half = self.nz // 2
        self.more = self.half + 8
        self.own = self.nl * self.plane
        self.np = self.nl + 6
        self.rows = self.np * self.plane + 2 * PAD
        names = ["b1", "d1", "x1", "fy1", "fz1", "d2", "b2", "fx2"]
        sizes = [self.plane] * 8 + [self.nc * self.half] * 3 + [self.nc * self.more]
        self.at = {}
        total = 0
        for name, size in zip(names + ["fy2", "d3", "g3", "fz2"], sizes):
            self.at[name] = total
            total += size
        self.sent = total


def lane_ids():
    return lax.broadcasted_iota(jnp.int32, (8, LANES), 1)


def row_ids():
    return lax.broadcasted_iota(jnp.int32, (8, LANES), 0)


def from_higher(tiles):
    lane = lane_ids()
    n = len(tiles)
    return [
        pltpu.roll(jnp.where(lane == 0, tiles[(c + 1) % n], tiles[c]), LANES - 1, 1)
        for c in range(n)
    ]


def from_lower(tiles):
    lane = lane_ids()
    n = len(tiles)
    return [
        pltpu.roll(jnp.where(lane == LANES - 1, tiles[(c - 1) % n], tiles[c]), 1, 1)
        for c in range(n)
    ]


def prepare(dm, par, cx, cy, cz, kappa, b, bf, df, xf, yf, zf, first):
    nc, nz, nl = dm.nc, dm.nz, dm.nl
    lane = lane_ids()
    sub = row_ids()

    def layer(p):
        return jnp.where(par == 0, p, nl - 1 - p)

    for p in range(nl):
        at = layer(p)

        def copy(zb, carry, at=at, p=p):
            z = pl.multiple_of(zb * 8, 8)
            base = PAD + (first + p) * dm.plane
            blocks = [ref[at, pl.ds(z, 8), :] for ref in (b, cx, cz)]
            for block, dst in zip(blocks, (bf, xf, zf)):
                for c in range(nc):
                    dst[pl.ds(base + c * nz + z, 8), :] = block[:, c * LANES : (c + 1) * LANES]
            return carry

        lax.fori_loop(0, nz // 8, copy, 0)

    for p in range(nl):
        at = layer(p)

        def faces(zb, carry, at=at, p=p):
            z = pl.multiple_of(zb * 8, 8)
            base = PAD + (first + p) * dm.plane
            conds = cy[at, pl.ds(z, 8), :]
            kap = kappa[at, pl.ds(z, 8), :]
            ys = [conds[:, c * LANES : (c + 1) * LANES] for c in range(nc)]
            up, down = from_higher(ys), from_lower(ys)
            up[-1] = jnp.where(lane == LANES - 1, 0.0, up[-1])
            down[0] = jnp.where(lane == 0, 0.0, down[0])
            for c in range(nc):
                row = base + c * nz + z
                high_y = 0.5 * (ys[c] + up[c])
                low_y = 0.5 * (ys[c] + down[c])
                here = zf[pl.ds(row, 8), :]
                above = zf[pl.ds(row + 1, 8), :]
                below = zf[pl.ds(row - 1, 8), :]
                high_z = 0.5 * (here + jnp.where(sub + z == nz - 1, 0.0, above))
                low_z = 0.5 * (here + jnp.where(sub + z == 0, 0.0, below))
                total = kap[:, c * LANES : (c + 1) * LANES]
                mine = xf[pl.ds(row, 8), :]
                if p > 0:
                    total = total + 0.5 * (mine + xf[pl.ds(row - dm.plane, 8), :])
                else:
                    total = total + 0.5 * mine
                if p < nl - 1:
                    total = total + 0.5 * (mine + xf[pl.ds(row + dm.plane, 8), :])
                else:
                    total = total + 0.5 * mine
                df[pl.ds(row, 8), :] = total + low_z + high_z + low_y + high_y
                if c == nc - 1:
                    high_y = jnp.where(lane == LANES - 1, 0.0, high_y)
                yf[pl.ds(row, 8), :] = high_y
            return carry

        lax.fori_loop(0, nz // 8, faces, 0)

    for p in range(nl):

        def faces_z(zb, carry, p=p):
            z = pl.multiple_of(zb * 8, 8)
            for c in range(nc):
                row = PAD + (first + p) * dm.plane + c * nz + z
                face = 0.5 * (zf[pl.ds(row, 8), :] + zf[pl.ds(row + 1, 8), :])
                zf[pl.ds(row, 8), :] = jnp.where(sub + z == nz - 1, 0.0, face)
            return carry

        lax.fori_loop(0, nz // 8, faces_z, 0)


def pack_body(dm, cx, cy, cz, kappa, b, to_off, to_in, bf, df, xf, yf, zf):
    par = lax.rem(lax.axis_index("slab"), 2)
    nc, nz, nl = dm.nc, dm.nz, dm.nl
    prepare(dm, par, cx, cy, cz, kappa, b, bf, df, xf, yf, zf, 0)
    at = dm.at
    other = 1 - par

    for out, edge, step in ((to_off, 0, 1), (to_in, nl - 1, -1)):

        def row_of(p):
            return PAD + p * dm.plane

        def put(name, ref, p, out=out, row_of=row_of):
            out[at[name] : at[name] + dm.plane, :] = ref[row_of(p) : row_of(p) + dm.plane, :]

        second, third = edge + step, edge + 2 * step
        put("b1", bf, edge)
        put("d1", df, edge)
        put("x1", xf, edge)
        put("fy1", yf, edge)
        put("fz1", zf, edge)
        put("d2", df, second)
        put("b2", bf, second)
        e, s, t = row_of(edge), row_of(second), row_of(third)
        out[at["fx2"] : at["fx2"] + dm.plane, :] = 0.5 * (
            xf[e : e + dm.plane, :] + xf[s : s + dm.plane, :]
        )
        for c in range(nc):
            z = pl.multiple_of(other * dm.half, 8) + c * nz
            z2 = pl.multiple_of(other * (nz - dm.more), 8) + c * nz
            h = c * dm.half
            out[at["fy2"] + h : at["fy2"] + h + dm.half, :] = yf[pl.ds(s + z, dm.half), :]
            out[at["d3"] + h : at["d3"] + h + dm.half, :] = df[pl.ds(t + z, dm.half), :]
            out[at["g3"] + h : at["g3"] + h + dm.half, :] = (
                0.5
                * (xf[pl.ds(s + z, dm.half), :] + xf[pl.ds(t + z, dm.half), :])
                * bf[pl.ds(t + z, dm.half), :]
            )
            h = c * dm.more
            out[at["fz2"] + h : at["fz2"] + h + dm.more, :] = zf[pl.ds(s + z2, dm.more), :]


def basis_body(
    dm, nk, cx, cy, cz, kappa, b, from_off, from_in, shifts, w0_out, w1_out, w2_out, moments,
    bf, df, xf, yf, zf, rf, w0, w1, w2, acc, sems,
):
    index = lax.axis_index("slab")
    count = lax.axis_size("slab")
    par = lax.rem(index, 2)
    has_off = jnp.where(jnp.logical_and(index > 0, index < count - 1), 1.0, 0.0)
    nc, nz, nl, plane = dm.nc, dm.nz, dm.nl, dm.plane
    at = dm.at
    first = 3
    last = first + nl - 1

    def row_of(i):
        return PAD + i * plane

    for ref in (bf, df, xf, yf, zf):
        ref[0:PAD, :] = jnp.zeros((PAD, LANES), jnp.float32)
        ref[dm.rows - PAD :, :] = jnp.zeros((PAD, LANES), jnp.float32)
    prepare(dm, par, cx, cy, cz, kappa, b, bf, df, xf, yf, zf, first)
    acc[...] = jnp.zeros(acc.shape, jnp.float32)
    for ref in (w0, w1, w2):
        rows = ref.shape[1]
        for k in range(nk):
            ref[k, 0:PAD, :] = jnp.zeros((PAD, LANES), jnp.float32)
            ref[k, plane : PAD + plane, :] = jnp.zeros((PAD, LANES), jnp.float32)
            ref[k, rows - PAD - plane : rows - plane, :] = jnp.zeros((PAD, LANES), jnp.float32)
            ref[k, rows - PAD :, :] = jnp.zeros((PAD, LANES), jnp.float32)

    zs = pl.multiple_of(par * dm.half, 8)
    zm = pl.multiple_of(par * (nz - dm.more), 8)

    cx_off = from_off[at["x1"] : at["x1"] + plane, :]
    cx_in = from_in[at["x1"] : at["x1"] + plane, :]
    e, l = row_of(first), row_of(last)
    df[e : e + plane, :] = df[e : e + plane, :] + 0.5 * cx_off
    df[l : l + plane, :] = df[l : l + plane, :] + 0.5 * cx_in
    xf[row_of(first - 1) : e, :] = has_off * 0.5 * (cx_off + xf[e : e + plane, :])
    df[row_of(first - 1) : e, :] = from_off[at["d1"] : at["d1"] + plane, :] + 0.5 * xf[e : e + plane, :]
    df[row_of(last + 1) : row_of(last + 2), :] = (
        from_in[at["d1"] : at["d1"] + plane, :] + 0.5 * xf[l : l + plane, :]
    )
    for i in range(first, last):
        xf[row_of(i) : row_of(i + 1), :] = 0.5 * (
            xf[row_of(i) : row_of(i + 1), :] + xf[row_of(i + 1) : row_of(i + 2), :]
        )
    xf[l : l + plane, :] = 0.5 * (xf[l : l + plane, :] + cx_in)

    for halo, edge, step in ((from_off, first - 1, -1), (from_in, last + 1, 1)):

        def get(name, halo=halo):
            return halo[at[name] : at[name] + plane, :]

        second, third = edge + step, edge + 2 * step
        e, s, t = row_of(edge), row_of(second), row_of(third)
        bf[e : e + plane, :] = get("b1")
        yf[e : e + plane, :] = get("fy1")
        zf[e : e + plane, :] = get("fz1")
        df[s : s + plane, :] = get("d2")
        bf[s : s + plane, :] = get("b2")
        face = row_of(min(edge, second))
        xf[face : face + plane, :] = get("fx2")
        far = row_of(min(second, third))
        xf[far : far + plane, :] = jnp.ones((plane, LANES), jnp.float32)
        zf[s : s + plane, :] = jnp.zeros((plane, LANES), jnp.float32)
        for c in range(nc):
            z, z2, h = zs + c * nz, zm + c * nz, c * dm.half
            yf[pl.ds(s + z, dm.half), :] = halo[at["fy2"] + h : at["fy2"] + h + dm.half, :]
            df[pl.ds(t + z, dm.half), :] = halo[at["d3"] + h : at["d3"] + h + dm.half, :]
            bf[pl.ds(t + z, dm.half), :] = halo[at["g3"] + h : at["g3"] + h + dm.half, :]
            h = c * dm.more
            zf[pl.ds(s + z2, dm.more), :] = halo[at["fz2"] + h : at["fz2"] + h + dm.more, :]

    def tiles(ref, row):
        return [ref[pl.ds(row + c * nz, 8), :] for c in range(nc)]

    def tiles_of(ref, k, row):
        return [ref[k, pl.ds(row + c * nz, 8), :] for c in range(nc)]

    def add(j, k, value):
        at_ = (j * nk + k) * 8
        acc[at_ : at_ + 8, :] += value

    def total(first_tiles, second_tiles):
        products = [p * q for p, q in zip(first_tiles, second_tiles)]
        return functools.reduce(jnp.add, products)

    def over(planes, z_from, z_count, body):
        low, high = planes
        blocks = z_count // 8

        def step(n, carry):
            i = low + lax.div(n, blocks)
            z = pl.multiple_of(z_from + lax.rem(n, blocks) * 8, 8)
            body(i, z)
            return carry

        lax.fori_loop(0, (high - low) * blocks, step, 0)

    def start(i, z, own):
        row = pl.multiple_of(PAD + i * plane + z, 8)
        d, rhs = tiles(df, row), tiles(bf, row)
        for k in range(nk):
            s = shifts[k]
            inverse = [1.0 / (t + s) for t in d]
            value = [x * y for x, y in zip(rhs, inverse)]
            for c in range(nc):
                rf[k, pl.ds(row + c * nz, 8), :] = inverse[c]
                w0[k, pl.ds(row + c * nz, 8), :] = value[c]
            if own:
                add(0, k, total(rhs, value))

    over((first, last + 1), 0, nz, functools.partial(start, own=True))
    over((first - 2, first), 0, nz, functools.partial(start, own=False))
    over((last + 1, last + 3), 0, nz, functools.partial(start, own=False))
    over((first - 3, first - 2), zs, dm.half, functools.partial(start, own=False))
    over((last + 3, last + 4), zs, dm.half, functools.partial(start, own=False))

    def apply(i, z, src, src_first, dst, dst_first, moment):
        row = pl.multiple_of(PAD + i * plane + z, 8)
        src_row = pl.multiple_of(PAD + (i - src_first) * plane + z, 8)
        dst_row = pl.multiple_of(PAD + (i - dst_first) * plane + z, 8)
        x_low, x_high = tiles(xf, row - plane), tiles(xf, row)
        z_low, z_high = tiles(zf, row - 1), tiles(zf, row)
        y_high = tiles(yf, row)
        y_low = from_lower(y_high)
        lane = lane_ids()
        y_low[0] = jnp.where(lane == 0, 0.0, y_low[0])
        for k in range(nk):
            v = tiles_of(src, k, src_row)
            below, above = tiles_of(src, k, src_row - 1), tiles_of(src, k, src_row + 1)
            before, after = tiles_of(src, k, src_row - plane), tiles_of(src, k, src_row + plane)
            left, right = from_lower(v), from_higher(v)
            inverse = tiles_of(rf, k, row)
            image = []
            for c in range(nc):
                image.append(
                    (x_low[c] * before[c] + x_high[c] * after[c])
                    + (z_low[c] * below[c] + z_high[c] * above[c])
                    + (y_low[c] * left[c] + y_high[c] * right[c])
                )
            value = [x * y for x, y in zip(image, inverse)]
            for c in range(nc):
                dst[k, pl.ds(dst_row + c * nz, 8), :] = value[c]
            if moment is not None:
                add(moment, k, total(v, image))
                add(moment + 1, k, total(value, image))

    one = functools.partial(apply, src=w0, src_first=0, dst=w1, dst_first=1)
    over((first, last + 1), 0, nz, functools.partial(one, moment=1))
    over((first - 1, first), 0, nz, functools.partial(one, moment=None))
    over((last + 1, last + 2), 0, nz, functools.partial(one, moment=None))
    over((first - 2, first - 1), zs, dm.half, functools.partial(one, moment=None))
    over((last + 2, last + 3), zs, dm.half, functools.partial(one, moment=None))

    def send_out(src, slot, dst, which):
        copies = []
        for p in range(nl):
            layer = jnp.where(par == 0, p, nl - 1 - p)
            copy = pltpu.make_async_copy(
                src.at[:, pl.ds(PAD + (slot + p) * plane, plane), :],
                dst.at[:, pl.ds(pl.multiple_of(layer * plane, 8), plane), :],
                sems.at[which, p],
            )
            copy.start()
            copies.append(copy)
        return copies

    copies = send_out(w0, first, w0_out, 0) + send_out(w1, first - 1, w1_out, 1)

    two = functools.partial(apply, src=w1, src_first=1, dst=w2, dst_first=2)
    over((first, last + 1), 0, nz, functools.partial(two, moment=3))
    over((first - 1, first), zs, dm.half, functools.partial(two, moment=None))
    over((last + 1, last + 2), zs, dm.half, functools.partial(two, moment=None))
    copies += send_out(w2, first - 2, w2_out, 2)

    def face_sum(i, z, inner, with_x):
        row = pl.multiple_of(PAD + i * plane + z, 8)
        src_row = pl.multiple_of(PAD + (i - 2) * plane + z, 8)
        x_high = tiles(xf, row) if with_x else None
        z_high, y_high = tiles(zf, row), tiles(yf, row)
        for k in range(nk):
            v = tiles_of(w2, k, src_row)
            image = [jnp.zeros((8, LANES), jnp.float32)] * nc
            if inner:
                above, right = tiles_of(w2, k, src_row + 1), from_higher(v)
                image = [z_high[c] * above[c] + y_high[c] * right[c] for c in range(nc)]
            if with_x:
                after = tiles_of(w2, k, src_row + plane)
                image = [image[c] + x_high[c] * after[c] for c in range(nc)]
            add(5, k, 2.0 * total(v, image))

    over((first, last), 0, nz, functools.partial(face_sum, inner=True, with_x=True))
    over((last, last + 1), 0, nz, functools.partial(face_sum, inner=True, with_x=False))
    over((first - 1, first), zs, dm.half, functools.partial(face_sum, inner=False, with_x=True))
    over((last, last + 1), zs, dm.half, functools.partial(face_sum, inner=False, with_x=True))

    count48 = 6 * nk
    sums = jnp.sum(acc[...].reshape(count48, 8, LANES), axis=1)
    sums = jnp.concatenate([sums, jnp.zeros((LANES - count48, LANES), jnp.float32)], axis=0)
    moments[...] = jnp.sum(jnp.transpose(sums), axis=0, keepdims=True)
    for copy in copies:
        copy.wait()


def combine_body(dm, nk, moments, weights, w0, w1, w2, out, coeff):
    nc, nz = dm.nc, dm.nz

    @pl.when(pl.program_id(0) == 0)
    def _():
        sums = jnp.sum(moments[...].reshape(-1, LANES), axis=0, keepdims=True)
        sums = jnp.broadcast_to(sums, (8, LANES))
        nu = [sums] + [pltpu.roll(sums, LANES - j * nk, 1) for j in range(1, 6)]

        def inner(p, q, shift=0):
            total = None
            for i, x in enumerate(p):
                for j, y in enumerate(q):
                    term = x * y * nu[i + j + shift]
                    total = term if total is None else total + term
            return total

        def energy(p):
            return inner(p, p) - inner(p, p, 1)

        one = jnp.ones((8, LANES), jnp.float32)
        zero = jnp.zeros((8, LANES), jnp.float32)
        z = [one]
        p = [one]
        x = [zero, zero, zero]
        norm = nu[0]
        for number in range(3):
            step = norm / energy(p)
            x = [x[j] + step * p[j] if j < len(p) else x[j] for j in range(3)]
            if number < 2:
                p_ext, z_ext = p + [zero], z + [zero]
                z = [
                    z_ext[j] - step * (p_ext[j] - (p_ext[j - 1] if j else zero))
                    for j in range(len(p_ext))
                ]
                norm_next = inner(z, z)
                beta = norm_next / norm
                p = [z[j] + beta * p_ext[j] for j in range(len(z))]
                norm = norm_next
        for j in range(3):
            for k in range(nk):
                at = (j * nk + k) * 8
                coeff[at : at + 8, :] = jnp.broadcast_to(
                    x[j][:, k : k + 1] * weights[k], (8, LANES)
                )

    def block(zb, carry):
        z = pl.multiple_of(zb * 8, 8)
        for c in range(nc):
            row = c * nz + z
            total = None
            for j, ref in enumerate((w0, w1, w2)):
                for k in range(nk):
                    at = (j * nk + k) * 8
                    term = coeff[at : at + 8, :] * ref[k, pl.ds(row, 8), :]
                    total = term if total is None else total + term
            out[0, pl.ds(z, 8), c * LANES : (c + 1) * LANES] = total
        return carry

    lax.fori_loop(0, nz // 8, block, 0)


def on_device(right_side, cond_x, cond_y, cond_z, kappa_sq, shifts, weights):
    dm = Dims(right_side.shape)
    nk = shifts.shape[0]
    count = lax.axis_size("slab")
    f32 = jnp.float32
    vmem = pl.BlockSpec(memory_space=pltpu.VMEM)
    smem = pl.BlockSpec(memory_space=pltpu.SMEM)
    anywhere = pl.BlockSpec(memory_space=pl.ANY)
    params = pltpu.CompilerParams(vmem_limit_bytes=VMEM_LIMIT)
    sent = jax.ShapeDtypeStruct((dm.sent, LANES), f32)
    to_off, to_in = pl.pallas_call(
        functools.partial(pack_body, dm),
        out_shape=(sent, sent),
        in_specs=[vmem] * 5,
        out_specs=(vmem, vmem),
        scratch_shapes=[pltpu.VMEM((dm.own + 2 * PAD, LANES), f32)] * 5,
        compiler_params=params,
        name="pack",
    )(cond_x, cond_y, cond_z, kappa_sq, right_side)

    from_off = lax.ppermute(
        to_off,
        "slab",
        [pair for i in range(1, count - 1, 2) for pair in ((i, i + 1), (i + 1, i))],
    )
    from_in = lax.ppermute(to_in, "slab", [(i, i ^ 1) for i in range(count)])

    fields = jax.ShapeDtypeStruct((nk, dm.own, LANES), f32)
    flat = pltpu.VMEM((dm.rows, LANES), f32)

    def stack(planes):
        return pltpu.VMEM((nk, planes * dm.plane + 2 * PAD, LANES), f32)

    w0, w1, w2, moments = pl.pallas_call(
        functools.partial(basis_body, dm, nk),
        out_shape=(fields, fields, fields, jax.ShapeDtypeStruct((1, LANES), f32)),
        in_specs=[vmem] * 7 + [smem],
        out_specs=(anywhere, anywhere, anywhere, vmem),
        scratch_shapes=[flat] * 5
        + [stack(dm.np), stack(dm.np), stack(dm.np - 2), stack(dm.np - 4)]
        + [pltpu.VMEM((6 * nk * 8, LANES), f32), pltpu.SemaphoreType.DMA((3, dm.nl))],
        compiler_params=params,
        name="basis",
    )(cond_x, cond_y, cond_z, kappa_sq, right_side, from_off, from_in, shifts)

    everywhere = jnp.broadcast_to(moments[None], (count, 1, LANES))
    gathered = lax.all_to_all(everywhere, "slab", 0, 0)

    stacked = pl.BlockSpec((nk, dm.plane, LANES), lambda i: (0, i, 0))
    return pl.pallas_call(
        functools.partial(combine_body, dm, nk),
        out_shape=jax.ShapeDtypeStruct(right_side.shape, f32),
        grid=(dm.nl,),
        in_specs=[
            pl.BlockSpec((count, 1, LANES), lambda i: (0, 0, 0)),
            smem,
            stacked,
            stacked,
            stacked,
        ],
        out_specs=pl.BlockSpec((1, dm.nz, dm.ny), lambda i: (i, 0, 0)),
        scratch_shapes=[pltpu.VMEM((3 * nk * 8, LANES), f32)],
        compiler_params=params,
        name="combine",
    )(gathered, weights, w0, w1, w2)


def solution(mesh):
    return jax.shard_map(
        on_device,
        mesh=mesh,
        in_specs=(
            P(("field", "slab"), None, None),
            P("slab", None, None),
            P("slab", None, None),
            P("slab", None, None),
            P("slab", None, None),
            P(),
            P(),
        ),
        out_specs=P(("field", "slab"), None, None),
        check_vma=False,
    )
```

time: 289 us -> 92.3 us (0.32)
  blocking collectives: 205 us -> 39.3 us
  other arithmetic: 52 us -> 0 us
  Pallas kernels: 0 us -> 40.5 us
  starting transfers between devices: 18.7 us -> 5.04 us
  waiting for transfers between devices: 10.5 us -> 2.89 us
    psum x5 -> x0, blocking collectives: 205 us -> none  [the longest x3 110 us: precond_total(): return lax.psum(inner_sum(residual, precond), 'slab')]
    pallas_call x0 -> x3, Pallas kernels: none -> 40.5 us  [the longest x1 27.5 us: on_device(): pl.pallas_call(functools.partial(basis_body, dm, nk), out_shape=(fields,...]
    all_to_all x0 -> x1, blocking collectives: none -> 39.3 us  [on_device(): gathered = lax.all_to_all(everywhere, 'slab', 0, 0)]
    reduce_sum x6 -> x0, other arithmetic: 37.4 us -> none  [the longest x5 32 us: inner_sum(): return jnp.sum(first * second, axis=(1, 2, 3))]
    ppermute x8 -> x2, starting transfers between devices: 18.7 us -> 5.04 us  [the longest x1 4.31 us: on_device(): from_in = lax.ppermute(to_in, 'slab', [(i, i ^ 1) for i in range(count)])]
    add x2 -> x0, other arithmetic: 7.79 us -> none  [on_device(): direction = precond + expand(norm_next / norm_now) * direction]
    ppermute x8 -> x2, waiting for transfers between devices: 10.5 us -> 2.89 us  [the longest x1 2.89 us: on_device(): from_in = lax.ppermute(to_in, 'slab', [(i, i ^ 1) for i in range(count)])]
    mul x3 -> x0, other arithmetic: 4.17 us -> none  [the longest x2 2.8 us: face_pair(): 0.5 * (lax.slice_in_dim(padded, 0, count + 1, axis=axis) + lax.slice_in_d...]
  transfers between devices with their start and end apart: 8 -> 2, of which waited for: 6 -> 1; matrix products, arithmetic and copies ran while one was open for 1% -> 0% of each run, Pallas kernels for 0% -> 0%
where the time goes in v1:
time: 92.3 us; the launch traced here: 91.9 us
  Pallas kernels  40.5 us (44%)
  blocking collectives  39.3 us (43%)
  starting transfers between devices  5.04 us (5%)
  local copies, waits for them, and re-layouts  4.21 us (5%)
  waiting for transfers between devices  2.89 us (3%)
    all_to_all x1, blocking collectives, on_device(): gathered = lax.all_to_all(everywhere, 'slab', 0, 0)  39.3 us
    pallas_call x1, Pallas kernels, on_device(): pl.pallas_call(functools.partial(basis_body, dm, nk), out_shape=(fields,...  27.5 us
    pallas_call x1, Pallas kernels, on_device(): pl.pallas_call(functools.partial(combine_body, dm, nk), out_shape=jax.Sha...  6.83 us
    pallas_call x1, Pallas kernels, on_device(): pl.pallas_call(functools.partial(pack_body, dm), out_shape=(sent, sent),...  6.14 us
    ppermute x1, starting transfers between devices, on_device(): from_in = lax.ppermute(to_in, 'slab', [(i, i ^ 1) for i in range(count)])  4.31 us
    unnamed x14, local copies, waits for them, and re-layouts  4.2 us
    ppermute x1, waiting for transfers between devices, on_device(): from_in = lax.ppermute(to_in, 'slab', [(i, i ^ 1) for i in range(count)])  2.89 us
  transfers between devices with their start and end apart: 2, of which 1 were waited for; matrix products, arithmetic and copies ran while one was open for 0% of the time, Pallas kernels for 0%

profile of v1, /device:TPU:0, one launch (start us, length us, event | category | flops | bytes accessed | tf_op | source)
XLA Modules:
  0.0 91.9 jit_solution(5538727963290222388)
XLA Ops:
  0.0 0.0 copy-start
  0.0 1.0 %copy-done = f32[4,64,512]{2,1,0:T(8,128)S(1)} copy-done((f32[4,64,512]{2,1,0:T(8,128)S(1)}, f32[4,64,512]{2,1,0:T(8,128)}, u32[]{:S(2)}) %copy-start) | copy-done | bytes 524312
  1.0 0.0 copy-start.1
  1.0 1.0 %copy-done.1 = f32[4,64,512]{2,1,0:T(8,128)S(1)} copy-done((f32[4,64,512]{2,1,0:T(8,128)S(1)}, f32[4,64,512]{2,1,0:T(8,128)}, u32[]{:S(2)}) %copy-start.1) | copy-done | bytes 524312
  2.1 0.0 copy-start.2
  2.1 1.0 %copy-done.2 = f32[4,64,512]{2,1,0:T(8,128)S(1)} copy-done((f32[4,64,512]{2,1,0:T(8,128)S(1)}, f32[4,64,512]{2,1,0:T(8,128)}, u32[]{:S(2)}) %copy-start.2) | copy-done | bytes 524312
  3.1 0.0 copy-start.4
  3.1 6.1 %pack.1 = (f32[2592,128]{1,0:T(8,128)}, f32[2592,128]{1,0:T(8,128)}) custom-call(f32[4,64,512]{2,1,0:T(8,128)S(1)} %copy-done, f32[4,64,512]{2,1,0:T(8,128)S(1)} %copy-done.1, f32[4,64,512]{2,1,0:T(8,128)S(1)} %copy-done.2, f32[4,64,512]{2,1,0:T(8,128)} %kappa.3, f32[4,64,512]{2,1,0:T(8,128)} %b.3), custom_call_target="tpu_custom_call" | custom-call | tf_op jit(solution)/shard_map/pack/pallas_call | solution.py:453
  9.3 0.7 collective-permute-start
  10.0 0.0 copy-start.3
  10.0 4.3 %collective-permute-start.1 = (f32[2592,128]{1,0:T(8,128)}, f32[2592,128]{1,0:T(8,128)S(1)}, u32[]{:S(2)}, u32[]{:S(2)}) collective-permute-start(f32[2592,128]{1,0:T(8,128)} %get-tuple-element.12), channel_id=1, source_target_pairs={{0,1},{1,0},{2,3},{3,2},{4,5},{5,4},{6,7},{7,6},{8,9},{9,8},{10,11... | collective-permute-start | bytes 3981320 | tf_op jit(solution)/shard_map/ppermute | solution.py:468
  14.3 0.0 collective-permute-done.from_off
  14.3 0.0 copy-start.5
  14.3 2.9 %collective-permute-done.1.from_in = f32[2592,128]{1,0:T(8,128)S(1)} collective-permute-done((f32[2592,128]{1,0:T(8,128)}, f32[2592,128]{1,0:T(8,128)S(1)}, u32[]{:S(2)}, u32[]{:S(2)}) %collective-permute-start.1) | collective-permute-done | bytes 1327136 | tf_op jit(solution)/shard_map/ppermute | solution.py:468
  17.2 0.0 copy-done.5
  17.2 0.0 copy-start.6
  17.2 1.1 %copy-done.6 = f32[2592,128]{1,0:T(8,128)} copy-done((f32[2592,128]{1,0:T(8,128)}, f32[2592,128]{1,0:T(8,128)S(1)}, u32[]{:S(2)}) %copy-start.6) | copy-done | bytes 1327128
  18.3 0.0 copy-done.4
  18.3 27.5 %basis.1 = (f32[8,1024,128]{2,1,0:T(8,128)}, f32[8,1024,128]{2,1,0:T(8,128)}, f32[8,1024,128]{2,1,0:T(8,128)}, f32[1,128]{1,0:T(1,128)S(1)}) custom-call(f32[4,64,512]{2,1,0:T(8,128)S(1)} %copy-done, f32[4,64,512]{2,1,0:T(8,128)S(1)} %copy-done.1, f32[4,64,512]{2,1,0:T(8,128)S(1)} %copy-done.2, f32[4,64,512]{2,1,0:T(8,128)} %kappa.3, f32[4,64,512]{2,1,0:T(8,128)} %b.3, ...), custom_call_target="tpu_custom_call" | custom-call | tf_op jit(solution)/shard_map/basis/pallas_call | solution.py:476
  45.8 39.3 %all_to_all.5.moments = f32[16,1,128]{2,1,0:T(1,128)S(1)} all-to-all(f32[16,1,128]{2,1,0:T(1,128)S(1)} %broadcast_in_dim.9), channel_id=1, replica_groups=mesh['field'=2,'slab'=16] {'slab'}, dimensions={0} | all-to-all | bytes 16384 | tf_op jit(solution)/shard_map/all_to_all | solution.py:489
  85.1 0.0 copy-done.3
  85.1 6.8 %combine.1 = f32[4,64,512]{2,1,0:T(8,128)} custom-call(f32[16,1,128]{2,1,0:T(1,128)S(1)} %all_to_all.5.moments, f32[8]{0:T(128)S(1)} %copy-done.3, f32[8,1024,128]{2,1,0:T(8,128)} %get-tuple-element.14.w0, f32[8,1024,128]{2,1,0:T(8,128)} %get-tuple-element.15.w1, f32[8,1024,128]{2,1,0:T(8,128)} %get-tuple-element.16.w2), custom_call_target="tpu_custom_call" | custom-call | tf_op jit(solution)/shard_map/combine/pallas_call | solution.py:492
  (1 shorter events, 0.0 us)
Async XLA Ops:
  0.0 1.0 %copy-start = (f32[4,64,512]{2,1,0:T(8,128)S(1)}, f32[4,64,512]{2,1,0:T(8,128)}, u32[]{:S(2)}) copy-start(f32[4,64,512]{2,1,0:T(8,128)} %cx.3) | copy-start | bytes 1572868
  1.0 1.0 %copy-start.1 = (f32[4,64,512]{2,1,0:T(8,128)S(1)}, f32[4,64,512]{2,1,0:T(8,128)}, u32[]{:S(2)}) copy-start(f32[4,64,512]{2,1,0:T(8,128)} %cy.3) | copy-start | bytes 1572868
  2.1 1.0 %copy-start.2 = (f32[4,64,512]{2,1,0:T(8,128)S(1)}, f32[4,64,512]{2,1,0:T(8,128)}, u32[]{:S(2)}) copy-start(f32[4,64,512]{2,1,0:T(8,128)} %cz.3) | copy-start | bytes 1572868
  3.1 15.2 %copy-start.4 = (f32[8]{0:T(128)S(1)}, f32[8]{0:T(128)}, u32[]{:S(2)}) copy-start(f32[8]{0:T(128)} %shifts.1) | copy-start | bytes 100
  9.3 5.1 %collective-permute-start = (f32[2592,128]{1,0:T(8,128)}, f32[2592,128]{1,0:T(8,128)S(1)}, u32[]{:S(2)}, u32[]{:S(2)}) collective-permute-start(f32[2592,128]{1,0:T(8,128)} %get-tuple-element.11), channel_id=1, source_target_pairs={{1,2},{2,1},{3,4},{4,3},{5,6},{6,5},{7,8},{8,7},{9,10},{10,9},{11,... | collective-permute-start | bytes 3981320 | tf_op jit(solution)/shard_map/ppermute | solution.py:463
  10.0 75.1 %copy-start.3 = (f32[8]{0:T(128)S(1)}, f32[8]{0:T(128)}, u32[]{:S(2)}) copy-start(f32[8]{0:T(128)} %weights.1) | copy-start | bytes 100
  10.0 7.2 %collective-permute-start.1 = (f32[2592,128]{1,0:T(8,128)}, f32[2592,128]{1,0:T(8,128)S(1)}, u32[]{:S(2)}, u32[]{:S(2)}) collective-permute-start(f32[2592,128]{1,0:T(8,128)} %get-tuple-element.12), channel_id=1, source_target_pairs={{0,1},{1,0},{2,3},{3,2},{4,5},{5,4},{6,7},{7,6},{8,9},{9,8},{10,11... | collective-permute-start | bytes 3981320 | tf_op jit(solution)/shard_map/ppermute | solution.py:468
  14.3 2.9 %copy-start.5 = (f32[2592,128]{1,0:T(8,128)}, f32[2592,128]{1,0:T(8,128)S(1)}, u32[]{:S(2)}) copy-start(f32[2592,128]{1,0:T(8,128)S(1)} %collective-permute-done.from_off) | copy-start | bytes 3981316
  17.2 1.1 %copy-start.6 = (f32[2592,128]{1,0:T(8,128)}, f32[2592,128]{1,0:T(8,128)S(1)}, u32[]{:S(2)}) copy-start(f32[2592,128]{1,0:T(8,128)S(1)} %collective-permute-done.1.from_in) | copy-start | bytes 3981316

commit v2 on v0

v2 whole, which is shorter than its diff:
```python
import functools
import jax
import jax.numpy as jnp
from jax import lax
from jax.experimental import pallas as pl
from jax.experimental.pallas import tpu as pltpu
from jax.sharding import PartitionSpec as P

LANES = 128
PAD = 8
MIB = 1024 * 1024


class Dims:
    def __init__(self, shape):
        self.nl, self.nz, self.ny = shape
        self.nc = self.ny // LANES
        self.plane = self.nc * self.nz
        self.slot = self.plane + PAD
        self.half = self.nz // 2
        self.more = self.half + 8
        full, half = self.plane, self.nc * self.half
        layout = [
            ("pad", PAD), ("fz1", full), ("d1", full), ("x1", full), ("fy1", full),
            ("d2", full), ("fx2", full), ("b1", full), ("b2", full),
            ("fy2", half), ("d3", half), ("g3", half), ("fz2", self.nc * self.more),
        ]
        self.at = {}
        total = 0
        for name, size in layout:
            self.at[name] = total
            total += size
        self.sent = total

    def stack_rows(self, slots):
        return slots * self.slot + PAD


class Plane:
    def __init__(self, ref, base, stride, zoff=0):
        self.ref, self.base, self.stride, self.zoff = ref, base, stride, zoff

    def row(self, c, z):
        return pl.multiple_of(z - self.zoff, 8) + (self.base + c * self.stride)

    def get(self, c, z, k=None, d=0):
        rows = pl.ds(self.row(c, z) + d, 8)
        return self.ref[rows, :] if k is None else self.ref[k, rows, :]

    def put(self, c, z, value, k=None):
        rows = pl.ds(self.row(c, z), 8)
        if k is None:
            self.ref[rows, :] = value
        else:
            self.ref[k, rows, :] = value


def lane_ids():
    return lax.broadcasted_iota(jnp.int32, (8, LANES), 1)


def row_ids():
    return lax.broadcasted_iota(jnp.int32, (8, LANES), 0)


def from_higher(tiles):
    lane = lane_ids()
    n = len(tiles)
    return [
        pltpu.roll(jnp.where(lane == 0, tiles[(c + 1) % n], tiles[c]), LANES - 1, 1)
        for c in range(n)
    ]


def from_lower(tiles):
    lane = lane_ids()
    n = len(tiles)
    return [
        pltpu.roll(jnp.where(lane == LANES - 1, tiles[(c - 1) % n], tiles[c]), 1, 1)
        for c in range(n)
    ]


def blocks(z_from, z_count, body, unroll=1):
    def step(n, carry):
        for u in range(unroll):
            body(pl.multiple_of(z_from + (n * unroll + u) * 8, 8))
        return carry

    lax.fori_loop(0, z_count // (8 * unroll), step, 0)


def own_planes(dm, ref):
    return [Plane(ref, PAD + p * dm.slot, dm.nz) for p in range(dm.nl)]


def prepare(dm, par, cx, cy, cz, kappa, b, flats):
    nc, nz, nl = dm.nc, dm.nz, dm.nl
    bf, df, xf, yf, zf, tf = [own_planes(dm, ref) for ref in flats]
    for ref in (flats[4], flats[5]):
        for p in range(nl + 1):
            ref[p * dm.slot : p * dm.slot + PAD, :] = jnp.zeros((PAD, LANES), jnp.float32)
    layers = [jnp.where(par == 0, p, nl - 1 - p) for p in range(nl)]

    def copy(z):
        for p in range(nl):
            for src, dst in ((b, bf), (cx, xf), (cz, tf)):
                block = src[layers[p], pl.ds(z, 8), :]
                for c in range(nc):
                    dst[p].put(c, z, block[:, c * LANES : (c + 1) * LANES])

    blocks(0, nz, copy)

    def faces(p, z):
        lane, sub = lane_ids(), row_ids()
        conds = cy[layers[p], pl.ds(z, 8), :]
        kap = kappa[layers[p], pl.ds(z, 8), :]
        ys = [conds[:, c * LANES : (c + 1) * LANES] for c in range(nc)]
        up, down = from_higher(ys), from_lower(ys)
        up[-1] = jnp.where(lane == LANES - 1, 0.0, up[-1])
        down[0] = jnp.where(lane == 0, 0.0, down[0])
        for c in range(nc):
            high_y = 0.5 * (ys[c] + up[c])
            low_y = 0.5 * (ys[c] + down[c])
            here = tf[p].get(c, z)
            high_z = 0.5 * (here + jnp.where(sub + z == nz - 1, 0.0, tf[p].get(c, z, d=1)))
            low_z = 0.5 * (here + jnp.where(sub + z == 0, 0.0, tf[p].get(c, z, d=-1)))
            mine = xf[p].get(c, z)
            total = kap[:, c * LANES : (c + 1) * LANES]
            total = total + 0.5 * (mine + xf[p - 1].get(c, z) if p > 0 else mine)
            total = total + 0.5 * (mine + xf[p + 1].get(c, z) if p < nl - 1 else mine)
            df[p].put(c, z, total + low_z + high_z + low_y + high_y)
            if c == nc - 1:
                high_y = jnp.where(lane == LANES - 1, 0.0, high_y)
            yf[p].put(c, z, high_y)
            zf[p].put(c, z, jnp.where(sub + z == nz - 1, 0.0, high_z))

    def all_faces(z):
        for p in range(nl):
            faces(p, z)

    blocks(0, nz, all_faces)


def load_own(sources, targets, sems):
    copies = [
        pltpu.make_async_copy(src, dst, sems.at[n])
        for n, (src, dst) in enumerate(zip(sources, targets))
    ]
    for copy in copies:
        copy.start()
    for copy in copies:
        copy.wait()


def pack_body(dm, cx, cy, cz, kappa, b, to_off, to_in, raw, flats, fx2, g3, zero, in_sems, out_sems):
    par = lax.rem(lax.axis_index("slab"), 2)
    nc, nz, nl = dm.nc, dm.nz, dm.nl
    load_own((cx, cy, cz, kappa, b), raw, in_sems)
    prepare(dm, par, *raw, flats)
    bf, df, xf, yf, zf = [own_planes(dm, ref) for ref in flats[:5]]
    other = 1 - par
    zs = pl.multiple_of(other * dm.half, 8)
    zm = pl.multiple_of(other * (nz - dm.more), 8)
    zero[...] = jnp.zeros(zero.shape, jnp.float32)
    copies = []

    def send(out, name, src, start, rows, shift=0):
        copy = pltpu.make_async_copy(
            src.at[pl.ds(start, rows), :],
            out.at[pl.ds(dm.at[name] + shift, rows), :],
            out_sems.at[len(copies)],
        )
        copy.start()
        copies.append(copy)

    for side, (out, edge, step) in enumerate(((to_off, 0, 1), (to_in, nl - 1, -1))):
        one, two, three = edge, edge + step, edge + 2 * step
        for name, planes, p in (
            ("fz1", zf, one), ("d1", df, one), ("x1", xf, one), ("fy1", yf, one),
            ("d2", df, two), ("b1", bf, one), ("b2", bf, two),
        ):
            send(out, name, planes[p].ref, planes[p].base, dm.plane)
        send(out, "pad", zero, 0, PAD)
        for c in range(nc):
            half = c * dm.half
            send(out, "fy2", yf[two].ref, yf[two].base + c * nz + zs, dm.half, half)
            send(out, "d3", df[three].ref, df[three].base + c * nz + zs, dm.half, half)
            send(out, "fz2", zf[two].ref, zf[two].base + c * nz + zm, dm.more, c * dm.more)

        def derived(z, side=side, one=one, two=two):
            for c in range(nc):
                fx2[pl.ds(side * dm.plane + c * nz + z, 8), :] = 0.5 * (
                    xf[one].get(c, z) + xf[two].get(c, z)
                )

        def derived_half(n, side=side, two=two, three=three):
            z = pl.multiple_of(zs + n, 8)
            for c in range(nc):
                g3[pl.ds((side * nc + c) * dm.half + n, 8), :] = (
                    0.5 * (xf[two].get(c, z) + xf[three].get(c, z)) * bf[three].get(c, z)
                )

        blocks(0, nz, derived)
        blocks(0, dm.half, derived_half)
        send(out, "fx2", fx2, side * dm.plane, dm.plane)
        send(out, "g3", g3, side * nc * dm.half, nc * dm.half)
    for copy in copies:
        copy.wait()


class Steps:
    def __init__(self, dm, nk, par, acc, shifts):
        self.dm, self.nk, self.acc, self.shifts = dm, nk, acc, shifts
        self.zs = pl.multiple_of(par * dm.half, 8)
        self.zm = pl.multiple_of(par * (dm.nz - dm.more), 8)

    def sweep(self, half, body, unroll=2):
        if half:
            blocks(self.zs, self.dm.half, body, unroll)
        else:
            blocks(0, self.dm.nz, body, unroll)

    def add(self, j, k, value):
        at = (j * self.nk + k) * 8
        self.acc[at : at + 8, :] += value

    def total(self, first, second):
        return functools.reduce(jnp.add, [p * q for p, q in zip(first, second)])

    def tiles(self, plane, z, k=None, d=0):
        return [plane.get(c, z, k, d) for c in range(self.dm.nc)]

    def start(self, d, b, w, r=None, half=False, own=False):
        def body(z):
            diagonal, rhs = self.tiles(d, z), self.tiles(b, z)
            for k in range(self.nk):
                s = self.shifts[k]
                inverse = [1.0 / (t + s) for t in diagonal]
                value = [x * y for x, y in zip(rhs, inverse)]
                for c in range(self.dm.nc):
                    if r is not None:
                        r.put(c, z, inverse[c], k)
                    w.put(c, z, value[c], k)
                if own:
                    self.add(0, k, self.total(rhs, value))

        self.sweep(half, body, 1)

    def inverses(self, d, r):
        def body(z):
            diagonal = self.tiles(d, z)
            for k in range(self.nk):
                s = self.shifts[k]
                for c in range(self.dm.nc):
                    r.put(c, z, 1.0 / (diagonal[c] + s), k)

        self.sweep(False, body, 1)

    def apply(self, v, sides, out, r=None, yz=None, base=None, half=False, moment=None):
        nc = self.dm.nc

        def body(z):
            xs = [(None if x is None else self.tiles(x, z), w) for x, w in sides]
            if yz is not None:
                fy, fz = yz
                lane, sub = lane_ids(), row_ids()
                y_high = self.tiles(fy, z)
                y_low = from_lower(y_high)
                y_low[0] = jnp.where(lane == 0, 0.0, y_low[0])
                z_high = self.tiles(fz, z)
                z_low = self.tiles(fz, z, d=-1)
                if half:
                    z_low = [jnp.where(sub + z == 0, 0.0, t) for t in z_low]
            for k in range(self.nk):
                value = self.tiles(v, z, k) if v is not None else None
                image = None if base is None else self.tiles(base, z, k)
                parts = []
                if yz is not None:
                    below, above = self.tiles(v, z, k, -1), self.tiles(v, z, k, 1)
                    left, right = from_lower(value), from_higher(value)
                    parts.append([z_low[c] * below[c] + z_high[c] * above[c] for c in range(nc)])
                for x, w in xs:
                    near = self.tiles(w, z, k)
                    parts.append(near if x is None else [x[c] * near[c] for c in range(nc)])
                if yz is not None:
                    parts.append([y_low[c] * left[c] + y_high[c] * right[c] for c in range(nc)])
                for part in parts:
                    image = part if image is None else [p + q for p, q in zip(image, part)]
                if r is None:
                    for c in range(nc):
                        out.put(c, z, image[c], k)
                    continue
                result = [p * q for p, q in zip(image, self.tiles(r, z, k))]
                for c in range(nc):
                    out.put(c, z, result[c], k)
                if moment is not None:
                    self.add(moment, k, self.total(value, image))
                    self.add(moment + 1, k, self.total(result, image))

        self.sweep(half, body)

    def face_sum(self, v, side=None, yz=None, half=False):
        nc = self.dm.nc

        def body(z):
            x = self.tiles(side[0], z) if side is not None else None
            if yz is not None:
                y_high, z_high = self.tiles(yz[0], z), self.tiles(yz[1], z)
            for k in range(self.nk):
                value = self.tiles(v, z, k)
                parts = []
                if yz is not None:
                    above, right = self.tiles(v, z, k, 1), from_higher(value)
                    parts.append([z_high[c] * above[c] + y_high[c] * right[c] for c in range(nc)])
                if side is not None:
                    near = self.tiles(side[1], z, k)
                    parts.append([x[c] * near[c] for c in range(nc)])
                image = parts[0]
                if len(parts) == 2:
                    image = [p + q for p, q in zip(*parts)]
                self.add(5, k, 2.0 * self.total(value, image))

        self.sweep(half, body)


def stack(dm, ref, planes):
    return {p: Plane(ref, PAD + n * dm.slot, dm.nz) for n, p in enumerate(planes)}


def clear_pads(dm, nk, ref):
    for n in range((ref.shape[1] - PAD) // dm.slot + 1):
        for k in range(nk):
            ref[k, n * dm.slot : n * dm.slot + PAD, :] = jnp.zeros((PAD, LANES), jnp.float32)


def halo_planes(dm, ref, st):
    planes = {n: Plane(ref, dm.at[n], dm.nz) for n in ("fz1", "d1", "x1", "fy1", "d2", "fx2", "b1", "b2")}
    for n in ("fy2", "d3", "g3"):
        planes[n] = Plane(ref, dm.at[n], dm.half, st.zs)
    planes["fz2"] = Plane(ref, dm.at["fz2"], dm.more, st.zm)
    return planes


def near_body(
    dm, nk, cx, cy, cz, kappa, b, from_in, shifts,
    coef, w0a, w1a, w2a, part1, part2, acc,
    raw, temp, extra, w0h, w1h, w2h, inv, sems,
):
    par = lax.rem(lax.axis_index("slab"), 2)
    nl, nc, nz = dm.nl, dm.nc, dm.nz
    last = nl - 1
    load_own((cx, cy, cz, kappa, b), raw, sems)
    prepare(dm, par, *raw, [coef.at[n] for n in range(5)] + [temp])
    bf, df, xf, yf, zf = [own_planes(dm, coef.at[n]) for n in range(5)]
    st = Steps(dm, nk, par, acc, shifts)
    hp = halo_planes(dm, from_in, st)
    acc[...] = jnp.zeros(acc.shape, jnp.float32)
    for ref in (w0a, w1a, w2a, w0h, w1h, w2h):
        clear_pads(dm, nk, ref)
    d_next = Plane(extra, 0, nz)
    raw0 = Plane(coef.at[5], PAD, nz)

    def edges(z):
        for c in range(nc):
            here, there = xf[last].get(c, z), hp["x1"].get(c, z)
            raw0.put(c, z, xf[0].get(c, z))
            df[last].put(c, z, df[last].get(c, z) + 0.5 * there)
            d_next.put(c, z, hp["d1"].get(c, z) + 0.5 * here)
            for p in range(last):
                xf[p].put(c, z, 0.5 * (xf[p].get(c, z) + xf[p + 1].get(c, z)))
            xf[last].put(c, z, 0.5 * (here + there))

    blocks(0, nz, edges)

    W0 = stack(dm, w0a, range(1, nl)) | stack(dm, w0h, (nl, nl + 1))
    far = Plane(w0h, PAD + 2 * dm.slot, dm.half, st.zs)
    W1 = stack(dm, w1a, range(2, nl)) | stack(dm, w1h, (nl,))
    W1[nl + 1] = Plane(w1h, PAD + dm.slot, nz)
    W2 = stack(dm, w2a, range(3, nl)) | stack(dm, w2h, (nl,))
    R = stack(dm, inv, range(1, nl + 2))
    I1, I2 = Plane(part1, 0, nz), Plane(part2, 0, nz)

    for p in range(1, nl):
        st.start(df[p], bf[p], W0[p], R[p], own=True)
    st.start(d_next, hp["b1"], W0[nl], R[nl])
    st.start(hp["d2"], hp["b2"], W0[nl + 1], R[nl + 1])
    st.start(hp["d3"], hp["g3"], far, half=True)

    yz = [(yf[p], zf[p]) for p in range(nl)]
    st.apply(W0[1], [(xf[1], W0[2])], I1, yz=yz[1])
    for p in range(2, nl):
        st.apply(W0[p], [(xf[p - 1], W0[p - 1]), (xf[p], W0[p + 1])], W1[p], R[p], yz[p], moment=1)
    st.apply(
        W0[nl], [(xf[last], W0[last]), (hp["fx2"], W0[nl + 1])], W1[nl], R[nl], (hp["fy1"], hp["fz1"])
    )
    st.apply(
        W0[nl + 1], [(hp["fx2"], W0[nl]), (None, far)], W1[nl + 1], R[nl + 1],
        (hp["fy2"], hp["fz2"]), half=True,
    )
    st.apply(W1[2], [(xf[2], W1[3])], I2, yz=yz[2])
    for p in range(3, nl):
        st.apply(W1[p], [(xf[p - 1], W1[p - 1]), (xf[p], W1[p + 1])], W2[p], R[p], yz[p], moment=3)
    st.apply(
        W1[nl], [(xf[last], W1[last]), (hp["fx2"], W1[nl + 1])], W2[nl], R[nl],
        (hp["fy1"], hp["fz1"]), half=True,
    )
    for p in range(3, nl):
        st.face_sum(W2[p], None if p == last else (xf[p], W2[p + 1]), yz[p])
    st.face_sum(W2[last], (xf[last], W2[nl]), half=True)


def far_body(
    dm, nk, coef, w0a, w1a, w2a, part1, part2, acc_in, from_off, shifts,
    w0b, w1b, w2b, moments, acc, extra, w0h, w1h, w2h, inv,
):
    index = lax.axis_index("slab")
    par = lax.rem(index, 2)
    has_off = jnp.where(jnp.logical_and(index > 0, index < lax.axis_size("slab") - 1), 0.5, 0.0)
    nl, nc, nz = dm.nl, dm.nc, dm.nz
    bf, df, xf, yf, zf = [own_planes(dm, coef.at[n]) for n in range(5)]
    raw0 = Plane(coef.at[5], PAD, nz)
    st = Steps(dm, nk, par, acc, shifts)
    hp = halo_planes(dm, from_off, st)
    acc[...] = acc_in[...]
    for ref in (w0b, w1b, w2b, w0h, w1h, w2h):
        clear_pads(dm, nk, ref)
    d_here, d_next, x_edge = [Plane(extra.at[n], 0, nz) for n in range(3)]

    def edges(z):
        for c in range(nc):
            here, there = raw0.get(c, z), hp["x1"].get(c, z)
            d_here.put(c, z, df[0].get(c, z) + 0.5 * there)
            d_next.put(c, z, hp["d1"].get(c, z) + 0.5 * here)
            x_edge.put(c, z, has_off * (here + there))

    blocks(0, nz, edges)

    W0 = stack(dm, w0a, range(1, nl)) | stack(dm, w0b, (0,)) | stack(dm, w0h, (-1, -2))
    far = Plane(w0h, PAD + 2 * dm.slot, dm.half, st.zs)
    W1 = stack(dm, w1a, range(2, nl)) | stack(dm, w1b, (0, 1)) | stack(dm, w1h, (-1, -2))
    W2 = stack(dm, w2a, range(3, nl)) | stack(dm, w2b, (0, 1, 2)) | stack(dm, w2h, (-1,))
    R = stack(dm, inv, (-2, -1, 0, 1, 2))
    I1, I2 = Plane(part1, 0, nz), Plane(part2, 0, nz)
    yz = [(yf[p], zf[p]) for p in range(nl)]

    st.inverses(df[1], R[1])
    st.inverses(df[2], R[2])
    st.start(d_here, bf[0], W0[0], R[0], own=True)
    st.start(d_next, hp["b1"], W0[-1], R[-1])
    st.start(hp["d2"], hp["b2"], W0[-2], R[-2])
    st.start(hp["d3"], hp["g3"], far, half=True)

    st.apply(W0[1], [(xf[0], W0[0])], W1[1], R[1], base=I1, moment=1)
    st.apply(W0[0], [(x_edge, W0[-1]), (xf[0], W0[1])], W1[0], R[0], yz[0], moment=1)
    st.apply(
        W0[-1], [(hp["fx2"], W0[-2]), (x_edge, W0[0])], W1[-1], R[-1], (hp["fy1"], hp["fz1"])
    )
    st.apply(
        W0[-2], [(None, far), (hp["fx2"], W0[-1])], W1[-2], R[-2], (hp["fy2"], hp["fz2"]), half=True
    )
    st.apply(W1[2], [(xf[1], W1[1])], W2[2], R[2], base=I2, moment=3)
    st.apply(W1[1], [(xf[0], W1[0]), (xf[1], W1[2])], W2[1], R[1], yz[1], moment=3)
    st.apply(W1[0], [(x_edge, W1[-1]), (xf[0], W1[1])], W2[0], R[0], yz[0], moment=3)
    st.apply(
        W1[-1], [(hp["fx2"], W1[-2]), (x_edge, W1[0])], W2[-1], R[-1],
        (hp["fy1"], hp["fz1"]), half=True,
    )
    for p in range(min(3, nl - 1)):
        st.face_sum(W2[p], (xf[p], W2[p + 1]), yz[p])
    st.face_sum(W2[0], (x_edge, W2[-1]), half=True)

    number = 6 * nk
    sums = jnp.sum(acc[...].reshape(number, 8, LANES), axis=1)
    sums = jnp.concatenate([sums, jnp.zeros((LANES - number, LANES), jnp.float32)], axis=0)
    moments[...] = jnp.sum(jnp.transpose(sums), axis=0, keepdims=True)


def coefficients(sums, nk):
    nu = [sums] + [pltpu.roll(sums, LANES - j * nk, 1) for j in range(1, 6)]

    def inner(p, q, shift=0):
        total = None
        for i, x in enumerate(p):
            for j, y in enumerate(q):
                term = x * y * nu[i + j + shift]
                total = term if total is None else total + term
        return total

    one = jnp.ones((8, LANES), jnp.float32)
    zero = jnp.zeros((8, LANES), jnp.float32)
    z = [one]
    p = [one]
    x = [zero, zero, zero]
    norm = nu[0]
    for number in range(3):
        step = norm / (inner(p, p) - inner(p, p, 1))
        x = [x[j] + step * p[j] if j < len(p) else x[j] for j in range(3)]
        if number < 2:
            p, z = p + [zero], z + [zero]
            z = [z[j] - step * (p[j] - (p[j - 1] if j else zero)) for j in range(len(p))]
            norm_next = inner(z, z)
            beta = norm_next / norm
            p = [z[j] + beta * p[j] for j in range(len(z))]
            norm = norm_next
    return x


def combine_body(dm, nk, moments, weights, w0a, w0b, w1a, w1b, w2a, w2b, out):
    par = lax.rem(lax.axis_index("slab"), 2)
    nl, nc, nz = dm.nl, dm.nc, dm.nz
    sums = jnp.sum(moments[...].reshape(-1, LANES), axis=0, keepdims=True)
    x = coefficients(jnp.broadcast_to(sums, (8, LANES)), nk)
    scale = [
        [jnp.broadcast_to(x[j][:, k : k + 1] * weights[k], (8, LANES)) for k in range(nk)]
        for j in range(3)
    ]
    W0 = stack(dm, w0a, range(1, nl)) | stack(dm, w0b, (0,))
    W1 = stack(dm, w1a, range(2, nl)) | stack(dm, w1b, (0, 1))
    W2 = stack(dm, w2a, range(3, nl)) | stack(dm, w2b, (0, 1, 2))
    for p in range(nl):
        layer = jnp.where(par == 0, p, nl - 1 - p)

        def body(z, p=p, layer=layer):
            for c in range(nc):
                terms = [
                    scale[j][k] * w[p].get(c, z, k) for j, w in enumerate((W0, W1, W2)) for k in range(nk)
                ]
                while len(terms) > 1:
                    terms = [sum(terms[n : n + 2][1:], terms[n]) for n in range(0, len(terms), 2)]
                out[layer, pl.ds(z, 8), c * LANES : (c + 1) * LANES] = terms[0]

        blocks(0, nz, body)


def on_device(right_side, cond_x, cond_y, cond_z, kappa_sq, shifts, weights):
    dm = Dims(right_side.shape)
    nk = shifts.shape[0]
    nl = dm.nl
    count = lax.axis_size("slab")
    f32 = jnp.float32
    vmem = pl.BlockSpec(memory_space=pltpu.VMEM)
    smem = pl.BlockSpec(memory_space=pltpu.SMEM)
    anywhere = pl.BlockSpec(memory_space=pl.ANY)

    def params(mib):
        return pltpu.CompilerParams(vmem_limit_bytes=mib * MIB)

    def shape(*dims):
        return jax.ShapeDtypeStruct(dims, f32)

    def stacked(slots):
        return (nk, dm.stack_rows(slots), LANES)

    own = (dm.stack_rows(nl), LANES)
    raw = [pltpu.VMEM(right_side.shape, f32)] * 5
    sent = shape(dm.sent, LANES)
    inputs = (cond_x, cond_y, cond_z, kappa_sq, right_side)
    to_off, to_in = pl.pallas_call(
        functools.partial(pack_body, dm),
        out_shape=(sent, sent),
        in_specs=[anywhere] * 5,
        out_specs=(anywhere, anywhere),
        scratch_shapes=[
            raw,
            [pltpu.VMEM(own, f32)] * 6,
            pltpu.VMEM((2 * dm.plane, LANES), f32),
            pltpu.VMEM((2 * dm.nc * dm.half, LANES), f32),
            pltpu.VMEM((PAD, LANES), f32),
            pltpu.SemaphoreType.DMA((5,)),
            pltpu.SemaphoreType.DMA((2 * (10 + 3 * dm.nc),)),
        ],
        compiler_params=params(16),
        name="pack",
    )(*inputs)

    from_off = lax.ppermute(
        to_off,
        "slab",
        [pair for i in range(1, count - 1, 2) for pair in ((i, i + 1), (i + 1, i))],
    )
    from_in = lax.ppermute(to_in, "slab", [(i, i ^ 1) for i in range(count)])

    plane_stack = shape(nk, dm.plane, LANES)
    near_shapes = (
        shape(6, *own), shape(*stacked(nl - 1)), shape(*stacked(nl - 2)), shape(*stacked(nl - 3)),
        plane_stack, plane_stack, shape(6 * nk * 8, LANES),
    )
    near = pl.pallas_call(
        functools.partial(near_body, dm, nk),
        out_shape=near_shapes,
        in_specs=[anywhere] * 5 + [vmem, smem],
        out_specs=(vmem,) * 7,
        scratch_shapes=[
            raw,
            pltpu.VMEM(own, f32),
            pltpu.VMEM((dm.plane, LANES), f32),
            pltpu.VMEM(stacked(3), f32),
            pltpu.VMEM(stacked(2), f32),
            pltpu.VMEM(stacked(1), f32),
            pltpu.VMEM(stacked(nl + 1), f32),
            pltpu.SemaphoreType.DMA((5,)),
        ],
        compiler_params=params(36),
        cost_estimate=pl.CostEstimate(flops=10**7, bytes_accessed=30 * 10**6, transcendentals=0),
        name="near",
    )(*inputs, from_in, shifts)
    coef, w0a, w1a, w2a, part1, part2, acc = near

    w0b, w1b, w2b, moments = pl.pallas_call(
        functools.partial(far_body, dm, nk),
        out_shape=(shape(*stacked(1)), shape(*stacked(2)), shape(*stacked(3)), shape(1, LANES)),
        in_specs=[vmem] * 8 + [smem],
        out_specs=(vmem,) * 4,
        scratch_shapes=[
            pltpu.VMEM((6 * nk * 8, LANES), f32),
            pltpu.VMEM((3, dm.plane, LANES), f32),
            pltpu.VMEM(stacked(3), f32),
            pltpu.VMEM(stacked(2), f32),
            pltpu.VMEM(stacked(1), f32),
            pltpu.VMEM(stacked(5), f32),
        ],
        compiler_params=params(36),
        name="far",
    )(*near, from_off, shifts)

    everywhere = jnp.broadcast_to(moments[None], (count, 1, LANES))
    gathered = lax.all_to_all(everywhere, "slab", 0, 0)

    return pl.pallas_call(
        functools.partial(combine_body, dm, nk),
        out_shape=jax.ShapeDtypeStruct(right_side.shape, f32),
        in_specs=[vmem, smem] + [vmem] * 6,
        out_specs=vmem,
        compiler_params=params(20),
        name="combine",
    )(gathered, weights, w0a, w0b, w1a, w1b, w2a, w2b)


def solution(mesh):
    return jax.shard_map(
        on_device,
        mesh=mesh,
        in_specs=(
            P(("field", "slab"), None, None),
            P("slab", None, None),
            P("slab", None, None),
            P("slab", None, None),
            P("slab", None, None),
            P(),
            P(),
        ),
        out_specs=P(("field", "slab"), None, None),
        check_vma=False,
    )
```

time: 289 us -> 71.6 us (0.25)
  blocking collectives: 205 us -> 30.5 us
  other arithmetic: 52 us -> 0 us
  Pallas kernels: 0 us -> 30.5 us
  starting transfers between devices: 18.7 us -> 1.25 us
  waiting for transfers between devices: 10.5 us -> 1.95 us
  local copies, waits for them, and re-layouts: 1.79 us -> 6.9 us
    psum x5 -> x0, blocking collectives: 205 us -> none  [the longest x3 110 us: precond_total(): return lax.psum(inner_sum(residual, precond), 'slab')]
    reduce_sum x6 -> x0, other arithmetic: 37.4 us -> none  [the longest x5 32 us: inner_sum(): return jnp.sum(first * second, axis=(1, 2, 3))]
    all_to_all x0 -> x1, blocking collectives: none -> 30.5 us  [on_device(): gathered = lax.all_to_all(everywhere, 'slab', 0, 0)]
    pallas_call x0 -> x4, Pallas kernels: none -> 30.5 us  [the longest x1 11.5 us: on_device(): pl.pallas_call(functools.partial(far_body, dm, nk), out_shape=(shape(*sta...]
    ppermute x8 -> x2, starting transfers between devices: 18.7 us -> 1.25 us  [the longest x1 0.73 us: on_device(): lax.ppermute(to_off, 'slab', [pair for i in range(1, count - 1, 2) for pa...]
    ppermute x8 -> x2, waiting for transfers between devices: 10.5 us -> 1.95 us  [the longest x1 1.95 us: on_device(): from_in = lax.ppermute(to_in, 'slab', [(i, i ^ 1) for i in range(count)])]
    add x2 -> x0, other arithmetic: 7.79 us -> none  [on_device(): direction = precond + expand(norm_next / norm_now) * direction]
    unnamed x20 -> x28, local copies, waits for them, and re-layouts: 0.05 us -> 6.89 us
  transfers between devices with their start and end apart: 8 -> 2, of which waited for: 6 -> 1; matrix products, arithmetic and copies ran while one was open for 1% -> 0% of each run, Pallas kernels for 0% -> 15%
where the time goes in v2:
time: 71.6 us; the launch traced here: 71.2 us
  Pallas kernels  30.5 us (43%)
  blocking collectives  30.5 us (43%)
  local copies, waits for them, and re-layouts  6.9 us (10%)
  waiting for transfers between devices  1.95 us (3%)
  starting transfers between devices  1.25 us (2%)
    all_to_all x1, blocking collectives, on_device(): gathered = lax.all_to_all(everywhere, 'slab', 0, 0)  30.5 us
    pallas_call x1, Pallas kernels, on_device(): pl.pallas_call(functools.partial(far_body, dm, nk), out_shape=(shape(*sta...  11.5 us
    pallas_call x1, Pallas kernels, on_device(): pl.pallas_call(functools.partial(near_body, dm, nk), out_shape=near_shape...  10.8 us
    unnamed x28, local copies, waits for them, and re-layouts  6.89 us
    pallas_call x1, Pallas kernels, on_device(): pl.pallas_call(functools.partial(pack_body, dm), out_shape=(sent, sent),...  5.36 us
    pallas_call x1, Pallas kernels, on_device(): pl.pallas_call(functools.partial(combine_body, dm, nk), out_shape=jax.Sha...  2.92 us
    ppermute x1, waiting for transfers between devices, on_device(): from_in = lax.ppermute(to_in, 'slab', [(i, i ^ 1) for i in range(count)])  1.95 us
  transfers between devices with their start and end apart: 2, of which 1 were waited for; matrix products, arithmetic and copies ran while one was open for 0% of the time, Pallas kernels for 15%

profile of v2, /device:TPU:0, one launch (start us, length us, event | category | flops | bytes accessed | tf_op | source)
XLA Modules:
  0.0 71.2 jit_solution(12228368593199988770)
XLA Ops:
  0.0 0.0 copy-start.2
  0.0 1.0 %copy-done.2 = f32[4,64,512]{2,1,0:T(8,128)S(1)} copy-done((f32[4,64,512]{2,1,0:T(8,128)S(1)}, f32[4,64,512]{2,1,0:T(8,128)}, u32[]{:S(2)}) %copy-start.2) | copy-done | bytes 524312
  1.0 1.0 %copy-done.4 = f32[4,64,512]{2,1,0:T(8,128)S(1)} copy-done((f32[4,64,512]{2,1,0:T(8,128)S(1)}, f32[4,64,512]{2,1,0:T(8,128)}, u32[]{:S(2)}) %copy-start.4) | copy-done | bytes 524312
  2.1 0.0 copy-start.6
  2.1 1.0 %copy-done.6 = f32[4,64,512]{2,1,0:T(8,128)S(1)} copy-done((f32[4,64,512]{2,1,0:T(8,128)S(1)}, f32[4,64,512]{2,1,0:T(8,128)}, u32[]{:S(2)}) %copy-start.6) | copy-done | bytes 524312
  3.1 0.0 copy-start.8
  3.1 1.0 %copy-done.8 = f32[4,64,512]{2,1,0:T(8,128)S(1)} copy-done((f32[4,64,512]{2,1,0:T(8,128)S(1)}, f32[4,64,512]{2,1,0:T(8,128)}, u32[]{:S(2)}) %copy-start.8) | copy-done | bytes 524312
  4.2 0.0 copy-start.10
  4.2 1.0 %copy-done.10 = f32[4,64,512]{2,1,0:T(8,128)S(1)} copy-done((f32[4,64,512]{2,1,0:T(8,128)S(1)}, f32[4,64,512]{2,1,0:T(8,128)}, u32[]{:S(2)}) %copy-start.10) | copy-done | bytes 524312
  5.2 0.0 copy-start.3
  5.2 0.0 copy-start.5
  5.2 0.0 copy-start.11
  5.2 0.0 copy-start.12
  5.2 5.4 %pack.1 = (f32[2600,128]{1,0:T(8,128)S(1)}, f32[2600,128]{1,0:T(8,128)S(1)}) custom-call(f32[4,64,512]{2,1,0:T(8,128)S(1)} %copy-done.2, f32[4,64,512]{2,1,0:T(8,128)S(1)} %copy-done.4, f32[4,64,512]{2,1,0:T(8,128)S(1)} %copy-done.6, f32[4,64,512]{2,1,0:T(8,128)S(1)} %copy-done.8, f32[4,64,512]{2,1,0:T(8,128)S(1)} %copy-done.10), custom_call_target="tpu_custom_call" | custom-call | tf_op jit(solution)/shard_map/pack/pallas_call | solution.py:559
  10.6 0.5 collective-permute-start
  11.1 0.7 %collective-permute-start.1 = (f32[2600,128]{1,0:T(8,128)S(1)}, f32[2600,128]{1,0:T(8,128)S(1)}, u32[]{:S(2)}, u32[]{:S(2)}) collective-permute-start(f32[2600,128]{1,0:T(8,128)S(1)} %get-tuple-element.26), channel_id=1, source_target_pairs={{1,2},{2,1},{3,4},{4,3},{5,6},{6,5},{7,8},{8,7},{9,10},{10,9},{11,... | collective-permute-start | bytes 3993608 | tf_op jit(solution)/shard_map/ppermute | solution.py:577
  11.9 1.9 %collective-permute-done.from_in = f32[2600,128]{1,0:T(8,128)S(1)} collective-permute-done((f32[2600,128]{1,0:T(8,128)S(1)}, f32[2600,128]{1,0:T(8,128)S(1)}, u32[]{:S(2)}, u32[]{:S(2)}) %collective-permute-start) | collective-permute-done | bytes 1331232 | tf_op jit(solution)/shard_map/ppermute | solution.py:582
  13.8 0.0 copy-done.3
  13.8 0.0 copy-done.5
  13.8 0.0 copy-done.7
  13.8 0.0 copy-done.9
  13.8 0.0 copy-done.11
  13.8 0.0 copy-done.12
  13.9 10.8 %near.1 = (f32[6,1064,128]{2,1,0:T(8,128)S(1)}, f32[8,800,128]{2,1,0:T(8,128)S(1)}, f32[8,536,128]{2,1,0:T(8,128)S(1)}, f32[8,272,128]{2,1,0:T(8,128)S(1)}, f32[...) custom-call(f32[4,64,512]{2,1,0:T(8,128)S(1)} %copy-done.3, ...), custom_call_target="tpu_custom_call" | custom-call | flops 10000000 | bytes 30000000 | tf_op jit(solution)/shard_map/near/pallas_call | solution.py:589
  24.6 0.0 copy-start
  24.6 1.7 %copy-done = f32[8,800,128]{2,1,0:T(8,128)} copy-done((f32[8,800,128]{2,1,0:T(8,128)}, f32[8,800,128]{2,1,0:T(8,128)S(1)}, u32[]{:S(2)}) %copy-start) | copy-done | bytes 3276824
  26.3 0.0 collective-permute-done.1.from_off
  26.3 11.5 %far.1 = (f32[8,272,128]{2,1,0:T(8,128)S(1)}, f32[8,536,128]{2,1,0:T(8,128)S(1)}, f32[8,800,128]{2,1,0:T(8,128)S(1)}, f32[1,128]{1,0:T(1,128)S(1)}) custom-call(f32[6,1064,128]{2,1,0:T(8,128)S(1)} %get-tuple-element.19.coef, f32[8,800,128]{2,1,0:T(8,128)} %copy-done, f32[8,536,128]{2,1,0:T(8,128)S(1)} %get-tuple-element.21.w1a, ...), custom_call_target="tpu_custom_call" | custom-call | tf_op jit(solution)/shard_map/far/pallas_call | solution.py:610
  37.8 30.5 %all_to_all.5.moments = f32[16,1,128]{2,1,0:T(1,128)S(1)} all-to-all(f32[16,1,128]{2,1,0:T(1,128)S(1)} %broadcast_in_dim.9), channel_id=1, replica_groups=mesh['field'=2,'slab'=16] {'slab'}, dimensions={0} | all-to-all | bytes 16384 | tf_op jit(solution)/shard_map/all_to_all | solution.py:628
  68.3 0.0 copy-done.1
  68.3 0.0 copy-done.13
  68.3 2.9 %combine.1 = f32[4,64,512]{2,1,0:T(8,128)} custom-call(f32[16,1,128]{2,1,0:T(1,128)S(1)} %all_to_all.5.moments, f32[8]{0:T(128)S(1)} %copy-done.13, f32[8,800,128]{2,1,0:T(8,128)S(1)} %copy-done.1, f32[8,272,128]{2,1,0:T(8,128)S(1)} %get-tuple-element.28.w0b, f32[8,536,128]{2,1,0:T(8,128)S(1)} %get-tuple-element.21.w1a, ...), custom_call_target="tpu_custom_call" | custom-call | tf_op jit(solution)/shard_map/combine/pallas_call | solution.py:630
  (6 shorter events, 0.0 us)
Async XLA Ops:
  0.0 1.0 %copy-start.2 = (f32[4,64,512]{2,1,0:T(8,128)S(1)}, f32[4,64,512]{2,1,0:T(8,128)}, u32[]{:S(2)}) copy-start(f32[4,64,512]{2,1,0:T(8,128)} %cx.3) | copy-start | bytes 1572868
  1.0 1.0 %copy-start.4 = (f32[4,64,512]{2,1,0:T(8,128)S(1)}, f32[4,64,512]{2,1,0:T(8,128)}, u32[]{:S(2)}) copy-start(f32[4,64,512]{2,1,0:T(8,128)} %cy.3) | copy-start | bytes 1572868
  2.1 1.0 %copy-start.6 = (f32[4,64,512]{2,1,0:T(8,128)S(1)}, f32[4,64,512]{2,1,0:T(8,128)}, u32[]{:S(2)}) copy-start(f32[4,64,512]{2,1,0:T(8,128)} %cz.3) | copy-start | bytes 1572868
  3.1 1.0 %copy-start.8 = (f32[4,64,512]{2,1,0:T(8,128)S(1)}, f32[4,64,512]{2,1,0:T(8,128)}, u32[]{:S(2)}) copy-start(f32[4,64,512]{2,1,0:T(8,128)} %kappa.3) | copy-start | bytes 1572868
  4.2 1.0 %copy-start.10 = (f32[4,64,512]{2,1,0:T(8,128)S(1)}, f32[4,64,512]{2,1,0:T(8,128)}, u32[]{:S(2)}) copy-start(f32[4,64,512]{2,1,0:T(8,128)} %b.3) | copy-start | bytes 1572868
  5.2 8.6 %copy-start.3 = (f32[4,64,512]{2,1,0:T(8,128)S(1)}, f32[4,64,512]{2,1,0:T(8,128)}, u32[]{:S(2)}) copy-start(f32[4,64,512]{2,1,0:T(8,128)} %cx.3) | copy-start | bytes 1572868
  5.2 8.6 %copy-start.5 = (f32[4,64,512]{2,1,0:T(8,128)S(1)}, f32[4,64,512]{2,1,0:T(8,128)}, u32[]{:S(2)}) copy-start(f32[4,64,512]{2,1,0:T(8,128)} %cy.3) | copy-start | bytes 1572868
  5.2 8.6 %copy-start.7 = (f32[4,64,512]{2,1,0:T(8,128)S(1)}, f32[4,64,512]{2,1,0:T(8,128)}, u32[]{:S(2)}) copy-start(f32[4,64,512]{2,1,0:T(8,128)} %cz.3) | copy-start | bytes 1572868
  5.2 8.6 %copy-start.9 = (f32[4,64,512]{2,1,0:T(8,128)S(1)}, f32[4,64,512]{2,1,0:T(8,128)}, u32[]{:S(2)}) copy-start(f32[4,64,512]{2,1,0:T(8,128)} %kappa.3) | copy-start | bytes 1572868
  5.2 8.6 %copy-start.11 = (f32[4,64,512]{2,1,0:T(8,128)S(1)}, f32[4,64,512]{2,1,0:T(8,128)}, u32[]{:S(2)}) copy-start(f32[4,64,512]{2,1,0:T(8,128)} %b.3) | copy-start | bytes 1572868
  5.2 8.6 %copy-start.12 = (f32[8]{0:T(128)S(1)}, f32[8]{0:T(128)}, u32[]{:S(2)}) copy-start(f32[8]{0:T(128)} %shifts.3) | copy-start | bytes 100
  10.6 3.2 %collective-permute-start = (f32[2600,128]{1,0:T(8,128)S(1)}, f32[2600,128]{1,0:T(8,128)S(1)}, u32[]{:S(2)}, u32[]{:S(2)}) collective-permute-start(f32[2600,128]{1,0:T(8,128)S(1)} %get-tuple-element.18), channel_id=1, source_target_pairs={{0,1},{1,0},{2,3},{3,2},{4,5},{5,4},{6,7},{7,6},{8,9},{9,8},{10,11... | collective-permute-start | bytes 3993608 | tf_op jit(solution)/shard_map/ppermute | solution.py:582
  11.1 15.2 %collective-permute-start.1 = (f32[2600,128]{1,0:T(8,128)S(1)}, f32[2600,128]{1,0:T(8,128)S(1)}, u32[]{:S(2)}, u32[]{:S(2)}) collective-permute-start(f32[2600,128]{1,0:T(8,128)S(1)} %get-tuple-element.26), channel_id=1, source_target_pairs={{1,2},{2,1},{3,4},{4,3},{5,6},{6,5},{7,8},{8,7},{9,10},{10,9},{11,... | collective-permute-start | bytes 3993608 | tf_op jit(solution)/shard_map/ppermute | solution.py:577
  24.6 1.7 %copy-start = (f32[8,800,128]{2,1,0:T(8,128)}, f32[8,800,128]{2,1,0:T(8,128)S(1)}, u32[]{:S(2)}) copy-start(f32[8,800,128]{2,1,0:T(8,128)S(1)} %get-tuple-element.20.w0a) | copy-start | bytes 9830404
  26.3 42.0 %copy-start.1 = (f32[8,800,128]{2,1,0:T(8,128)S(1)}, f32[8,800,128]{2,1,0:T(8,128)}, u32[]{:S(2)}) copy-start(f32[8,800,128]{2,1,0:T(8,128)} %copy-done) | copy-start | bytes 9830404
  26.3 42.0 %copy-start.13 = (f32[8]{0:T(128)S(1)}, f32[8]{0:T(128)}, u32[]{:S(2)}) copy-start(f32[8]{0:T(128)} %weights.1) | copy-start | bytes 100

commit v3 on v2

--- a/solution.py
+++ b/solution.py
@@ -20,17 +20,23 @@
         self.half = self.nz // 2
         self.more = self.half + 8
         full, half = self.plane, self.nc * self.half
-        layout = [
-            ("pad", PAD), ("fz1", full), ("d1", full), ("x1", full), ("fy1", full),
-            ("d2", full), ("fx2", full), ("b1", full), ("b2", full),
-            ("fy2", half), ("d3", half), ("g3", half), ("fz2", self.nc * self.more),
-        ]
-        self.at = {}
-        total = 0
-        for name, size in layout:
-            self.at[name] = total
-            total += size
-        self.sent = total
+        faces_yz = [("pad", PAD), ("fz1", full), ("fy1", full)]
+        faces_x = [("gap", PAD), ("fx2", full), ("d2", full)]
+        edge = [("x1", full), ("d1", full), ("b1", full), ("b2", full)]
+        rest = [("fy2", half), ("d3", half), ("g3", half), ("fz2", self.nc * self.more)]
+        self.at_yz, self.rows_yz = self.layout(faces_yz)
+        self.at_x, self.rows_x = self.layout(faces_x)
+        self.at_edge, self.rows_edge = self.layout(edge)
+        self.at_rest, self.rows_rest = self.layout(rest)
+        self.at_all, self.rows_all = self.layout(faces_yz + faces_x + edge + rest)
+
+    @staticmethod
+    def layout(parts):
+        at, total = {}, 0
+        for name, rows in parts:
+            at[name] = total
+            total += rows
+        return at, total
 
     def stack_rows(self, slots):
         return slots * self.slot + PAD
@@ -142,71 +148,74 @@
     blocks(0, nz, all_faces)
 
 
-def load_own(sources, targets, sems):
-    copies = [
-        pltpu.make_async_copy(src, dst, sems.at[n])
-        for n, (src, dst) in enumerate(zip(sources, targets))
-    ]
-    for copy in copies:
-        copy.start()
-    for copy in copies:
-        copy.wait()
-
-
-def pack_body(dm, cx, cy, cz, kappa, b, to_off, to_in, raw, flats, fx2, g3, zero, in_sems, out_sems):
+def pack_body(
+    dm, conds, cz, kappa, b, to_swap, to_edge, to_rest, to_in, coef, temp,
+):
     par = lax.rem(lax.axis_index("slab"), 2)
+    side_field = lax.rem(lax.axis_index("field"), 2)
     nc, nz, nl = dm.nc, dm.nz, dm.nl
-    load_own((cx, cy, cz, kappa, b), raw, in_sems)
-    prepare(dm, par, *raw, flats)
-    bf, df, xf, yf, zf = [own_planes(dm, ref) for ref in flats[:5]]
-    other = 1 - par
-    zs = pl.multiple_of(other * dm.half, 8)
-    zm = pl.multiple_of(other * (nz - dm.more), 8)
-    zero[...] = jnp.zeros(zero.shape, jnp.float32)
-    copies = []
-
-    def send(out, name, src, start, rows, shift=0):
-        copy = pltpu.make_async_copy(
-            src.at[pl.ds(start, rows), :],
-            out.at[pl.ds(dm.at[name] + shift, rows), :],
-            out_sems.at[len(copies)],
-        )
-        copy.start()
-        copies.append(copy)
-
-    for side, (out, edge, step) in enumerate(((to_off, 0, 1), (to_in, nl - 1, -1))):
-        one, two, three = edge, edge + step, edge + 2 * step
-        for name, planes, p in (
-            ("fz1", zf, one), ("d1", df, one), ("x1", xf, one), ("fy1", yf, one),
-            ("d2", df, two), ("b1", bf, one), ("b2", bf, two),
-        ):
-            send(out, name, planes[p].ref, planes[p].base, dm.plane)
-        send(out, "pad", zero, 0, PAD)
-        for c in range(nc):
-            half = c * dm.half
-            send(out, "fy2", yf[two].ref, yf[two].base + c * nz + zs, dm.half, half)
-            send(out, "d3", df[three].ref, df[three].base + c * nz + zs, dm.half, half)
-            send(out, "fz2", zf[two].ref, zf[two].base + c * nz + zm, dm.more, c * dm.more)
-
-        def derived(z, side=side, one=one, two=two):
-            for c in range(nc):
-                fx2[pl.ds(side * dm.plane + c * nz + z, 8), :] = 0.5 * (
-                    xf[one].get(c, z) + xf[two].get(c, z)
-                )
-
-        def derived_half(n, side=side, two=two, three=three):
-            z = pl.multiple_of(zs + n, 8)
-            for c in range(nc):
-                g3[pl.ds((side * nc + c) * dm.half + n, 8), :] = (
-                    0.5 * (xf[two].get(c, z) + xf[three].get(c, z)) * bf[three].get(c, z)
-                )
-
-        blocks(0, nz, derived)
-        blocks(0, dm.half, derived_half)
-        send(out, "fx2", fx2, side * dm.plane, dm.plane)
-        send(out, "g3", g3, side * nc * dm.half, nc * dm.half)
-    for copy in copies:
-        copy.wait()
+    raw = [conds.at[0], conds.at[1], cz, kappa, b]
+    prepare(dm, par, *raw, [coef.at[n] for n in range(5)] + [temp])
+    bf, df, xf, yf, zf = [own_planes(dm, coef.at[n]) for n in range(5)]
+    zs = pl.multiple_of((1 - par) * dm.half, 8)
+    zm = pl.multiple_of((1 - par) * (nz - dm.more), 8)
+
+    def x_face(c, z, one, two):
+        return 0.5 * (xf[one].get(c, z) + xf[two].get(c, z))
+
+    def fill(out, at, z_count, sources):
+        def body(n):
+            for name, value in sources:
+                for c in range(nc):
+                    out[pl.ds(pl.multiple_of(n, 8) + (at[name] + c * z_count), 8), :] = value(c, n)
+
+        blocks(0, z_count, body, min(4, z_count // 8) if z_count % 32 == 0 else 1)
+
+    def edge(out, at, one, two):
+        fill(out, at, nz, [
+            ("x1", lambda c, n: xf[one].get(c, n)),
+            ("d1", lambda c, n: df[one].get(c, n)),
+            ("b1", lambda c, n: bf[one].get(c, n)),
+            ("b2", lambda c, n: bf[two].get(c, n)),
+        ])
+
+    def rest(out, at, two, three):
+        fill(out, at, dm.half, [
+            ("fy2", lambda c, n: yf[two].get(c, zs + n)),
+            ("d3", lambda c, n: df[three].get(c, zs + n)),
+            ("g3", lambda c, n: x_face(c, zs + n, two, three) * bf[three].get(c, zs + n)),
+        ])
+        fill(out, at, dm.more, [("fz2", lambda c, n: zf[two].get(c, zm + n))])
+
+    def yz(out, at, one):
+        out[at["pad"] : at["pad"] + PAD, :] = jnp.zeros((PAD, LANES), jnp.float32)
+        fill(out, at, nz, [
+            ("fz1", lambda c, n: zf[one].get(c, n)),
+            ("fy1", lambda c, n: yf[one].get(c, n)),
+        ])
+
+    def x(out, at, one, two):
+        out[at["gap"] : at["gap"] + PAD, :] = jnp.zeros((PAD, LANES), jnp.float32)
+        fill(out, at, nz, [
+            ("fx2", lambda c, n: x_face(c, n, one, two)),
+            ("d2", lambda c, n: df[two].get(c, n)),
+        ])
+
+    @pl.when(side_field == 0)
+    def _():
+        yz(to_swap, dm.at_yz, 0)
+
+    @pl.when(side_field == 1)
+    def _():
+        x(to_swap, dm.at_x, 0, 1)
+
+    edge(to_edge, dm.at_edge, 0, 1)
+    rest(to_rest, dm.at_rest, 1, 2)
+    last = nl - 1
+    yz(to_in, dm.at_all, last)
+    x(to_in, dm.at_all, last, last - 1)
+    edge(to_in, dm.at_all, last, last - 1)
+    rest(to_in, dm.at_all, last - 1, last - 2)
 
 
 class Steps:
@@ -215,7 +224,7 @@
         self.zs = pl.multiple_of(par * dm.half, 8)
         self.zm = pl.multiple_of(par * (dm.nz - dm.more), 8)
 
-    def sweep(self, half, body, unroll=2):
+    def sweep(self, half, body, unroll=4):
         if half:
             blocks(self.zs, self.dm.half, body, unroll)
         else:
@@ -245,17 +254,7 @@
                 if own:
                     self.add(0, k, self.total(rhs, value))
 
-        self.sweep(half, body, 1)
-
-    def inverses(self, d, r):
-        def body(z):
-            diagonal = self.tiles(d, z)
-            for k in range(self.nk):
-                s = self.shifts[k]
-                for c in range(self.dm.nc):
-                    r.put(c, z, 1.0 / (diagonal[c] + s), k)
-
-        self.sweep(False, body, 1)
+        self.sweep(half, body, 2)
 
     def apply(self, v, sides, out, r=None, yz=None, base=None, half=False, moment=None):
         nc = self.dm.nc
@@ -334,51 +333,53 @@
             ref[k, n * dm.slot : n * dm.slot + PAD, :] = jnp.zeros((PAD, LANES), jnp.float32)
 
 
-def halo_planes(dm, ref, st):
-    planes = {n: Plane(ref, dm.at[n], dm.nz) for n in ("fz1", "d1", "x1", "fy1", "d2", "fx2", "b1", "b2")}
-    for n in ("fy2", "d3", "g3"):
-        planes[n] = Plane(ref, dm.at[n], dm.half, st.zs)
-    planes["fz2"] = Plane(ref, dm.at["fz2"], dm.more, st.zm)
+def halo_planes(dm, st, *parts):
+    planes = {}
+    for ref, at in parts:
+        for name, row in at.items():
+            if name in ("fy2", "d3", "g3"):
+                planes[name] = Plane(ref, row, dm.half, st.zs)
+            elif name == "fz2":
+                planes[name] = Plane(ref, row, dm.more, st.zm)
+            else:
+                planes[name] = Plane(ref, row, dm.nz)
     return planes
 
 
 def near_body(
-    dm, nk, cx, cy, cz, kappa, b, from_in, shifts,
-    coef, w0a, w1a, w2a, part1, part2, acc,
-    raw, temp, extra, w0h, w1h, w2h, inv, sems,
+    dm, nk, flats, from_in, shifts, w0a, w1a, w2a, part1, part2, acc, coef, inv_out,
+    extra, w0h, w1h, w2h, inv,
 ):
     par = lax.rem(lax.axis_index("slab"), 2)
     nl, nc, nz = dm.nl, dm.nc, dm.nz
     last = nl - 1
-    load_own((cx, cy, cz, kappa, b), raw, sems)
-    prepare(dm, par, *raw, [coef.at[n] for n in range(5)] + [temp])
-    bf, df, xf, yf, zf = [own_planes(dm, coef.at[n]) for n in range(5)]
+    bf, df, raw_x, yf, zf = [own_planes(dm, flats.at[n]) for n in range(5)]
+    xf = own_planes(dm, coef)
     st = Steps(dm, nk, par, acc, shifts)
-    hp = halo_planes(dm, from_in, st)
+    hp = halo_planes(dm, st, (from_in, dm.at_all))
     acc[...] = jnp.zeros(acc.shape, jnp.float32)
     for ref in (w0a, w1a, w2a, w0h, w1h, w2h):
         clear_pads(dm, nk, ref)
-    d_next = Plane(extra, 0, nz)
-    raw0 = Plane(coef.at[5], PAD, nz)
+    d_last, d_next = Plane(extra.at[0], 0, nz), Plane(extra.at[1], 0, nz)
 
     def edges(z):
         for c in range(nc):
-            here, there = xf[last].get(c, z), hp["x1"].get(c, z)
-            raw0.put(c, z, xf[0].get(c, z))
-            df[last].put(c, z, df[last].get(c, z) + 0.5 * there)
+            here, there = raw_x[last].get(c, z), hp["x1"].get(c, z)
+            d_last.put(c, z, df[last].get(c, z) + 0.5 * there)
             d_next.put(c, z, hp["d1"].get(c, z) + 0.5 * here)
             for p in range(last):
-                xf[p].put(c, z, 0.5 * (xf[p].get(c, z) + xf[p + 1].get(c, z)))
+                xf[p].put(c, z, 0.5 * (raw_x[p].get(c, z) + raw_x[p + 1].get(c, z)))
             xf[last].put(c, z, 0.5 * (here + there))
 
-    blocks(0, nz, edges)
+    blocks(0, nz, edges, 2)
+    df[last] = d_last
 
     W0 = stack(dm, w0a, range(1, nl)) | stack(dm, w0h, (nl, nl + 1))
     far = Plane(w0h, PAD + 2 * dm.slot, dm.half, st.zs)
     W1 = stack(dm, w1a, range(2, nl)) | stack(dm, w1h, (nl,))
     W1[nl + 1] = Plane(w1h, PAD + dm.slot, nz)
     W2 = stack(dm, w2a, range(3, nl)) | stack(dm, w2h, (nl,))
-    R = stack(dm, inv, range(1, nl + 2))
+    R = stack(dm, inv_out, (1, 2)) | stack(dm, inv, range(3, nl + 2))
     I1, I2 = Plane(part1, 0, nz), Plane(part2, 0, nz)
 
     for p in range(1, nl):
@@ -410,65 +411,114 @@
     st.face_sum(W2[last], (xf[last], W2[nl]), half=True)
 
 
-def far_body(
-    dm, nk, coef, w0a, w1a, w2a, part1, part2, acc_in, from_off, shifts,
-    w0b, w1b, w2b, moments, acc, extra, w0h, w1h, w2h, inv,
+def far_a_body(
+    dm, nk, flats, coef, w0a, w1a, w2a, part1, part2, acc_in, inv, from_edge, shifts,
+    w0b, w1b, w2b, part3, acc, edge, w0h, inv_out,
 ):
     index = lax.axis_index("slab")
     par = lax.rem(index, 2)
     has_off = jnp.where(jnp.logical_and(index > 0, index < lax.axis_size("slab") - 1), 0.5, 0.0)
     nl, nc, nz = dm.nl, dm.nc, dm.nz
-    bf, df, xf, yf, zf = [own_planes(dm, coef.at[n]) for n in range(5)]
-    raw0 = Plane(coef.at[5], PAD, nz)
+    bf, df, raw_x, yf, zf = [own_planes(dm, flats.at[n]) for n in range(5)]
+    xf = own_planes(dm, coef)
     st = Steps(dm, nk, par, acc, shifts)
-    hp = halo_planes(dm, from_off, st)
+    hp = halo_planes(dm, st, (from_edge, dm.at_edge))
     acc[...] = acc_in[...]
-    for ref in (w0b, w1b, w2b, w0h, w1h, w2h):
+    for ref in (w0b, w1b, w2b, w0h):
         clear_pads(dm, nk, ref)
-    d_here, d_next, x_edge = [Plane(extra.at[n], 0, nz) for n in range(3)]
+    d_here, d_next, x_edge = [Plane(edge.at[n], 0, nz) for n in range(3)]
 
     def edges(z):
         for c in range(nc):
-            here, there = raw0.get(c, z), hp["x1"].get(c, z)
+            here, there = raw_x[0].get(c, z), hp["x1"].get(c, z)
             d_here.put(c, z, df[0].get(c, z) + 0.5 * there)
             d_next.put(c, z, hp["d1"].get(c, z) + 0.5 * here)
             x_edge.put(c, z, has_off * (here + there))
 
-    blocks(0, nz, edges)
-
-    W0 = stack(dm, w0a, range(1, nl)) | stack(dm, w0b, (0,)) | stack(dm, w0h, (-1, -2))
-    far = Plane(w0h, PAD + 2 * dm.slot, dm.half, st.zs)
-    W1 = stack(dm, w1a, range(2, nl)) | stack(dm, w1b, (0, 1)) | stack(dm, w1h, (-1, -2))
-    W2 = stack(dm, w2a, range(3, nl)) | stack(dm, w2b, (0, 1, 2)) | stack(dm, w2h, (-1,))
-    R = stack(dm, inv, (-2, -1, 0, 1, 2))
-    I1, I2 = Plane(part1, 0, nz), Plane(part2, 0, nz)
+    blocks(0, nz, edges, 4)
+
+    W0 = stack(dm, w0a, range(1, nl)) | stack(dm, w0b, (0,)) | stack(dm, w0h, (-1,))
+    W1 = stack(dm, w1a, range(2, nl)) | stack(dm, w1b, (0, 1))
+    W2 = stack(dm, w2a, range(3, nl)) | stack(dm, w2b, (1, 2))
+    R = stack(dm, inv_out, (-1, 0)) | stack(dm, inv, (1, 2))
+    I1, I2, I3 = Plane(part1, 0, nz), Plane(part2, 0, nz), Plane(part3, 0, nz)
     yz = [(yf[p], zf[p]) for p in range(nl)]
 
-    st.inverses(df[1], R[1])
-    st.inverses(df[2], R[2])
     st.start(d_here, bf[0], W0[0], R[0], own=True)
     st.start(d_next, hp["b1"], W0[-1], R[-1])
-    st.start(hp["d2"], hp["b2"], W0[-2], R[-2])
-    st.start(hp["d3"], hp["g3"], far, half=True)
 
     st.apply(W0[1], [(xf[0], W0[0])], W1[1], R[1], base=I1, moment=1)
     st.apply(W0[0], [(x_edge, W0[-1]), (xf[0], W0[1])], W1[0], R[0], yz[0], moment=1)
+    st.apply(W1[2], [(xf[1], W1[1])], W2[2], R[2], base=I2, moment=3)
+    st.apply(W1[1], [(xf[0], W1[0]), (xf[1], W1[2])], W2[1], R[1], yz[1], moment=3)
+    st.apply(W1[0], [(xf[0], W1[1])], I3, yz=yz[0])
+    for p in range(1, min(3, nl - 1)):
+        st.face_sum(W2[p], (xf[p], W2[p + 1]), yz[p])
+
+
+def far_b_body(
+    dm, nk, flats, coef, w0b, w0h, w1b, w2b, part3, acc_in, edge, inv_in, from_edge, swap_a, swap_b, shifts,
+    w2c, acc, w1h, inv_out, w0f, shared,
+):
+    par = lax.rem(lax.axis_index("slab"), 2)
+    side_field = lax.rem(lax.axis_index("field"), 2)
+    nl, nc, nz = dm.nl, dm.nc, dm.nz
+    bf, df, raw_x, yf, zf = [own_planes(dm, flats.at[n]) for n in range(5)]
+    xf = own_planes(dm, coef)
+    st = Steps(dm, nk, par, acc, shifts)
+
+    @pl.when(side_field == 0)
+    def _():
+        shared[0 : dm.rows_yz, :] = swap_a[...]
+        shared[dm.rows_yz :, :] = swap_b[...]
+
+    @pl.when(side_field == 1)
+    def _():
+        shared[0 : dm.rows_yz, :] = swap_b[...]
+        shared[dm.rows_yz :, :] = swap_a[...]
+
+    at_x = {name: row + dm.rows_yz for name, row in dm.at_x.items()}
+    hp = halo_planes(dm, st, (from_edge, dm.at_edge), (shared, dm.at_yz), (shared, at_x))
+    acc[...] = acc_in[...]
+    for ref in (w2c, w1h, w0f):
+        clear_pads(dm, nk, ref)
+    x_edge = Plane(edge.at[2], 0, nz)
+    W0 = stack(dm, w0b, (0,)) | stack(dm, w0h, (-1,)) | stack(dm, w0f, (-2,))
+    W1 = stack(dm, w1b, (0, 1)) | stack(dm, w1h, (-1,))
+    W2 = stack(dm, w2b, (1, 2)) | stack(dm, w2c, (0,))
+    R = stack(dm, inv_in, (-1, 0)) | stack(dm, inv_out, (-2,))
+    st.start(hp["d2"], hp["b2"], W0[-2], R[-2])
     st.apply(
         W0[-1], [(hp["fx2"], W0[-2]), (x_edge, W0[0])], W1[-1], R[-1], (hp["fy1"], hp["fz1"])
     )
+    st.apply(W1[0], [(x_edge, W1[-1])], W2[0], R[0], base=Plane(part3, 0, nz), moment=3)
+    st.face_sum(W2[0], (xf[0], W2[1]), (yf[0], zf[0]))
+
+
+def far_c_body(
+    dm, nk, w0h, w0f, w1b, w1h, w2c, acc_in, edge, inv_in, inv2, from_rest, shared, shifts,
+    moments, acc, w0g, w1g, w2g,
+):
+    par = lax.rem(lax.axis_index("slab"), 2)
+    nz = dm.nz
+    st = Steps(dm, nk, par, acc, shifts)
+    at_x = {name: row + dm.rows_yz for name, row in dm.at_x.items()}
+    hp = halo_planes(dm, st, (from_rest, dm.at_rest), (shared, dm.at_yz), (shared, at_x))
+    acc[...] = acc_in[...]
+    x_edge = Plane(edge.at[2], 0, nz)
+    far, near, w2 = [Plane(ref, 0, dm.half, st.zs) for ref in (w0g, w1g, w2g)]
+    W0 = stack(dm, w0h, (-1,)) | stack(dm, w0f, (-2,))
+    W1 = stack(dm, w1b, (0, 1)) | stack(dm, w1h, (-1,))
+    W2 = stack(dm, w2c, (0,))
+    R = stack(dm, inv_in, (-1, 0)) | stack(dm, inv2, (-2,))
+    st.start(hp["d3"], hp["g3"], far, half=True)
     st.apply(
-        W0[-2], [(None, far), (hp["fx2"], W0[-1])], W1[-2], R[-2], (hp["fy2"], hp["fz2"]), half=True
-    )
-    st.apply(W1[2], [(xf[1], W1[1])], W2[2], R[2], base=I2, moment=3)
-    st.apply(W1[1], [(xf[0], W1[0]), (xf[1], W1[2])], W2[1], R[1], yz[1], moment=3)
-    st.apply(W1[0], [(x_edge, W1[-1]), (xf[0], W1[1])], W2[0], R[0], yz[0], moment=3)
+        W0[-2], [(None, far), (hp["fx2"], W0[-1])], near, R[-2], (hp["fy2"], hp["fz2"]), half=True
+    )
     st.apply(
-        W1[-1], [(hp["fx2"], W1[-2]), (x_edge, W1[0])], W2[-1], R[-1],
-        (hp["fy1"], hp["fz1"]), half=True,
-    )
-    for p in range(min(3, nl - 1)):
-        st.face_sum(W2[p], (xf[p], W2[p + 1]), yz[p])
-    st.face_sum(W2[0], (x_edge, W2[-1]), half=True)
+        W1[-1], [(hp["fx2"], near), (x_edge, W1[0])], w2, R[-1], (hp["fy1"], hp["fz1"]), half=True
+    )
+    st.face_sum(W2[0], (x_edge, w2), half=True)
 
     number = 6 * nk
     sums = jnp.sum(acc[...].reshape(number, 8, LANES), axis=1)
@@ -506,7 +556,7 @@
     return x
 
 
-def combine_body(dm, nk, moments, weights, w0a, w0b, w1a, w1b, w2a, w2b, out):
+def combine_body(dm, nk, moments, weights, w0a, w0b, w1a, w1b, w2a, w2b, w2c, out):
     par = lax.rem(lax.axis_index("slab"), 2)
     nl, nc, nz = dm.nl, dm.nc, dm.nz
     sums = jnp.sum(moments[...].reshape(-1, LANES), axis=0, keepdims=True)
@@ -517,7 +567,7 @@
     ]
     W0 = stack(dm, w0a, range(1, nl)) | stack(dm, w0b, (0,))
     W1 = stack(dm, w1a, range(2, nl)) | stack(dm, w1b, (0, 1))
-    W2 = stack(dm, w2a, range(3, nl)) | stack(dm, w2b, (0, 1, 2))
+    W2 = stack(dm, w2a, range(3, nl)) | stack(dm, w2b, (1, 2)) | stack(dm, w2c, (0,))
     for p in range(nl):
         layer = jnp.where(par == 0, p, nl - 1 - p)
 
@@ -541,7 +591,6 @@
     f32 = jnp.float32
     vmem = pl.BlockSpec(memory_space=pltpu.VMEM)
     smem = pl.BlockSpec(memory_space=pltpu.SMEM)
-    anywhere = pl.BlockSpec(memory_space=pl.ANY)
 
     def params(mib):
         return pltpu.CompilerParams(vmem_limit_bytes=mib * MIB)
@@ -553,76 +602,79 @@
         return (nk, dm.stack_rows(slots), LANES)
 
     own = (dm.stack_rows(nl), LANES)
-    raw = [pltpu.VMEM(right_side.shape, f32)] * 5
-    sent = shape(dm.sent, LANES)
-    inputs = (cond_x, cond_y, cond_z, kappa_sq, right_side)
-    to_off, to_in = pl.pallas_call(
+    half_stack = pltpu.VMEM((nk, dm.nc * dm.half, LANES), f32)
+    plane_stack = shape(nk, dm.plane, LANES)
+    sums = shape(6 * nk * 8, LANES)
+    assert dm.rows_yz == dm.rows_x
+
+    to_swap, to_edge, to_rest, to_in, flats = pl.pallas_call(
         functools.partial(pack_body, dm),
-        out_shape=(sent, sent),
-        in_specs=[anywhere] * 5,
-        out_specs=(anywhere, anywhere),
+        out_shape=(
+            shape(dm.rows_yz, LANES), shape(dm.rows_edge, LANES), shape(dm.rows_rest, LANES),
+            shape(dm.rows_all, LANES), shape(5, *own),
+        ),
+        in_specs=[vmem] * 4,
+        out_specs=(vmem,) * 5,
         scratch_shapes=[
-            raw,
-            [pltpu.VMEM(own, f32)] * 6,
-            pltpu.VMEM((2 * dm.plane, LANES), f32),
-            pltpu.VMEM((2 * dm.nc * dm.half, LANES), f32),
-            pltpu.VMEM((PAD, LANES), f32),
-            pltpu.SemaphoreType.DMA((5,)),
-            pltpu.SemaphoreType.DMA((2 * (10 + 3 * dm.nc),)),
+            pltpu.VMEM(own, f32),
         ],
-        compiler_params=params(16),
+        compiler_params=params(20),
         name="pack",
-    )(*inputs)
-
-    from_off = lax.ppermute(
-        to_off,
-        "slab",
-        [pair for i in range(1, count - 1, 2) for pair in ((i, i + 1), (i + 1, i))],
-    )
+    )(jnp.stack([cond_x, cond_y]), cond_z, kappa_sq, right_side)
+
+    outward = [pair for i in range(1, count - 1, 2) for pair in ((i, i + 1), (i + 1, i))]
+    swap_a = lax.ppermute(to_swap, "slab", outward)
+    from_edge = lax.ppermute(to_edge, "slab", outward)
+    from_rest = lax.ppermute(to_rest, "slab", outward)
     from_in = lax.ppermute(to_in, "slab", [(i, i ^ 1) for i in range(count)])
-
-    plane_stack = shape(nk, dm.plane, LANES)
-    near_shapes = (
-        shape(6, *own), shape(*stacked(nl - 1)), shape(*stacked(nl - 2)), shape(*stacked(nl - 3)),
-        plane_stack, plane_stack, shape(6 * nk * 8, LANES),
-    )
-    near = pl.pallas_call(
-        functools.partial(near_body, dm, nk),
-        out_shape=near_shapes,
-        in_specs=[anywhere] * 5 + [vmem, smem],
-        out_specs=(vmem,) * 7,
-        scratch_shapes=[
-            raw,
-            pltpu.VMEM(own, f32),
-            pltpu.VMEM((dm.plane, LANES), f32),
-            pltpu.VMEM(stacked(3), f32),
-            pltpu.VMEM(stacked(2), f32),
-            pltpu.VMEM(stacked(1), f32),
-            pltpu.VMEM(stacked(nl + 1), f32),
-            pltpu.SemaphoreType.DMA((5,)),
-        ],
-        compiler_params=params(36),
-        cost_estimate=pl.CostEstimate(flops=10**7, bytes_accessed=30 * 10**6, transcendentals=0),
-        name="near",
-    )(*inputs, from_in, shifts)
-    coef, w0a, w1a, w2a, part1, part2, acc = near
-
-    w0b, w1b, w2b, moments = pl.pallas_call(
-        functools.partial(far_body, dm, nk),
-        out_shape=(shape(*stacked(1)), shape(*stacked(2)), shape(*stacked(3)), shape(1, LANES)),
-        in_specs=[vmem] * 8 + [smem],
-        out_specs=(vmem,) * 4,
-        scratch_shapes=[
-            pltpu.VMEM((6 * nk * 8, LANES), f32),
-            pltpu.VMEM((3, dm.plane, LANES), f32),
-            pltpu.VMEM(stacked(3), f32),
-            pltpu.VMEM(stacked(2), f32),
-            pltpu.VMEM(stacked(1), f32),
-            pltpu.VMEM(stacked(5), f32),
-        ],
-        compiler_params=params(36),
-        name="far",
-    )(*near, from_off, shifts)
+    fields = lax.axis_size("field")
+
+    def call(body, name, mib, results, scratch, operands, cost):
+        return pl.pallas_call(
+            functools.partial(body, dm, nk),
+            out_shape=results,
+            in_specs=[vmem] * len(operands) + [smem],
+            out_specs=(vmem,) * len(results),
+            scratch_shapes=scratch,
+            compiler_params=params(mib),
+            cost_estimate=pl.CostEstimate(
+                flops=10**6, bytes_accessed=cost * 3 * 10**6, transcendentals=0
+            ),
+            name=name,
+        )(*operands, shifts)
+
+    def wide(slots):
+        return shape(*stacked(slots))
+
+    def held(slots):
+        return pltpu.VMEM(stacked(slots), f32)
+
+    w0a, w1a, w2a, part1, part2, acc, coef, inv12 = call(
+        near_body, "near", 20,
+        (wide(nl - 1), wide(nl - 2), wide(nl - 3), plane_stack, plane_stack, sums, shape(*own), wide(2)),
+        [pltpu.VMEM((2, dm.plane, LANES), f32), held(3), held(2), held(1), held(nl - 1)],
+        (flats, from_in), 10,
+    )
+    swap_a, acc = lax.optimization_barrier((swap_a, acc))
+    swap_b = lax.ppermute(swap_a, "field", [(i, i ^ 1) for i in range(fields)])
+    w0b, w1b, w2b, part3, acc, edge, w0h, inv = call(
+        far_a_body, "far_a", 20,
+        (wide(1), wide(2), wide(2), plane_stack, sums, shape(3, dm.plane, LANES), wide(1), wide(2)),
+        [],
+        (flats, coef, w0a, w1a, w2a, part1, part2, acc, inv12, from_edge), 6,
+    )
+    w2c, acc, w1h, inv2, w0f, shared = call(
+        far_b_body, "far_b", 20,
+        (wide(1), sums, wide(1), wide(1), wide(1), shape(dm.rows_yz + dm.rows_x, LANES)),
+        [],
+        (flats, coef, w0b, w0h, w1b, w2b, part3, acc, edge, inv, from_edge, swap_a, swap_b), 3,
+    )
+    moments, _ = call(
+        far_c_body, "far_c", 20,
+        (shape(1, LANES), sums),
+        [half_stack] * 3,
+        (w0h, w0f, w1b, w1h, w2c, acc, edge, inv, inv2, from_rest, shared), 2,
+    )
 
     everywhere = jnp.broadcast_to(moments[None], (count, 1, LANES))
     gathered = lax.all_to_all(everywhere, "slab", 0, 0)
@@ -630,11 +682,11 @@
     return pl.pallas_call(
         functools.partial(combine_body, dm, nk),
         out_shape=jax.ShapeDtypeStruct(right_side.shape, f32),
-        in_specs=[vmem, smem] + [vmem] * 6,
+        in_specs=[vmem, smem] + [vmem] * 7,
         out_specs=vmem,
         compiler_params=params(20),
         name="combine",
-    )(gathered, weights, w0a, w0b, w1a, w1b, w2a, w2b)
+    )(gathered, weights, w0a, w0b, w1a, w1b, w2a, w2b, w2c)
 
 
 def solution(mesh):

time: 71.6 us -> 54.2 us (0.76)
  Pallas kernels: 30.5 us -> 22.4 us
  blocking collectives: 30.5 us -> 23.6 us
  local copies, waits for them, and re-layouts: 6.9 us -> 0.29 us
  starting transfers between devices: 1.25 us -> 5.49 us
  other arithmetic: 0 us -> 1.39 us
  waiting for transfers between devices: 1.95 us -> 0.65 us
    pallas_call x3 -> x5, Pallas kernels: 27.6 us -> 19.7 us  [the longest x4 18.3 us: call(): pl.pallas_call(functools.partial(body, dm, nk), out_shape=results, in_spe...]
    all_to_all x1, blocking collectives: 30.5 us -> 23.6 us  [on_device(): gathered = lax.all_to_all(everywhere, 'slab', 0, 0)]
    unnamed x28 -> x10, local copies, waits for them, and re-layouts: 6.89 us -> 0.28 us
    ppermute x1 -> x4, starting transfers between devices: 0.73 us -> 4.97 us  [the longest x1 2.93 us: on_device(): swap_b = lax.ppermute(swap_a, 'field', [(i, i ^ 1) for i in range(fields)])]
    another operation x0 -> x1, other arithmetic: none -> 1.39 us  [on_device(): jnp.stack([cond_x, cond_y])]
    ppermute x1, waiting for transfers between devices: 1.95 us -> 0.63 us  [on_device(): from_in = lax.ppermute(to_in, 'slab', [(i, i ^ 1) for i in range(count)])]
  transfers between devices with their start and end apart: 2 -> 5, of which waited for: 1 -> 1; matrix products, arithmetic and copies ran while one was open for 0% -> 0% of each run, Pallas kernels for 15% -> 30%
where the time goes in v3:
time: 54.2 us; the launch traced here: 53.9 us
  blocking collectives  23.6 us (44%)
  Pallas kernels  22.4 us (41%)
  starting transfers between devices  5.49 us (10%)
  other arithmetic  1.39 us (3%)
  waiting for transfers between devices  0.65 us (1%)
    all_to_all x1, blocking collectives, on_device(): gathered = lax.all_to_all(everywhere, 'slab', 0, 0)  23.6 us
    pallas_call x4, Pallas kernels, call(): pl.pallas_call(functools.partial(body, dm, nk), out_shape=results, in_spe...  18.3 us
    ppermute x1, starting transfers between devices, on_device(): swap_b = lax.ppermute(swap_a, 'field', [(i, i ^ 1) for i in range(fields)])  2.93 us
    pallas_call x1, Pallas kernels, on_device(): pl.pallas_call(functools.partial(combine_body, dm, nk), out_shape=jax.Sha...  2.76 us
    another operation x1, other arithmetic, on_device(): jnp.stack([cond_x, cond_y])  1.39 us
    pallas_call x1, Pallas kernels, on_device(): pl.pallas_call(functools.partial(pack_body, dm), out_shape=(shape(dm.rows...  1.35 us
  transfers between devices with their start and end apart: 5, of which 1 were waited for; matrix products, arithmetic and copies ran while one was open for 0% of the time, Pallas kernels for 30%

profile of v3, /device:TPU:0, one launch (start us, length us, event | category | flops | bytes accessed | tf_op | source)
XLA Modules:
  0.0 53.9 jit_solution(15463108633246096014)
XLA Ops:
  0.0 0.0 copy-start.1
  0.0 0.0 copy-start
  0.0 0.0 copy-start.2
  0.0 1.4 %pad_maximum_fusion.conds = f32[2,4,64,512]{3,2,1,0:T(8,128)S(1)} fusion(f32[1,4,64,512]{3,2,1,0:T(8,128)} %bitcast.4, f32[1,4,64,512]{3,2,1,0:T(8,128)} %bitcast.5), kind=kLoop, calls=%fused_computation | loop fusion | flops 262144 | bytes 2097152 | tf_op jit(solution)/shard_map/stack | solution.py:623
  1.4 0.0 copy-done.1
  1.4 0.1 copy-done
  1.5 0.2 copy-done.2
  1.7 0.0 copy-start.3
  1.7 1.3 %pack.1 = (f32[520,128]{1,0:T(8,128)S(1)}, f32[1024,128]{1,0:T(8,128)S(1)}, f32[544,128]{1,0:T(8,128)S(1)}, f32[2608,128]{1,0:T(8,128)S(1)}, f32[5,1064,128]{2,1,0:T(8,128)S(1)}) custom-call(f32[2,4,64,512]{3,2,1,0:T(8,128)S(1)} %pad_maximum_fusion.conds, f32[4,64,512]{2,1,0:T(8,128)S(1)} %copy-done, f32[4,64,512]{2,1,0:T(8,128)S(1)} %copy-done.1, ...), custom_call_target="tpu_custom_call" | custom-call | tf_op jit(solution)/shard_map/pack/pallas_call | solution.py:610
  3.0 0.5 collective-permute-start
  3.5 0.7 %collective-permute-start.1 = (f32[520,128]{1,0:T(8,128)S(1)}, f32[520,128]{1,0:T(8,128)S(1)}, u32[]{:S(2)}, u32[]{:S(2)}) collective-permute-start(f32[520,128]{1,0:T(8,128)S(1)} %get-tuple-element.43), channel_id=1, source_target_pairs={{1,2},{2,1},{3,4},{4,3},{5,6},{6,5},{7,8},{8,7},{9,10},{10,9},{11,... | collective-permute-start | bytes 798728 | tf_op jit(solution)/shard_map/ppermute | solution.py:626
  4.2 0.7 %collective-permute-start.2 = (f32[1024,128]{1,0:T(8,128)S(1)}, f32[1024,128]{1,0:T(8,128)S(1)}, u32[]{:S(2)}, u32[]{:S(2)}) collective-permute-start(f32[1024,128]{1,0:T(8,128)S(1)} %get-tuple-element.47), channel_id=1, source_target_pairs={{1,2},{2,1},{3,4},{4,3},{5,6},{6,5},{7,8},{8,7},{9,10},{10,9},{11,... | collective-permute-start | bytes 1572872 | tf_op jit(solution)/shard_map/ppermute | solution.py:627
  4.9 0.7 %collective-permute-start.4 = (f32[544,128]{1,0:T(8,128)S(1)}, f32[544,128]{1,0:T(8,128)S(1)}, u32[]{:S(2)}, u32[]{:S(2)}) collective-permute-start(f32[544,128]{1,0:T(8,128)S(1)} %get-tuple-element.62), channel_id=1, source_target_pairs={{1,2},{2,1},{3,4},{4,3},{5,6},{6,5},{7,8},{8,7},{9,10},{10,9},{11,... | collective-permute-start | bytes 835592 | tf_op jit(solution)/shard_map/ppermute | solution.py:628
  5.6 0.6 %collective-permute-done.from_in = f32[2608,128]{1,0:T(8,128)S(1)} collective-permute-done((f32[2608,128]{1,0:T(8,128)S(1)}, f32[2608,128]{1,0:T(8,128)S(1)}, u32[]{:S(2)}, u32[]{:S(2)}) %collective-permute-start) | collective-permute-done | bytes 1335328 | tf_op jit(solution)/shard_map/ppermute | solution.py:629
  6.2 0.0 copy-done.3
  6.2 8.1 %near.1 = (f32[8,800,128]{2,1,0:T(8,128)S(1)}, f32[8,536,128]{2,1,0:T(8,128)S(1)}, f32[8,272,128]{2,1,0:T(8,128)S(1)}, f32[8,256,128]{2,1,0:T(8,128)S(1)}, f32[8...) custom-call(f32[5,1064,128]{2,1,0:T(8,128)S(1)} %get-tuple-element.35.flat, ...), custom_call_target="tpu_custom_call" | custom-call | flops 1000000 | bytes 30000000 | tf_op jit(solution)/shard_map/near/pallas_call | solution.py:633
  14.4 0.0 collective-permute-done.1.swap_a
  14.4 2.9 %collective-permute-start.3 = (f32[520,128]{1,0:T(8,128)S(1)}, f32[520,128]{1,0:T(8,128)S(1)}, u32[]{:S(2)}, u32[]{:S(2)}) collective-permute-start(f32[520,128]{1,0:T(8,128)S(1)} %collective-permute-done.1.swap_a), channel_id=1, source_target_pairs={{0,16},{16,0},{1,17},{17,1},{2,18},{18,2},{3,19},{19,3},{4,20},{20... | collective-permute-start | bytes 798728 | tf_op jit(solution)/shard_map/ppermute | solution.py:659
  17.3 0.0 collective-permute-done.2.from_edge
  17.3 5.4 %far_a.1 = (f32[8,272,128]{2,1,0:T(8,128)S(1)}, f32[8,536,128]{2,1,0:T(8,128)S(1)}, f32[8,536,128]{2,1,0:T(8,128)S(1)}, f32[8,256,128]{2,1,0:T(8,128)S(1)}, f32[...) custom-call(f32[5,1064,128]{2,1,0:T(8,128)S(1)} %get-tuple-element.35., ...), custom_call_target="tpu_custom_call" | custom-call | flops 1000000 | bytes 18000000 | tf_op jit(solution)/shard_map/far_a/pallas_call | solution.py:633
  22.7 0.0 collective-permute-done.3.swap_b
  22.8 2.5 %far_b.1 = (f32[8,272,128]{2,1,0:T(8,128)S(1)}, f32[384,128]{1,0:T(8,128)S(1)}, f32[8,272,128]{2,1,0:T(8,128)S(1)}, f32[8,272,128]{2,1,0:T(8,128)S(1)}, f32[8,27...) custom-call(f32[5,1064,128]{2,1,0:T(8,128)S(1)} %get-tuple-element.35.flats, f32[1064,128]{1,0:T(8,128)S(1)} %get-tuple-element.37.coef, ...), custom_call_target="tpu_custom_call" | custom-call | flops 1000000 | bytes 9000000 | tf_op jit(solution)/shard_map/far_b/pallas_call | solution.py:633
  25.2 0.0 collective-permute-done.4.from_rest
  25.3 0.0 copy-start.4
  25.3 2.3 %far_c.1 = (f32[1,128]{1,0:T(1,128)S(1)}, f32[384,128]{1,0:T(8,128)}) custom-call(f32[8,272,128]{2,1,0:T(8,128)S(1)} %get-tuple-element.48.w0h, f32[8,272,128]{2,1,0:T(8,128)S(1)} %get-tuple-element.57.w0f, f32[8,536,128]{2,1,0:T(8,128)S(1)} %get-tuple-element.50.w1b, f32[8,272,128]{2,1,0:T(8,128)S(1)} %get-tuple-element.58.w1h, ...), custom_call_target="tpu_custom_call" | custom-call | flops 1000000 | bytes 6000000 | tf_op jit(solution)/shard_map/far_c/pallas_call | solution.py:633
  27.6 23.6 %all_to_all.5.moments = f32[16,1,128]{2,1,0:T(1,128)S(1)} all-to-all(f32[16,1,128]{2,1,0:T(1,128)S(1)} %broadcast_in_dim.9), channel_id=1, replica_groups=mesh['field'=2,'slab'=16] {'slab'}, dimensions={0} | all-to-all | bytes 16384 | tf_op jit(solution)/shard_map/all_to_all | solution.py:680
  51.2 0.0 copy-done.4
  51.2 2.8 %combine.1 = f32[4,64,512]{2,1,0:T(8,128)} custom-call(f32[16,1,128]{2,1,0:T(1,128)S(1)} %all_to_all.5.moments, f32[8]{0:T(128)S(1)} %copy-done.4, f32[8,800,128]{2,1,0:T(8,128)S(1)} %get-tuple-element.38.w0a, f32[8,272,128]{2,1,0:T(8,128)S(1)} %get-tuple-element.49.w0b, f32[8,536,128]{2,1,0:T(8,128)S(1)} %get-tuple-element.39.w1a, ...), custom_call_target="tpu_custom_call" | custom-call | tf_op jit(solution)/shard_map/combine/pallas_call | solution.py:682
  (1 shorter events, 0.0 us)
Async XLA Ops:
  0.0 1.4 %copy-start.1 = (f32[4,64,512]{2,1,0:T(8,128)S(1)}, f32[4,64,512]{2,1,0:T(8,128)}, u32[]{:S(2)}) copy-start(f32[4,64,512]{2,1,0:T(8,128)} %kappa.1) | copy-start | bytes 1572868
  0.0 1.5 %copy-start = (f32[4,64,512]{2,1,0:T(8,128)S(1)}, f32[4,64,512]{2,1,0:T(8,128)}, u32[]{:S(2)}) copy-start(f32[4,64,512]{2,1,0:T(8,128)} %cz.1) | copy-start | bytes 1572868
  0.0 1.7 %copy-start.2 = (f32[4,64,512]{2,1,0:T(8,128)S(1)}, f32[4,64,512]{2,1,0:T(8,128)}, u32[]{:S(2)}) copy-start(f32[4,64,512]{2,1,0:T(8,128)} %b.1) | copy-start | bytes 1572868
  1.7 4.6 %copy-start.3 = (f32[8]{0:T(128)S(1)}, f32[8]{0:T(128)}, u32[]{:S(2)}) copy-start(f32[8]{0:T(128)} %shifts.7) | copy-start | bytes 100
  3.0 3.2 %collective-permute-start = (f32[2608,128]{1,0:T(8,128)S(1)}, f32[2608,128]{1,0:T(8,128)S(1)}, u32[]{:S(2)}, u32[]{:S(2)}) collective-permute-start(f32[2608,128]{1,0:T(8,128)S(1)} %get-tuple-element.36), channel_id=1, source_target_pairs={{0,1},{1,0},{2,3},{3,2},{4,5},{5,4},{6,7},{7,6},{8,9},{9,8},{10,11... | collective-permute-start | bytes 4005896 | tf_op jit(solution)/shard_map/ppermute | solution.py:629
  3.5 10.8 %collective-permute-start.1 = (f32[520,128]{1,0:T(8,128)S(1)}, f32[520,128]{1,0:T(8,128)S(1)}, u32[]{:S(2)}, u32[]{:S(2)}) collective-permute-start(f32[520,128]{1,0:T(8,128)S(1)} %get-tuple-element.43), channel_id=1, source_target_pairs={{1,2},{2,1},{3,4},{4,3},{5,6},{6,5},{7,8},{8,7},{9,10},{10,9},{11,... | collective-permute-start | bytes 798728 | tf_op jit(solution)/shard_map/ppermute | solution.py:626
  4.2 13.1 %collective-permute-start.2 = (f32[1024,128]{1,0:T(8,128)S(1)}, f32[1024,128]{1,0:T(8,128)S(1)}, u32[]{:S(2)}, u32[]{:S(2)}) collective-permute-start(f32[1024,128]{1,0:T(8,128)S(1)} %get-tuple-element.47), channel_id=1, source_target_pairs={{1,2},{2,1},{3,4},{4,3},{5,6},{6,5},{7,8},{8,7},{9,10},{10,9},{11,... | collective-permute-start | bytes 1572872 | tf_op jit(solution)/shard_map/ppermute | solution.py:627
  4.9 20.3 %collective-permute-start.4 = (f32[544,128]{1,0:T(8,128)S(1)}, f32[544,128]{1,0:T(8,128)S(1)}, u32[]{:S(2)}, u32[]{:S(2)}) collective-permute-start(f32[544,128]{1,0:T(8,128)S(1)} %get-tuple-element.62), channel_id=1, source_target_pairs={{1,2},{2,1},{3,4},{4,3},{5,6},{6,5},{7,8},{8,7},{9,10},{10,9},{11,... | collective-permute-start | bytes 835592 | tf_op jit(solution)/shard_map/ppermute | solution.py:628
  14.4 8.3 %collective-permute-start.3 = (f32[520,128]{1,0:T(8,128)S(1)}, f32[520,128]{1,0:T(8,128)S(1)}, u32[]{:S(2)}, u32[]{:S(2)}) collective-permute-start(f32[520,128]{1,0:T(8,128)S(1)} %collective-permute-done.1.swap_a), channel_id=1, source_target_pairs={{0,16},{16,0},{1,17},{17,1},{2,18},{18,2},{3,19},{19,3},{4,20},{20... | collective-permute-start | bytes 798728 | tf_op jit(solution)/shard_map/ppermute | solution.py:659
  25.3 25.9 %copy-start.4 = (f32[8]{0:T(128)S(1)}, f32[8]{0:T(128)}, u32[]{:S(2)}) copy-start(f32[8]{0:T(128)} %weights.1) | copy-start | bytes 100

commit v4 on v3

--- a/solution.py
+++ b/solution.py
@@ -22,13 +22,15 @@
         full, half = self.plane, self.nc * self.half
         faces_yz = [("pad", PAD), ("fz1", full), ("fy1", full)]
         faces_x = [("gap", PAD), ("fx2", full), ("d2", full)]
-        edge = [("x1", full), ("d1", full), ("b1", full), ("b2", full)]
+        first = [("x1", full)]
+        edge = [("d1", full), ("b1", full), ("b2", full)]
         rest = [("fy2", half), ("d3", half), ("g3", half), ("fz2", self.nc * self.more)]
         self.at_yz, self.rows_yz = self.layout(faces_yz)
         self.at_x, self.rows_x = self.layout(faces_x)
+        self.at_first, self.rows_first = self.layout([("swapped", self.rows_yz)] + first)
         self.at_edge, self.rows_edge = self.layout(edge)
         self.at_rest, self.rows_rest = self.layout(rest)
-        self.at_all, self.rows_all = self.layout(faces_yz + faces_x + edge + rest)
+        self.at_all, self.rows_all = self.layout(faces_yz + faces_x + first + edge + rest)
 
     @staticmethod
     def layout(parts):
@@ -149,11 +151,15 @@
 
 
 def pack_body(
-    dm, conds, cz, kappa, b, to_swap, to_edge, to_rest, to_in, coef, temp,
+    dm, nk, conds, cz, kappa, b, shifts, weights, to_swap, to_edge, to_rest, to_in, coef, scalars, temp,
 ):
     par = lax.rem(lax.axis_index("slab"), 2)
     side_field = lax.rem(lax.axis_index("field"), 2)
     nc, nz, nl = dm.nc, dm.nz, dm.nl
+    for k in range(nk):
+        scalars[k * 8 : k * 8 + 8, :] = jnp.broadcast_to(shifts[:, k : k + 1], (8, LANES))
+    scalars[nk * 8 :, :] = jnp.zeros((8, LANES), jnp.float32)
+    scalars[nk * 8 : nk * 8 + 1, 0:nk] = weights[...]
     raw = [conds.at[0], conds.at[1], cz, kappa, b]
     prepare(dm, par, *raw, [coef.at[n] for n in range(5)] + [temp])
     bf, df, xf, yf, zf = [own_planes(dm, coef.at[n]) for n in range(5)]
@@ -171,9 +177,11 @@
 
         blocks(0, z_count, body, min(4, z_count // 8) if z_count % 32 == 0 else 1)
 
+    def first(out, at, one):
+        fill(out, at, nz, [("x1", lambda c, n: xf[one].get(c, n))])
+
     def edge(out, at, one, two):
         fill(out, at, nz, [
-            ("x1", lambda c, n: xf[one].get(c, n)),
             ("d1", lambda c, n: df[one].get(c, n)),
             ("b1", lambda c, n: bf[one].get(c, n)),
             ("b2", lambda c, n: bf[two].get(c, n)),
@@ -209,11 +217,13 @@
     def _():
         x(to_swap, dm.at_x, 0, 1)
 
+    first(to_swap, dm.at_first, 0)
     edge(to_edge, dm.at_edge, 0, 1)
     rest(to_rest, dm.at_rest, 1, 2)
     last = nl - 1
     yz(to_in, dm.at_all, last)
     x(to_in, dm.at_all, last, last - 1)
+    first(to_in, dm.at_all, last)
     edge(to_in, dm.at_all, last, last - 1)
     rest(to_in, dm.at_all, last - 1, last - 2)
 
@@ -244,7 +254,7 @@
         def body(z):
             diagonal, rhs = self.tiles(d, z), self.tiles(b, z)
             for k in range(self.nk):
-                s = self.shifts[k]
+                s = self.shifts[pl.ds(k * 8, 8), :]
                 inverse = [1.0 / (t + s) for t in diagonal]
                 value = [x * y for x, y in zip(rhs, inverse)]
                 for c in range(self.dm.nc):
@@ -346,9 +356,9 @@
     return planes
 
 
-def near_body(
-    dm, nk, flats, from_in, shifts, w0a, w1a, w2a, part1, part2, acc, coef, inv_out,
-    extra, w0h, w1h, w2h, inv,
+def near_a_body(
+    dm, nk, flats, from_in, shifts, w0a, w1a, w1h, part1, acc, coef, inv12, inv34,
+    extra, w0h, inv5,
 ):
     par = lax.rem(lax.axis_index("slab"), 2)
     nl, nc, nz = dm.nl, dm.nc, dm.nz
@@ -358,7 +368,7 @@
     st = Steps(dm, nk, par, acc, shifts)
     hp = halo_planes(dm, st, (from_in, dm.at_all))
     acc[...] = jnp.zeros(acc.shape, jnp.float32)
-    for ref in (w0a, w1a, w2a, w0h, w1h, w2h):
+    for ref in (w0a, w1a, w0h, w1h):
         clear_pads(dm, nk, ref)
     d_last, d_next = Plane(extra.at[0], 0, nz), Plane(extra.at[1], 0, nz)
 
@@ -376,11 +386,8 @@
 
     W0 = stack(dm, w0a, range(1, nl)) | stack(dm, w0h, (nl, nl + 1))
     far = Plane(w0h, PAD + 2 * dm.slot, dm.half, st.zs)
-    W1 = stack(dm, w1a, range(2, nl)) | stack(dm, w1h, (nl,))
-    W1[nl + 1] = Plane(w1h, PAD + dm.slot, nz)
-    W2 = stack(dm, w2a, range(3, nl)) | stack(dm, w2h, (nl,))
-    R = stack(dm, inv_out, (1, 2)) | stack(dm, inv, range(3, nl + 2))
-    I1, I2 = Plane(part1, 0, nz), Plane(part2, 0, nz)
+    W1 = stack(dm, w1a, range(2, nl)) | stack(dm, w1h, (nl, nl + 1))
+    R = stack(dm, inv12, (1, 2)) | stack(dm, inv34, range(3, nl + 1)) | stack(dm, inv5, (nl + 1,))
 
     for p in range(1, nl):
         st.start(df[p], bf[p], W0[p], R[p], own=True)
@@ -388,10 +395,11 @@
     st.start(hp["d2"], hp["b2"], W0[nl + 1], R[nl + 1])
     st.start(hp["d3"], hp["g3"], far, half=True)
 
-    yz = [(yf[p], zf[p]) for p in range(nl)]
-    st.apply(W0[1], [(xf[1], W0[2])], I1, yz=yz[1])
+    st.apply(W0[1], [(xf[1], W0[2])], Plane(part1, 0, nz), yz=(yf[1], zf[1]))
     for p in range(2, nl):
-        st.apply(W0[p], [(xf[p - 1], W0[p - 1]), (xf[p], W0[p + 1])], W1[p], R[p], yz[p], moment=1)
+        st.apply(
+            W0[p], [(xf[p - 1], W0[p - 1]), (xf[p], W0[p + 1])], W1[p], R[p], (yf[p], zf[p]), moment=1
+        )
     st.apply(
         W0[nl], [(xf[last], W0[last]), (hp["fx2"], W0[nl + 1])], W1[nl], R[nl], (hp["fy1"], hp["fz1"])
     )
@@ -399,21 +407,42 @@
         W0[nl + 1], [(hp["fx2"], W0[nl]), (None, far)], W1[nl + 1], R[nl + 1],
         (hp["fy2"], hp["fz2"]), half=True,
     )
-    st.apply(W1[2], [(xf[2], W1[3])], I2, yz=yz[2])
+
+
+def near_b_body(
+    dm, nk, flats, coef, w1a, w1h, acc_in, inv34, from_in, shifts, w2a, part2, acc, w2h,
+):
+    par = lax.rem(lax.axis_index("slab"), 2)
+    nl, nz = dm.nl, dm.nz
+    last = nl - 1
+    bf, df, raw_x, yf, zf = [own_planes(dm, flats.at[n]) for n in range(5)]
+    xf = own_planes(dm, coef)
+    st = Steps(dm, nk, par, acc, shifts)
+    hp = halo_planes(dm, st, (from_in, dm.at_all))
+    acc[...] = acc_in[...]
+    for ref in (w2a, w2h):
+        clear_pads(dm, nk, ref)
+    W1 = stack(dm, w1a, range(2, nl)) | stack(dm, w1h, (nl, nl + 1))
+    W2 = stack(dm, w2a, range(3, nl)) | stack(dm, w2h, (nl,))
+    R = stack(dm, inv34, range(3, nl + 1))
+
+    st.apply(W1[2], [(xf[2], W1[3])], Plane(part2, 0, nz), yz=(yf[2], zf[2]))
     for p in range(3, nl):
-        st.apply(W1[p], [(xf[p - 1], W1[p - 1]), (xf[p], W1[p + 1])], W2[p], R[p], yz[p], moment=3)
+        st.apply(
+            W1[p], [(xf[p - 1], W1[p - 1]), (xf[p], W1[p + 1])], W2[p], R[p], (yf[p], zf[p]), moment=3
+        )
     st.apply(
         W1[nl], [(xf[last], W1[last]), (hp["fx2"], W1[nl + 1])], W2[nl], R[nl],
         (hp["fy1"], hp["fz1"]), half=True,
     )
     for p in range(3, nl):
-        st.face_sum(W2[p], None if p == last else (xf[p], W2[p + 1]), yz[p])
+        st.face_sum(W2[p], None if p == last else (xf[p], W2[p + 1]), (yf[p], zf[p]))
     st.face_sum(W2[last], (xf[last], W2[nl]), half=True)
 
 
-def far_a_body(
-    dm, nk, flats, coef, w0a, w1a, w2a, part1, part2, acc_in, inv, from_edge, shifts,
-    w0b, w1b, w2b, part3, acc, edge, w0h, inv_out,
+def far_0_body(
+    dm, nk, flats, coef, w0a, w1a, w2a, part1, part2, acc_in, inv, from_first, shifts,
+    w0b, w1b, w2b, acc, edge, inv_out,
 ):
     index = lax.axis_index("slab")
     par = lax.rem(index, 2)
@@ -422,43 +451,68 @@
     bf, df, raw_x, yf, zf = [own_planes(dm, flats.at[n]) for n in range(5)]
     xf = own_planes(dm, coef)
     st = Steps(dm, nk, par, acc, shifts)
+    x1 = Plane(from_first, dm.at_first["x1"], nz)
+    acc[...] = acc_in[...]
+    for ref in (w0b, w1b, w2b):
+        clear_pads(dm, nk, ref)
+    d_here, x_edge = [Plane(edge.at[n], 0, nz) for n in range(2)]
+
+    def edges(z):
+        for c in range(nc):
+            here, there = raw_x[0].get(c, z), x1.get(c, z)
+            d_here.put(c, z, df[0].get(c, z) + 0.5 * there)
+            x_edge.put(c, z, has_off * (here + there))
+
+    blocks(0, nz, edges, 4)
+
+    W0 = stack(dm, w0a, range(1, nl)) | stack(dm, w0b, (0,))
+    W1 = stack(dm, w1a, range(2, nl)) | stack(dm, w1b, (1,))
+    W2 = stack(dm, w2a, range(3, nl)) | stack(dm, w2b, (2,))
+    R = stack(dm, inv_out, (0,)) | stack(dm, inv, (1, 2))
+    I1, I2 = Plane(part1, 0, nz), Plane(part2, 0, nz)
+
+    st.start(d_here, bf[0], W0[0], R[0], own=True)
+    st.apply(W0[1], [(xf[0], W0[0])], W1[1], R[1], base=I1, moment=1)
+    st.apply(W1[2], [(xf[1], W1[1])], W2[2], R[2], base=I2, moment=3)
+    st.face_sum(W2[2], (xf[2], W2[3]), (yf[2], zf[2]))
+
+
+def far_a_body(
+    dm, nk, flats, coef, w0a, w0b, w1a, w1b, w2b, acc_in, inv, inv0, edge, from_edge, shifts,
+    w0h, w1c, w2c, part3, acc, inv_out, d_ref,
+):
+    par = lax.rem(lax.axis_index("slab"), 2)
+    nl, nc, nz = dm.nl, dm.nc, dm.nz
+    bf, df, raw_x, yf, zf = [own_planes(dm, flats.at[n]) for n in range(5)]
+    xf = own_planes(dm, coef)
+    st = Steps(dm, nk, par, acc, shifts)
     hp = halo_planes(dm, st, (from_edge, dm.at_edge))
     acc[...] = acc_in[...]
-    for ref in (w0b, w1b, w2b, w0h):
+    for ref in (w0h, w1c, w2c):
         clear_pads(dm, nk, ref)
-    d_here, d_next, x_edge = [Plane(edge.at[n], 0, nz) for n in range(3)]
+    x_edge, d_next = Plane(edge.at[1], 0, nz), Plane(d_ref, 0, nz)
 
     def edges(z):
         for c in range(nc):
-            here, there = raw_x[0].get(c, z), hp["x1"].get(c, z)
-            d_here.put(c, z, df[0].get(c, z) + 0.5 * there)
-            d_next.put(c, z, hp["d1"].get(c, z) + 0.5 * here)
-            x_edge.put(c, z, has_off * (here + there))
+            d_next.put(c, z, hp["d1"].get(c, z) + 0.5 * raw_x[0].get(c, z))
 
     blocks(0, nz, edges, 4)
 
     W0 = stack(dm, w0a, range(1, nl)) | stack(dm, w0b, (0,)) | stack(dm, w0h, (-1,))
-    W1 = stack(dm, w1a, range(2, nl)) | stack(dm, w1b, (0, 1))
-    W2 = stack(dm, w2a, range(3, nl)) | stack(dm, w2b, (1, 2))
-    R = stack(dm, inv_out, (-1, 0)) | stack(dm, inv, (1, 2))
-    I1, I2, I3 = Plane(part1, 0, nz), Plane(part2, 0, nz), Plane(part3, 0, nz)
-    yz = [(yf[p], zf[p]) for p in range(nl)]
-
-    st.start(d_here, bf[0], W0[0], R[0], own=True)
+    W1 = stack(dm, w1a, range(2, nl)) | stack(dm, w1b, (1,)) | stack(dm, w1c, (0,))
+    W2 = stack(dm, w2b, (2,)) | stack(dm, w2c, (1,))
+    R = stack(dm, inv_out, (-1,)) | stack(dm, inv0, (0,)) | stack(dm, inv, (1, 2))
+
     st.start(d_next, hp["b1"], W0[-1], R[-1])
-
-    st.apply(W0[1], [(xf[0], W0[0])], W1[1], R[1], base=I1, moment=1)
-    st.apply(W0[0], [(x_edge, W0[-1]), (xf[0], W0[1])], W1[0], R[0], yz[0], moment=1)
-    st.apply(W1[2], [(xf[1], W1[1])], W2[2], R[2], base=I2, moment=3)
-    st.apply(W1[1], [(xf[0], W1[0]), (xf[1], W1[2])], W2[1], R[1], yz[1], moment=3)
-    st.apply(W1[0], [(xf[0], W1[1])], I3, yz=yz[0])
-    for p in range(1, min(3, nl - 1)):
-        st.face_sum(W2[p], (xf[p], W2[p + 1]), yz[p])
+    st.apply(W0[0], [(x_edge, W0[-1]), (xf[0], W0[1])], W1[0], R[0], (yf[0], zf[0]), moment=1)
+    st.apply(W1[1], [(xf[0], W1[0]), (xf[1], W1[2])], W2[1], R[1], (yf[1], zf[1]), moment=3)
+    st.apply(W1[0], [(xf[0], W1[1])], Plane(part3, 0, nz), yz=(yf[0], zf[0]))
+    st.face_sum(W2[1], (xf[1], W2[2]), (yf[1], zf[1]))
 
 
 def far_b_body(
-    dm, nk, flats, coef, w0b, w0h, w1b, w2b, part3, acc_in, edge, inv_in, from_edge, swap_a, swap_b, shifts,
-    w2c, acc, w1h, inv_out, w0f, shared,
+    dm, nk, flats, coef, w0b, w0h, w1c, w2c, part3, acc_in, edge, inv0, inv1, from_edge,
+    swap_a, swap_b, shifts, w2d, acc, w1h, inv_out, w0f, shared,
 ):
     par = lax.rem(lax.axis_index("slab"), 2)
     side_field = lax.rem(lax.axis_index("field"), 2)
@@ -480,13 +534,13 @@
     at_x = {name: row + dm.rows_yz for name, row in dm.at_x.items()}
     hp = halo_planes(dm, st, (from_edge, dm.at_edge), (shared, dm.at_yz), (shared, at_x))
     acc[...] = acc_in[...]
-    for ref in (w2c, w1h, w0f):
+    for ref in (w2d, w1h, w0f):
         clear_pads(dm, nk, ref)
-    x_edge = Plane(edge.at[2], 0, nz)
+    x_edge = Plane(edge.at[1], 0, nz)
     W0 = stack(dm, w0b, (0,)) | stack(dm, w0h, (-1,)) | stack(dm, w0f, (-2,))
-    W1 = stack(dm, w1b, (0, 1)) | stack(dm, w1h, (-1,))
-    W2 = stack(dm, w2b, (1, 2)) | stack(dm, w2c, (0,))
-    R = stack(dm, inv_in, (-1, 0)) | stack(dm, inv_out, (-2,))
+    W1 = stack(dm, w1c, (0,)) | stack(dm, w1h, (-1,))
+    W2 = stack(dm, w2c, (1,)) | stack(dm, w2d, (0,))
+    R = stack(dm, inv0, (0,)) | stack(dm, inv1, (-1,)) | stack(dm, inv_out, (-2,))
     st.start(hp["d2"], hp["b2"], W0[-2], R[-2])
     st.apply(
         W0[-1], [(hp["fx2"], W0[-2]), (x_edge, W0[0])], W1[-1], R[-1], (hp["fy1"], hp["fz1"])
@@ -496,7 +550,7 @@
 
 
 def far_c_body(
-    dm, nk, w0h, w0f, w1b, w1h, w2c, acc_in, edge, inv_in, inv2, from_rest, shared, shifts,
+    dm, nk, w0h, w0f, w1c, w1h, w2d, acc_in, edge, inv1, inv2, from_rest, shared, shifts,
     moments, acc, w0g, w1g, w2g,
 ):
     par = lax.rem(lax.axis_index("slab"), 2)
@@ -505,12 +559,12 @@
     at_x = {name: row + dm.rows_yz for name, row in dm.at_x.items()}
     hp = halo_planes(dm, st, (from_rest, dm.at_rest), (shared, dm.at_yz), (shared, at_x))
     acc[...] = acc_in[...]
-    x_edge = Plane(edge.at[2], 0, nz)
+    x_edge = Plane(edge.at[1], 0, nz)
     far, near, w2 = [Plane(ref, 0, dm.half, st.zs) for ref in (w0g, w1g, w2g)]
     W0 = stack(dm, w0h, (-1,)) | stack(dm, w0f, (-2,))
-    W1 = stack(dm, w1b, (0, 1)) | stack(dm, w1h, (-1,))
-    W2 = stack(dm, w2c, (0,))
-    R = stack(dm, inv_in, (-1, 0)) | stack(dm, inv2, (-2,))
+    W1 = stack(dm, w1c, (0,)) | stack(dm, w1h, (-1,))
+    W2 = stack(dm, w2d, (0,))
+    R = stack(dm, inv1, (-1,)) | stack(dm, inv2, (-2,))
     st.start(hp["d3"], hp["g3"], far, half=True)
     st.apply(
         W0[-2], [(None, far), (hp["fx2"], W0[-1])], near, R[-2], (hp["fy2"], hp["fz2"]), half=True
@@ -556,31 +610,35 @@
     return x
 
 
-def combine_body(dm, nk, moments, weights, w0a, w0b, w1a, w1b, w2a, w2b, w2c, out):
+def combine_body(dm, nk, moments, scalars, w0a, w0b, w1a, w1b, w1c, w2a, w2b, w2c, w2d, out, made, sems):
     par = lax.rem(lax.axis_index("slab"), 2)
     nl, nc, nz = dm.nl, dm.nc, dm.nz
     sums = jnp.sum(moments[...].reshape(-1, LANES), axis=0, keepdims=True)
     x = coefficients(jnp.broadcast_to(sums, (8, LANES)), nk)
-    scale = [
-        [jnp.broadcast_to(x[j][:, k : k + 1] * weights[k], (8, LANES)) for k in range(nk)]
-        for j in range(3)
-    ]
+    x = [t * scalars[nk * 8 : nk * 8 + 1, :] for t in x]
+    scale = [[jnp.broadcast_to(t[:, k : k + 1], (8, LANES)) for k in range(nk)] for t in x]
     W0 = stack(dm, w0a, range(1, nl)) | stack(dm, w0b, (0,))
-    W1 = stack(dm, w1a, range(2, nl)) | stack(dm, w1b, (0, 1))
-    W2 = stack(dm, w2a, range(3, nl)) | stack(dm, w2b, (1, 2)) | stack(dm, w2c, (0,))
+    W1 = stack(dm, w1a, range(2, nl)) | stack(dm, w1b, (1,)) | stack(dm, w1c, (0,))
+    W2 = stack(dm, w2a, range(3, nl)) | stack(dm, w2b, (2,)) | stack(dm, w2c, (1,)) | stack(dm, w2d, (0,))
+    copies = []
     for p in range(nl):
-        layer = jnp.where(par == 0, p, nl - 1 - p)
-
-        def body(z, p=p, layer=layer):
+
+        def body(z, p=p):
             for c in range(nc):
                 terms = [
                     scale[j][k] * w[p].get(c, z, k) for j, w in enumerate((W0, W1, W2)) for k in range(nk)
                 ]
                 while len(terms) > 1:
                     terms = [sum(terms[n : n + 2][1:], terms[n]) for n in range(0, len(terms), 2)]
-                out[layer, pl.ds(z, 8), c * LANES : (c + 1) * LANES] = terms[0]
+                made[p, pl.ds(z, 8), c * LANES : (c + 1) * LANES] = terms[0]
 
         blocks(0, nz, body)
+        layer = jnp.where(par == 0, p, nl - 1 - p)
+        copy = pltpu.make_async_copy(made.at[p], out.at[layer], sems.at[p])
+        copy.start()
+        copies.append(copy)
+    for copy in copies:
+        copy.wait()
 
 
 def on_device(right_side, cond_x, cond_y, cond_z, kappa_sq, shifts, weights):
@@ -590,7 +648,6 @@
     count = lax.axis_size("slab")
     f32 = jnp.float32
     vmem = pl.BlockSpec(memory_space=pltpu.VMEM)
-    smem = pl.BlockSpec(memory_space=pltpu.SMEM)
 
     def params(mib):
         return pltpu.CompilerParams(vmem_limit_bytes=mib * MIB)
@@ -607,25 +664,23 @@
     sums = shape(6 * nk * 8, LANES)
     assert dm.rows_yz == dm.rows_x
 
-    to_swap, to_edge, to_rest, to_in, flats = pl.pallas_call(
-        functools.partial(pack_body, dm),
+    to_swap, to_edge, to_rest, to_in, flats, scalars = pl.pallas_call(
+        functools.partial(pack_body, dm, nk),
         out_shape=(
-            shape(dm.rows_yz, LANES), shape(dm.rows_edge, LANES), shape(dm.rows_rest, LANES),
-            shape(dm.rows_all, LANES), shape(5, *own),
+            shape(dm.rows_first, LANES), shape(dm.rows_edge, LANES), shape(dm.rows_rest, LANES),
+            shape(dm.rows_all, LANES), shape(5, *own), shape(nk * 8 + 8, LANES),
         ),
-        in_specs=[vmem] * 4,
-        out_specs=(vmem,) * 5,
+        in_specs=[vmem] * 6,
+        out_specs=(vmem,) * 6,
         scratch_shapes=[
             pltpu.VMEM(own, f32),
         ],
         compiler_params=params(20),
         name="pack",
-    )(jnp.stack([cond_x, cond_y]), cond_z, kappa_sq, right_side)
+    )(jnp.stack([cond_x, cond_y]), cond_z, kappa_sq, right_side, shifts[None], weights[None])
 
     outward = [pair for i in range(1, count - 1, 2) for pair in ((i, i + 1), (i + 1, i))]
-    swap_a = lax.ppermute(to_swap, "slab", outward)
-    from_edge = lax.ppermute(to_edge, "slab", outward)
-    from_rest = lax.ppermute(to_rest, "slab", outward)
+    from_first = lax.ppermute(to_swap, "slab", outward)
     from_in = lax.ppermute(to_in, "slab", [(i, i ^ 1) for i in range(count)])
     fields = lax.axis_size("field")
 
@@ -633,7 +688,7 @@
         return pl.pallas_call(
             functools.partial(body, dm, nk),
             out_shape=results,
-            in_specs=[vmem] * len(operands) + [smem],
+            in_specs=[vmem] * (len(operands) + 1),
             out_specs=(vmem,) * len(results),
             scratch_shapes=scratch,
             compiler_params=params(mib),
@@ -641,7 +696,7 @@
                 flops=10**6, bytes_accessed=cost * 3 * 10**6, transcendentals=0
             ),
             name=name,
-        )(*operands, shifts)
+        )(*operands, scalars)
 
     def wide(slots):
         return shape(*stacked(slots))
@@ -649,31 +704,48 @@
     def held(slots):
         return pltpu.VMEM(stacked(slots), f32)
 
-    w0a, w1a, w2a, part1, part2, acc, coef, inv12 = call(
-        near_body, "near", 20,
-        (wide(nl - 1), wide(nl - 2), wide(nl - 3), plane_stack, plane_stack, sums, shape(*own), wide(2)),
-        [pltpu.VMEM((2, dm.plane, LANES), f32), held(3), held(2), held(1), held(nl - 1)],
-        (flats, from_in), 10,
-    )
-    swap_a, acc = lax.optimization_barrier((swap_a, acc))
+    w0a, w1a, w1h, part1, acc, coef, inv12, inv34 = call(
+        near_a_body, "near_a", 20,
+        (wide(nl - 1), wide(nl - 2), wide(2), plane_stack, sums, shape(*own), wide(2), wide(nl - 2)),
+        [pltpu.VMEM((2, dm.plane, LANES), f32), held(3), held(1)],
+        (flats, from_in), 6,
+    )
+    to_edge, acc = lax.optimization_barrier((to_edge, acc))
+    from_edge = lax.ppermute(to_edge, "slab", outward)
+    w2a, part2, acc = call(
+        near_b_body, "near_b", 20,
+        (wide(nl - 3), plane_stack, sums),
+        [held(1)],
+        (flats, coef, w1a, w1h, acc, inv34, from_in), 3,
+    )
+    from_first, acc = lax.optimization_barrier((from_first, acc))
+    swap_a = from_first[: dm.rows_yz]
     swap_b = lax.ppermute(swap_a, "field", [(i, i ^ 1) for i in range(fields)])
-    w0b, w1b, w2b, part3, acc, edge, w0h, inv = call(
+    w0b, w1b, w2b, acc, edge, inv0 = call(
+        far_0_body, "far_0", 20,
+        (wide(1), wide(1), wide(1), sums, shape(2, dm.plane, LANES), wide(1)),
+        [],
+        (flats, coef, w0a, w1a, w2a, part1, part2, acc, inv12, from_first), 2,
+    )
+    to_rest, acc = lax.optimization_barrier((to_rest, acc))
+    from_rest = lax.ppermute(to_rest, "slab", outward)
+    w0h, w1c, w2c, part3, acc, inv1 = call(
         far_a_body, "far_a", 20,
-        (wide(1), wide(2), wide(2), plane_stack, sums, shape(3, dm.plane, LANES), wide(1), wide(2)),
-        [],
-        (flats, coef, w0a, w1a, w2a, part1, part2, acc, inv12, from_edge), 6,
-    )
-    w2c, acc, w1h, inv2, w0f, shared = call(
+        (wide(1), wide(1), wide(1), plane_stack, sums, wide(1)),
+        [pltpu.VMEM((dm.plane, LANES), f32)],
+        (flats, coef, w0a, w0b, w1a, w1b, w2b, acc, inv12, inv0, edge, from_edge), 4,
+    )
+    w2d, acc, w1h, inv2, w0f, shared = call(
         far_b_body, "far_b", 20,
         (wide(1), sums, wide(1), wide(1), wide(1), shape(dm.rows_yz + dm.rows_x, LANES)),
         [],
-        (flats, coef, w0b, w0h, w1b, w2b, part3, acc, edge, inv, from_edge, swap_a, swap_b), 3,
+        (flats, coef, w0b, w0h, w1c, w2c, part3, acc, edge, inv0, inv1, from_edge, swap_a, swap_b), 3,
     )
     moments, _ = call(
         far_c_body, "far_c", 20,
         (shape(1, LANES), sums),
         [half_stack] * 3,
-        (w0h, w0f, w1b, w1h, w2c, acc, edge, inv, inv2, from_rest, shared), 2,
+        (w0h, w0f, w1c, w1h, w2d, acc, edge, inv1, inv2, from_rest, shared), 2,
     )
 
     everywhere = jnp.broadcast_to(moments[None], (count, 1, LANES))
@@ -682,11 +754,12 @@
     return pl.pallas_call(
         functools.partial(combine_body, dm, nk),
         out_shape=jax.ShapeDtypeStruct(right_side.shape, f32),
-        in_specs=[vmem, smem] + [vmem] * 7,
-        out_specs=vmem,
+        in_specs=[vmem] * 11,
+        out_specs=pl.BlockSpec(memory_space=pl.ANY),
+        scratch_shapes=[pltpu.VMEM(right_side.shape, f32), pltpu.SemaphoreType.DMA((nl,))],
         compiler_params=params(20),
         name="combine",
-    )(gathered, weights, w0a, w0b, w1a, w1b, w2a, w2b, w2c)
+    )(gathered, scalars, w0a, w0b, w1a, w1b, w1c, w2a, w2b, w2c, w2d)
 
 
 def solution(mesh):

time: 54.2 us -> 50.5 us (0.932)
  blocking collectives: 23.6 us -> 20.5 us
  Pallas kernels: 22.4 us -> 19.4 us
  waiting for transfers between devices: 0.65 us -> 3.01 us
    all_to_all x1, blocking collectives: 23.6 us -> 20.5 us  [on_device(): gathered = lax.all_to_all(everywhere, 'slab', 0, 0)]
    pallas_call x4 -> x6, Pallas kernels: 18.3 us -> 15.9 us  [call(): pl.pallas_call(functools.partial(body, dm, nk), out_shape=results, in_spe...]
    ppermute x1, waiting for transfers between devices: 0.63 us -> 2.01 us  [on_device(): from_in = lax.ppermute(to_in, 'slab', [(i, i ^ 1) for i in range(count)])]
    ppermute x1, waiting for transfers between devices: 0.01 us -> 0.99 us  [on_device(): swap_b = lax.ppermute(swap_a, 'field', [(i, i ^ 1) for i in range(fields)])]
    pallas_call x1, Pallas kernels: 2.76 us -> 2.09 us  [on_device(): pl.pallas_call(functools.partial(combine_body, dm, nk), out_shape=jax.Sha...]
  transfers between devices with their start and end apart: 5 -> 5, of which waited for: 1 -> 2; matrix products, arithmetic and copies ran while one was open for 0% -> 0% of each run, Pallas kernels for 30% -> 28%
where the time goes in v4:
time: 50.5 us; the launch traced here: 50.3 us
  blocking collectives  20.5 us (41%)
  Pallas kernels  19.4 us (38%)
  starting transfers between devices  5.49 us (11%)
  waiting for transfers between devices  3.01 us (6%)
  other arithmetic  1.39 us (3%)
    all_to_all x1, blocking collectives, on_device(): gathered = lax.all_to_all(everywhere, 'slab', 0, 0)  20.5 us
    pallas_call x6, Pallas kernels, call(): pl.pallas_call(functools.partial(body, dm, nk), out_shape=results, in_spe...  15.9 us
    ppermute x1, starting transfers between devices, on_device(): swap_b = lax.ppermute(swap_a, 'field', [(i, i ^ 1) for i in range(fields)])  2.93 us
    pallas_call x1, Pallas kernels, on_device(): pl.pallas_call(functools.partial(combine_body, dm, nk), out_shape=jax.Sha...  2.09 us
    ppermute x1, waiting for transfers between devices, on_device(): from_in = lax.ppermute(to_in, 'slab', [(i, i ^ 1) for i in range(count)])  2.01 us
    pallas_call x1, Pallas kernels, on_device(): pl.pallas_call(functools.partial(pack_body, dm, nk), out_shape=(shape(dm....  1.4 us
    another operation x1, other arithmetic, on_device(): jnp.stack([cond_x, cond_y])  1.39 us
  transfers between devices with their start and end apart: 5, of which 2 were waited for; matrix products, arithmetic and copies ran while one was open for 0% of the time, Pallas kernels for 28%

profile of v4, /device:TPU:0, one launch (start us, length us, event | category | flops | bytes accessed | tf_op | source)
XLA Modules:
  0.0 50.3 jit_solution(2083422153088121649)
XLA Ops:
  0.0 0.0 copy-start.4
  0.0 0.0 copy-start.3
  0.0 0.0 copy-start.1
  0.0 0.0 copy-start
  0.0 0.0 copy-start.2
  0.0 1.4 %pad_maximum_fusion.conds = f32[2,4,64,512]{3,2,1,0:T(8,128)S(1)} fusion(f32[1,4,64,512]{3,2,1,0:T(8,128)} %bitcast.8, f32[1,4,64,512]{3,2,1,0:T(8,128)} %bitcast.9), kind=kLoop, calls=%fused_computation | loop fusion | flops 262144 | bytes 2097152 | tf_op jit(solution)/shard_map/stack | solution.py:680
  1.4 0.0 copy-done.4
  1.4 0.0 copy-done.3
  1.4 0.0 copy-done.1
  1.4 0.1 copy-done
  1.5 0.2 copy-done.2
  1.7 1.4 %pack.1 = (f32[776,128]{1,0:T(8,128)S(1)}, f32[768,128]{1,0:T(8,128)S(1)}, f32[544,128]{1,0:T(8,128)S(1)}, f32[2608,128]{1,0:T(8,128)S(1)}, f32[5,1064,128]{2,1,0:T(8,128)S(1)}, /*index=5*/f32[72,128]{1,0:T(8,128)S(1)}) custom-call(f32[2,4,64,512]{3,2,1,0:T(8,128)S(1)} %pad_maximum_fusion.conds, f32[4,64,512]{2,1,0:T(8,128)S(1)} %copy-done, ...), custom_call_target="tpu_custom_call" | custom-call | tf_op jit(solution)/shard_map/pack/pallas_call | solution.py:667
  3.1 0.5 %collective-permute-start = (f32[2608,128]{1,0:T(8,128)S(1)}, f32[2608,128]{1,0:T(8,128)S(1)}, u32[]{:S(2)}, u32[]{:S(2)}) collective-permute-start(f32[2608,128]{1,0:T(8,128)S(1)} %get-tuple-element.48), channel_id=1, source_target_pairs={{0,1},{1,0},{2,3},{3,2},{4,5},{5,4},{6,7},{7,6},{8,9},{9,8},{10,11... | collective-permute-start | bytes 4005896 | tf_op jit(solution)/shard_map/ppermute | solution.py:684
  3.6 0.7 %collective-permute-start.1 = (f32[776,128]{1,0:T(8,128)S(1)}, f32[776,128]{1,0:T(8,128)S(1)}, u32[]{:S(2)}, u32[]{:S(2)}) collective-permute-start(f32[776,128]{1,0:T(8,128)S(1)} %get-tuple-element.61), channel_id=1, source_target_pairs={{1,2},{2,1},{3,4},{4,3},{5,6},{6,5},{7,8},{8,7},{9,10},{10,9},{11,... | collective-permute-start | bytes 1191944 | tf_op jit(solution)/shard_map/ppermute | solution.py:683
  4.3 2.0 %collective-permute-done.from_in = f32[2608,128]{1,0:T(8,128)S(1)} collective-permute-done((f32[2608,128]{1,0:T(8,128)S(1)}, f32[2608,128]{1,0:T(8,128)S(1)}, u32[]{:S(2)}, u32[]{:S(2)}) %collective-permute-start) | collective-permute-done | bytes 1335328 | tf_op jit(solution)/shard_map/ppermute | solution.py:684
  6.3 4.9 %near_a.1 = (f32[8,800,128]{2,1,0:T(8,128)S(1)}, f32[8,536,128]{2,1,0:T(8,128)S(1)}, f32[8,536,128]{2,1,0:T(8,128)S(1)}, f32[8,256,128]{2,1,0:T(8,128)S(1)}, f32...) custom-call(f32[5,1064,128]{2,1,0:T(8,128)S(1)} %get-tuple-element.47.fl, ...), custom_call_target="tpu_custom_call" | custom-call | flops 1000000 | bytes 18000000 | tf_op jit(solution)/shard_map/near_a/pallas_call | solution.py:688
  11.3 0.7 %collective-permute-start.2 = (f32[768,128]{1,0:T(8,128)S(1)}, f32[768,128]{1,0:T(8,128)S(1)}, u32[]{:S(2)}, u32[]{:S(2)}) collective-permute-start(f32[768,128]{1,0:T(8,128)S(1)} %get-tuple-element.74), channel_id=1, source_target_pairs={{1,2},{2,1},{3,4},{4,3},{5,6},{6,5},{7,8},{8,7},{9,10},{10,9},{11,... | collective-permute-start | bytes 1179656 | tf_op jit(solution)/shard_map/ppermute | solution.py:714
  12.0 2.6 %near_b.1 = (f32[8,272,128]{2,1,0:T(8,128)S(1)}, f32[8,256,128]{2,1,0:T(8,128)S(1)}, f32[384,128]{1,0:T(8,128)S(1)}) custom-call(f32[5,1064,128]{2,1,0:T(8,128)S(1)} %get-tuple-element.47.flats, f32[1064,128]{1,0:T(8,128)S(1)} %get-tuple-element.50.coef, f32[8,536,128]{2,1,0:T(8,128)S(1)} %get-tuple-element.52.w1a, ...), custom_call_target="tpu_custom_call" | custom-call | flops 1000000 | bytes 9000000 | tf_op jit(solution)/shard_map/near_b/pallas_call | solution.py:688
  14.5 0.0 collective-permute-done.1.from_first
  14.5 1.3 %far_0.1 = (f32[8,272,128]{2,1,0:T(8,128)S(1)}, f32[8,272,128]{2,1,0:T(8,128)S(1)}, f32[8,272,128]{2,1,0:T(8,128)S(1)}, f32[384,128]{1,0:T(8,128)S(1)}, f32[2,25...) custom-call(f32[5,1064,128]{2,1,0:T(8,128)S(1)} %get-tuple-element.47.flats, f32[1064,128]{1,0:T(8,128)S(1)} %get-tuple-element.50.coef, ...), custom_call_target="tpu_custom_call" | custom-call | flops 1000000 | bytes 6000000 | tf_op jit(solution)/shard_map/far_0/pallas_call | solution.py:688
  15.9 0.7 %collective-permute-start.4 = (f32[544,128]{1,0:T(8,128)S(1)}, f32[544,128]{1,0:T(8,128)S(1)}, u32[]{:S(2)}, u32[]{:S(2)}) collective-permute-start(f32[544,128]{1,0:T(8,128)S(1)} %get-tuple-element.86), channel_id=1, source_target_pairs={{1,2},{2,1},{3,4},{4,3},{5,6},{6,5},{7,8},{8,7},{9,10},{10,9},{11,... | collective-permute-start | bytes 835592 | tf_op jit(solution)/shard_map/ppermute | solution.py:731
  16.6 2.9 %collective-permute-start.3 = (f32[520,128]{1,0:T(8,128)S(1)}, f32[520,128]{1,0:T(8,128)S(1)}, u32[]{:S(2)}, u32[]{:S(2)}) collective-permute-start(f32[520,128]{1,0:T(8,128)S(1)} %slice.3.swap_a), channel_id=1, source_target_pairs={{0,16},{16,0},{1,17},{17,1},{2,18},{18,2},{3,19},{19,3},{4,20},{20... | collective-permute-start | bytes 798728 | tf_op jit(solution)/shard_map/ppermute | solution.py:723
  19.5 0.0 collective-permute-done.2.from_edge
  19.5 3.4 %far_a.1 = (f32[8,272,128]{2,1,0:T(8,128)S(1)}, f32[8,272,128]{2,1,0:T(8,128)S(1)}, f32[8,272,128]{2,1,0:T(8,128)S(1)}, f32[8,256,128]{2,1,0:T(8,128)S(1)}, f32[...) custom-call(f32[5,1064,128]{2,1,0:T(8,128)S(1)} %get-tuple-element.47.flats, f32[1064,128]{1,0:T(8,128)S(1)} %get-tuple-element.50.coef, ...), custom_call_target="tpu_custom_call" | custom-call | flops 1000000 | bytes 12000000 | tf_op jit(solution)/shard_map/far_a/pallas_call | solution.py:688
  22.9 1.0 %collective-permute-done.3.swap_b = f32[520,128]{1,0:T(8,128)S(1)} collective-permute-done((f32[520,128]{1,0:T(8,128)S(1)}, f32[520,128]{1,0:T(8,128)S(1)}, u32[]{:S(2)}, u32[]{:S(2)}) %collective-permute-start.3) | collective-permute-done | bytes 266272 | tf_op jit(solution)/shard_map/ppermute | solution.py:723
  23.9 2.0 %far_b.1 = (f32[8,272,128]{2,1,0:T(8,128)S(1)}, f32[384,128]{1,0:T(8,128)S(1)}, f32[8,272,128]{2,1,0:T(8,128)S(1)}, f32[8,272,128]{2,1,0:T(8,128)S(1)}, f32[8,27...) custom-call(f32[5,1064,128]{2,1,0:T(8,128)S(1)} %get-tuple-element.47.flats, f32[1064,128]{1,0:T(8,128)S(1)} %get-tuple-element.50.coef, ...), custom_call_target="tpu_custom_call" | custom-call | flops 1000000 | bytes 9000000 | tf_op jit(solution)/shard_map/far_b/pallas_call | solution.py:688
  25.9 0.0 collective-permute-done.4.from_rest
  25.9 1.7 %far_c.1 = (f32[1,128]{1,0:T(1,128)S(1)}, f32[384,128]{1,0:T(8,128)}) custom-call(f32[8,272,128]{2,1,0:T(8,128)S(1)} %get-tuple-element.75.w0h, f32[8,272,128]{2,1,0:T(8,128)S(1)} %get-tuple-element.81.w0f, f32[8,272,128]{2,1,0:T(8,128)S(1)} %get-tuple-element.76.w1c, f32[8,272,128]{2,1,0:T(8,128)S(1)} %get-tuple-element.82.w1h, ...), custom_call_target="tpu_custom_call" | custom-call | flops 1000000 | bytes 6000000 | tf_op jit(solution)/shard_map/far_c/pallas_call | solution.py:688
  27.6 20.5 %all_to_all.5.moments = f32[16,1,128]{2,1,0:T(1,128)S(1)} all-to-all(f32[16,1,128]{2,1,0:T(1,128)S(1)} %broadcast_in_dim.17), channel_id=1, replica_groups=mesh['field'=2,'slab'=16] {'slab'}, dimensions={0} | all-to-all | bytes 16384 | tf_op jit(solution)/shard_map/all_to_all | solution.py:752
  48.2 2.1 %combine.1 = f32[4,64,512]{2,1,0:T(8,128)} custom-call(f32[16,1,128]{2,1,0:T(1,128)S(1)} %all_to_all.5.moments, f32[72,128]{1,0:T(8,128)S(1)} %get-tuple-element.49.shifts.scalars, f32[8,800,128]{2,1,0:T(8,128)S(1)} %get-tuple-element.51.w0a, f32[8,272,128]{2,1,0:T(8,128)S(1)} %get-tuple-element.66.w0b, f32[8,536,128]{2,1,0:T(8,128)S(1)} %get-tuple-element.52.w1a, ...), custom_call_target="tpu_custom_call" | custom-call | tf_op jit(solution)/shard_map/combine/pallas_call | solution.py:754
  (2 shorter events, 0.0 us)
Async XLA Ops:
  0.0 1.4 %copy-start.4 = (f32[8]{0:T(128)S(1)}, f32[8]{0:T(128)}, u32[]{:S(2)}) copy-start(f32[8]{0:T(128)} %param.13) | copy-start | bytes 100
  0.0 1.4 %copy-start.3 = (f32[8]{0:T(128)S(1)}, f32[8]{0:T(128)}, u32[]{:S(2)}) copy-start(f32[8]{0:T(128)} %param.12) | copy-start | bytes 100
  0.0 1.4 %copy-start.1 = (f32[4,64,512]{2,1,0:T(8,128)S(1)}, f32[4,64,512]{2,1,0:T(8,128)}, u32[]{:S(2)}) copy-start(f32[4,64,512]{2,1,0:T(8,128)} %kappa.1) | copy-start | bytes 1572868
  0.0 1.5 %copy-start = (f32[4,64,512]{2,1,0:T(8,128)S(1)}, f32[4,64,512]{2,1,0:T(8,128)}, u32[]{:S(2)}) copy-start(f32[4,64,512]{2,1,0:T(8,128)} %cz.1) | copy-start | bytes 1572868
  0.0 1.7 %copy-start.2 = (f32[4,64,512]{2,1,0:T(8,128)S(1)}, f32[4,64,512]{2,1,0:T(8,128)}, u32[]{:S(2)}) copy-start(f32[4,64,512]{2,1,0:T(8,128)} %b.1) | copy-start | bytes 1572868
  3.1 3.2 %collective-permute-start = (f32[2608,128]{1,0:T(8,128)S(1)}, f32[2608,128]{1,0:T(8,128)S(1)}, u32[]{:S(2)}, u32[]{:S(2)}) collective-permute-start(f32[2608,128]{1,0:T(8,128)S(1)} %get-tuple-element.48), channel_id=1, source_target_pairs={{0,1},{1,0},{2,3},{3,2},{4,5},{5,4},{6,7},{7,6},{8,9},{9,8},{10,11... | collective-permute-start | bytes 4005896 | tf_op jit(solution)/shard_map/ppermute | solution.py:684
  3.6 10.9 %collective-permute-start.1 = (f32[776,128]{1,0:T(8,128)S(1)}, f32[776,128]{1,0:T(8,128)S(1)}, u32[]{:S(2)}, u32[]{:S(2)}) collective-permute-start(f32[776,128]{1,0:T(8,128)S(1)} %get-tuple-element.61), channel_id=1, source_target_pairs={{1,2},{2,1},{3,4},{4,3},{5,6},{6,5},{7,8},{8,7},{9,10},{10,9},{11,... | collective-permute-start | bytes 1191944 | tf_op jit(solution)/shard_map/ppermute | solution.py:683
  11.3 8.3 %collective-permute-start.2 = (f32[768,128]{1,0:T(8,128)S(1)}, f32[768,128]{1,0:T(8,128)S(1)}, u32[]{:S(2)}, u32[]{:S(2)}) collective-permute-start(f32[768,128]{1,0:T(8,128)S(1)} %get-tuple-element.74), channel_id=1, source_target_pairs={{1,2},{2,1},{3,4},{4,3},{5,6},{6,5},{7,8},{8,7},{9,10},{10,9},{11,... | collective-permute-start | bytes 1179656 | tf_op jit(solution)/shard_map/ppermute | solution.py:714
  15.9 10.0 %collective-permute-start.4 = (f32[544,128]{1,0:T(8,128)S(1)}, f32[544,128]{1,0:T(8,128)S(1)}, u32[]{:S(2)}, u32[]{:S(2)}) collective-permute-start(f32[544,128]{1,0:T(8,128)S(1)} %get-tuple-element.86), channel_id=1, source_target_pairs={{1,2},{2,1},{3,4},{4,3},{5,6},{6,5},{7,8},{8,7},{9,10},{10,9},{11,... | collective-permute-start | bytes 835592 | tf_op jit(solution)/shard_map/ppermute | solution.py:731
  16.6 7.3 %collective-permute-start.3 = (f32[520,128]{1,0:T(8,128)S(1)}, f32[520,128]{1,0:T(8,128)S(1)}, u32[]{:S(2)}, u32[]{:S(2)}) collective-permute-start(f32[520,128]{1,0:T(8,128)S(1)} %slice.3.swap_a), channel_id=1, source_target_pairs={{0,16},{16,0},{1,17},{17,1},{2,18},{18,2},{3,19},{19,3},{4,20},{20... | collective-permute-start | bytes 798728 | tf_op jit(solution)/shard_map/ppermute | solution.py:723

commit v5 on v4

--- a/solution.py
+++ b/solution.py
@@ -20,17 +20,19 @@
         self.half = self.nz // 2
         self.more = self.half + 8
         full, half = self.plane, self.nc * self.half
-        faces_yz = [("pad", PAD), ("fz1", full), ("fy1", full)]
-        faces_x = [("gap", PAD), ("fx2", full), ("d2", full)]
-        first = [("x1", full)]
-        edge = [("d1", full), ("b1", full), ("b2", full)]
-        rest = [("fy2", half), ("d3", half), ("g3", half), ("fz2", self.nc * self.more)]
-        self.at_yz, self.rows_yz = self.layout(faces_yz)
-        self.at_x, self.rows_x = self.layout(faces_x)
-        self.at_first, self.rows_first = self.layout([("swapped", self.rows_yz)] + first)
+        more = self.nc * self.more
+        yz = [("pad", PAD), ("fz1", full), ("fy1", full)]
+        x = [("fx2h", more), ("d2", full), ("d3", half)]
+        edge = [("d1", full), ("b1", full), ("g2", full)]
+        rest = [("fy2", half), ("g3", half), ("fz2", more)]
+        self.at_yz, self.rows_yz = self.layout(yz)
+        self.at_x, self.rows_x = self.layout(x)
+        self.rows_swap = max(self.rows_yz, self.rows_x)
+        self.at_first, self.rows_first = self.layout([("swapped", self.rows_swap), ("x1", full)])
         self.at_edge, self.rows_edge = self.layout(edge)
         self.at_rest, self.rows_rest = self.layout(rest)
-        self.at_all, self.rows_all = self.layout(faces_yz + faces_x + first + edge + rest)
+        near = [("fx2", full), ("d2", full), ("x1", full), ("d1", full), ("b1", full), ("b2", full)]
+        self.at_all, self.rows_all = self.layout(yz + near + [("d3", half)] + rest)
 
     @staticmethod
     def layout(parts):
@@ -177,24 +179,6 @@
 
         blocks(0, z_count, body, min(4, z_count // 8) if z_count % 32 == 0 else 1)
 
-    def first(out, at, one):
-        fill(out, at, nz, [("x1", lambda c, n: xf[one].get(c, n))])
-
-    def edge(out, at, one, two):
-        fill(out, at, nz, [
-            ("d1", lambda c, n: df[one].get(c, n)),
-            ("b1", lambda c, n: bf[one].get(c, n)),
-            ("b2", lambda c, n: bf[two].get(c, n)),
-        ])
-
-    def rest(out, at, two, three):
-        fill(out, at, dm.half, [
-            ("fy2", lambda c, n: yf[two].get(c, zs + n)),
-            ("d3", lambda c, n: df[three].get(c, zs + n)),
-            ("g3", lambda c, n: x_face(c, zs + n, two, three) * bf[three].get(c, zs + n)),
-        ])
-        fill(out, at, dm.more, [("fz2", lambda c, n: zf[two].get(c, zm + n))])
-
     def yz(out, at, one):
         out[at["pad"] : at["pad"] + PAD, :] = jnp.zeros((PAD, LANES), jnp.float32)
         fill(out, at, nz, [
@@ -202,30 +186,47 @@
             ("fy1", lambda c, n: yf[one].get(c, n)),
         ])
 
-    def x(out, at, one, two):
-        out[at["gap"] : at["gap"] + PAD, :] = jnp.zeros((PAD, LANES), jnp.float32)
-        fill(out, at, nz, [
-            ("fx2", lambda c, n: x_face(c, n, one, two)),
-            ("d2", lambda c, n: df[two].get(c, n)),
+    def rest(out, at, two, three):
+        fill(out, at, dm.half, [
+            ("fy2", lambda c, n: yf[two].get(c, zs + n)),
+            ("g3", lambda c, n: x_face(c, zs + n, two, three) * bf[three].get(c, zs + n)),
         ])
+        fill(out, at, dm.more, [("fz2", lambda c, n: zf[two].get(c, zm + n))])
+
+    def third(out, at, three):
+        fill(out, at, dm.half, [("d3", lambda c, n: df[three].get(c, zs + n))])
 
     @pl.when(side_field == 0)
     def _():
         yz(to_swap, dm.at_yz, 0)
+        if dm.rows_swap > dm.rows_yz:
+            to_swap[dm.rows_yz : dm.rows_swap, :] = jnp.zeros((dm.rows_swap - dm.rows_yz, LANES), jnp.float32)
 
     @pl.when(side_field == 1)
     def _():
-        x(to_swap, dm.at_x, 0, 1)
-
-    first(to_swap, dm.at_first, 0)
-    edge(to_edge, dm.at_edge, 0, 1)
+        fill(to_swap, dm.at_x, dm.more, [("fx2h", lambda c, n: x_face(c, zm + n, 0, 1))])
+        fill(to_swap, dm.at_x, nz, [("d2", lambda c, n: df[1].get(c, n))])
+        third(to_swap, dm.at_x, 2)
+
+    fill(to_swap, dm.at_first, nz, [("x1", lambda c, n: xf[0].get(c, n))])
+    fill(to_edge, dm.at_edge, nz, [
+        ("d1", lambda c, n: df[0].get(c, n)),
+        ("b1", lambda c, n: bf[0].get(c, n)),
+        ("g2", lambda c, n: x_face(c, n, 0, 1) * bf[1].get(c, n)),
+    ])
     rest(to_rest, dm.at_rest, 1, 2)
-    last = nl - 1
-    yz(to_in, dm.at_all, last)
-    x(to_in, dm.at_all, last, last - 1)
-    first(to_in, dm.at_all, last)
-    edge(to_in, dm.at_all, last, last - 1)
-    rest(to_in, dm.at_all, last - 1, last - 2)
+    one, two, three = nl - 1, nl - 2, nl - 3
+    yz(to_in, dm.at_all, one)
+    fill(to_in, dm.at_all, nz, [
+        ("fx2", lambda c, n: x_face(c, n, one, two)),
+        ("d2", lambda c, n: df[two].get(c, n)),
+        ("x1", lambda c, n: xf[one].get(c, n)),
+        ("d1", lambda c, n: df[one].get(c, n)),
+        ("b1", lambda c, n: bf[one].get(c, n)),
+        ("b2", lambda c, n: bf[two].get(c, n)),
+    ])
+    third(to_in, dm.at_all, three)
+    rest(to_in, dm.at_all, two, three)
 
 
 class Steps:
@@ -349,7 +350,7 @@
         for name, row in at.items():
             if name in ("fy2", "d3", "g3"):
                 planes[name] = Plane(ref, row, dm.half, st.zs)
-            elif name == "fz2":
+            elif name in ("fz2", "fx2h"):
                 planes[name] = Plane(ref, row, dm.more, st.zm)
             else:
                 planes[name] = Plane(ref, row, dm.nz)
@@ -442,7 +443,7 @@
 
 def far_0_body(
     dm, nk, flats, coef, w0a, w1a, w2a, part1, part2, acc_in, inv, from_first, shifts,
-    w0b, w1b, w2b, acc, edge, inv_out,
+    w0b, w1b, w2b, acc, edge, inv_out, part0, part3,
 ):
     index = lax.axis_index("slab")
     par = lax.rem(index, 2)
@@ -474,12 +475,14 @@
     st.start(d_here, bf[0], W0[0], R[0], own=True)
     st.apply(W0[1], [(xf[0], W0[0])], W1[1], R[1], base=I1, moment=1)
     st.apply(W1[2], [(xf[1], W1[1])], W2[2], R[2], base=I2, moment=3)
+    st.apply(W0[0], [(xf[0], W0[1])], Plane(part0, 0, nz), yz=(yf[0], zf[0]))
+    st.apply(W1[1], [(xf[1], W1[2])], Plane(part3, 0, nz), yz=(yf[1], zf[1]))
     st.face_sum(W2[2], (xf[2], W2[3]), (yf[2], zf[2]))
 
 
 def far_a_body(
-    dm, nk, flats, coef, w0a, w0b, w1a, w1b, w2b, acc_in, inv, inv0, edge, from_edge, shifts,
-    w0h, w1c, w2c, part3, acc, inv_out, d_ref,
+    dm, nk, flats, coef, w0b, w1b, w2b, part0, part3, acc_in, inv, inv0, edge, from_edge, shifts,
+    w0h, w1c, w2c, part4, acc, inv_out, d_ref,
 ):
     par = lax.rem(lax.axis_index("slab"), 2)
     nl, nc, nz = dm.nl, dm.nc, dm.nz
@@ -498,21 +501,21 @@
 
     blocks(0, nz, edges, 4)
 
-    W0 = stack(dm, w0a, range(1, nl)) | stack(dm, w0b, (0,)) | stack(dm, w0h, (-1,))
-    W1 = stack(dm, w1a, range(2, nl)) | stack(dm, w1b, (1,)) | stack(dm, w1c, (0,))
+    W0 = stack(dm, w0b, (0,)) | stack(dm, w0h, (-1,))
+    W1 = stack(dm, w1b, (1,)) | stack(dm, w1c, (0,))
     W2 = stack(dm, w2b, (2,)) | stack(dm, w2c, (1,))
     R = stack(dm, inv_out, (-1,)) | stack(dm, inv0, (0,)) | stack(dm, inv, (1, 2))
 
     st.start(d_next, hp["b1"], W0[-1], R[-1])
-    st.apply(W0[0], [(x_edge, W0[-1]), (xf[0], W0[1])], W1[0], R[0], (yf[0], zf[0]), moment=1)
-    st.apply(W1[1], [(xf[0], W1[0]), (xf[1], W1[2])], W2[1], R[1], (yf[1], zf[1]), moment=3)
-    st.apply(W1[0], [(xf[0], W1[1])], Plane(part3, 0, nz), yz=(yf[0], zf[0]))
+    st.apply(W0[0], [(x_edge, W0[-1])], W1[0], R[0], base=Plane(part0, 0, nz), moment=1)
+    st.apply(W1[1], [(xf[0], W1[0])], W2[1], R[1], base=Plane(part3, 0, nz), moment=3)
+    st.apply(W1[0], [(xf[0], W1[1])], Plane(part4, 0, nz), yz=(yf[0], zf[0]))
     st.face_sum(W2[1], (xf[1], W2[2]), (yf[1], zf[1]))
 
 
 def far_b_body(
-    dm, nk, flats, coef, w0b, w0h, w1c, w2c, part3, acc_in, edge, inv0, inv1, from_edge,
-    swap_a, swap_b, shifts, w2d, acc, w1h, inv_out, w0f, shared,
+    dm, nk, flats, coef, w0b, w0h, w1c, w2c, part4, acc_in, edge, inv0, inv1, from_edge,
+    swap_a, swap_b, shifts, w2d, acc, w1h, inv_out, shared, w0x,
 ):
     par = lax.rem(lax.axis_index("slab"), 2)
     side_field = lax.rem(lax.axis_index("field"), 2)
@@ -523,54 +526,66 @@
 
     @pl.when(side_field == 0)
     def _():
-        shared[0 : dm.rows_yz, :] = swap_a[...]
-        shared[dm.rows_yz :, :] = swap_b[...]
+        shared[0 : dm.rows_swap, :] = swap_a[...]
+        shared[dm.rows_swap :, :] = swap_b[...]
 
     @pl.when(side_field == 1)
     def _():
-        shared[0 : dm.rows_yz, :] = swap_b[...]
-        shared[dm.rows_yz :, :] = swap_a[...]
-
-    at_x = {name: row + dm.rows_yz for name, row in dm.at_x.items()}
+        shared[0 : dm.rows_swap, :] = swap_b[...]
+        shared[dm.rows_swap :, :] = swap_a[...]
+
+    at_x = {name: row + dm.rows_swap for name, row in dm.at_x.items()}
     hp = halo_planes(dm, st, (from_edge, dm.at_edge), (shared, dm.at_yz), (shared, at_x))
     acc[...] = acc_in[...]
-    for ref in (w2d, w1h, w0f):
+    for ref in (w2d, w1h):
         clear_pads(dm, nk, ref)
     x_edge = Plane(edge.at[1], 0, nz)
-    W0 = stack(dm, w0b, (0,)) | stack(dm, w0h, (-1,)) | stack(dm, w0f, (-2,))
+    W0 = stack(dm, w0b, (0,)) | stack(dm, w0h, (-1,))
+    behind = Plane(w0x, 0, nz)
     W1 = stack(dm, w1c, (0,)) | stack(dm, w1h, (-1,))
     W2 = stack(dm, w2c, (1,)) | stack(dm, w2d, (0,))
     R = stack(dm, inv0, (0,)) | stack(dm, inv1, (-1,)) | stack(dm, inv_out, (-2,))
-    st.start(hp["d2"], hp["b2"], W0[-2], R[-2])
-    st.apply(
-        W0[-1], [(hp["fx2"], W0[-2]), (x_edge, W0[0])], W1[-1], R[-1], (hp["fy1"], hp["fz1"])
-    )
-    st.apply(W1[0], [(x_edge, W1[-1])], W2[0], R[0], base=Plane(part3, 0, nz), moment=3)
+    st.start(hp["d2"], hp["g2"], behind, R[-2])
+    st.apply(W0[-1], [(None, behind), (x_edge, W0[0])], W1[-1], R[-1], (hp["fy1"], hp["fz1"]))
+    st.apply(W1[0], [(x_edge, W1[-1])], W2[0], R[0], base=Plane(part4, 0, nz), moment=3)
     st.face_sum(W2[0], (xf[0], W2[1]), (yf[0], zf[0]))
 
 
 def far_c_body(
-    dm, nk, w0h, w0f, w1c, w1h, w2d, acc_in, edge, inv1, inv2, from_rest, shared, shifts,
-    moments, acc, w0g, w1g, w2g,
+    dm, nk, w0h, w1c, w1h, w2d, acc_in, edge, inv1, inv2, from_edge, rest_a, rest_b, shared, shifts,
+    moments, acc, w0g, w1g, w2g, w0m, rest,
 ):
     par = lax.rem(lax.axis_index("slab"), 2)
-    nz = dm.nz
+    nz, nc = dm.nz, dm.nc
     st = Steps(dm, nk, par, acc, shifts)
-    at_x = {name: row + dm.rows_yz for name, row in dm.at_x.items()}
-    hp = halo_planes(dm, st, (from_rest, dm.at_rest), (shared, dm.at_yz), (shared, at_x))
+    rest[...] = rest_a[...] + rest_b[...]
+    at_x = {name: row + dm.rows_swap for name, row in dm.at_x.items()}
+    hp = halo_planes(dm, st, (from_edge, dm.at_edge), (rest, dm.at_rest), (shared, dm.at_yz), (shared, at_x))
     acc[...] = acc_in[...]
     x_edge = Plane(edge.at[1], 0, nz)
     far, near, w2 = [Plane(ref, 0, dm.half, st.zs) for ref in (w0g, w1g, w2g)]
-    W0 = stack(dm, w0h, (-1,)) | stack(dm, w0f, (-2,))
+    behind = Plane(w0m, PAD, dm.more, st.zm)
+    W0 = stack(dm, w0h, (-1,))
     W1 = stack(dm, w1c, (0,)) | stack(dm, w1h, (-1,))
     W2 = stack(dm, w2d, (0,))
     R = stack(dm, inv1, (-1,)) | stack(dm, inv2, (-2,))
+    for k in range(nk):
+        w0m[k, 0:PAD, :] = jnp.zeros((PAD, LANES), jnp.float32)
+        w0m[k, PAD + nc * dm.more :, :] = jnp.zeros((PAD, LANES), jnp.float32)
+
+    def right_side(z):
+        for c in range(nc):
+            rhs = hp["g2"].get(c, z) / jnp.maximum(hp["fx2h"].get(c, z), 0.1)
+            for k in range(nk):
+                behind.put(c, z, rhs * R[-2].get(c, z, k), k)
+
+    blocks(st.zm, dm.more, right_side)
     st.start(hp["d3"], hp["g3"], far, half=True)
     st.apply(
-        W0[-2], [(None, far), (hp["fx2"], W0[-1])], near, R[-2], (hp["fy2"], hp["fz2"]), half=True
+        behind, [(None, far), (hp["fx2h"], W0[-1])], near, R[-2], (hp["fy2"], hp["fz2"]), half=True
     )
     st.apply(
-        W1[-1], [(hp["fx2"], near), (x_edge, W1[0])], w2, R[-1], (hp["fy1"], hp["fz1"]), half=True
+        W1[-1], [(hp["fx2h"], near), (x_edge, W1[0])], w2, R[-1], (hp["fy1"], hp["fz1"]), half=True
     )
     st.face_sum(W2[0], (x_edge, w2), half=True)
 
@@ -662,7 +677,6 @@
     half_stack = pltpu.VMEM((nk, dm.nc * dm.half, LANES), f32)
     plane_stack = shape(nk, dm.plane, LANES)
     sums = shape(6 * nk * 8, LANES)
-    assert dm.rows_yz == dm.rows_x
 
     to_swap, to_edge, to_rest, to_in, flats, scalars = pl.pallas_call(
         functools.partial(pack_body, dm, nk),
@@ -719,33 +733,36 @@
         (flats, coef, w1a, w1h, acc, inv34, from_in), 3,
     )
     from_first, acc = lax.optimization_barrier((from_first, acc))
-    swap_a = from_first[: dm.rows_yz]
+    swap_a = from_first[: dm.rows_swap]
     swap_b = lax.ppermute(swap_a, "field", [(i, i ^ 1) for i in range(fields)])
-    w0b, w1b, w2b, acc, edge, inv0 = call(
+    w0b, w1b, w2b, acc, edge, inv0, part0, part3 = call(
         far_0_body, "far_0", 20,
-        (wide(1), wide(1), wide(1), sums, shape(2, dm.plane, LANES), wide(1)),
+        (wide(1), wide(1), wide(1), sums, shape(2, dm.plane, LANES), wide(1), plane_stack, plane_stack),
         [],
         (flats, coef, w0a, w1a, w2a, part1, part2, acc, inv12, from_first), 2,
     )
     to_rest, acc = lax.optimization_barrier((to_rest, acc))
-    from_rest = lax.ppermute(to_rest, "slab", outward)
-    w0h, w1c, w2c, part3, acc, inv1 = call(
+    rest_a = lax.ppermute(to_rest, "slab", outward[0::4] + outward[1::4])
+    w0h, w1c, w2c, part4, acc, inv1 = call(
         far_a_body, "far_a", 20,
         (wide(1), wide(1), wide(1), plane_stack, sums, wide(1)),
         [pltpu.VMEM((dm.plane, LANES), f32)],
-        (flats, coef, w0a, w0b, w1a, w1b, w2b, acc, inv12, inv0, edge, from_edge), 4,
-    )
-    w2d, acc, w1h, inv2, w0f, shared = call(
+        (flats, coef, w0b, w1b, w2b, part0, part3, acc, inv12, inv0, edge, from_edge), 4,
+    )
+    to_rest, from_edge = lax.optimization_barrier((to_rest, from_edge))
+    rest_b = lax.ppermute(to_rest, "slab", outward[2::4] + outward[3::4])
+    w2d, acc, w1h, inv2, shared = call(
         far_b_body, "far_b", 20,
-        (wide(1), sums, wide(1), wide(1), wide(1), shape(dm.rows_yz + dm.rows_x, LANES)),
-        [],
-        (flats, coef, w0b, w0h, w1c, w2c, part3, acc, edge, inv0, inv1, from_edge, swap_a, swap_b), 3,
+        (wide(1), sums, wide(1), wide(1), shape(2 * dm.rows_swap, LANES)),
+        [pltpu.VMEM((nk, dm.plane, LANES), f32)],
+        (flats, coef, w0b, w0h, w1c, w2c, part4, acc, edge, inv0, inv1, from_edge, swap_a, swap_b), 3,
     )
     moments, _ = call(
         far_c_body, "far_c", 20,
         (shape(1, LANES), sums),
-        [half_stack] * 3,
-        (w0h, w0f, w1c, w1h, w2d, acc, edge, inv1, inv2, from_rest, shared), 2,
+        [half_stack] * 3
+        + [pltpu.VMEM((nk, dm.nc * dm.more + 2 * PAD, LANES), f32), pltpu.VMEM((dm.rows_rest, LANES), f32)],
+        (w0h, w1c, w1h, w2d, acc, edge, inv1, inv2, from_edge, rest_a, rest_b, shared), 2,
     )
 
     everywhere = jnp.broadcast_to(moments[None], (count, 1, LANES))

time: 50.5 us -> 48.1 us (0.952)
  blocking collectives: 20.5 us -> 17.2 us
  Pallas kernels: 19.4 us -> 20.6 us
  waiting for transfers between devices: 3.01 us -> 2.02 us
  starting transfers between devices: 5.49 us -> 6.18 us
    all_to_all x1, blocking collectives: 20.5 us -> 17.2 us  [on_device(): gathered = lax.all_to_all(everywhere, 'slab', 0, 0)]
    pallas_call x6, Pallas kernels: 15.9 us -> 17 us  [call(): pl.pallas_call(functools.partial(body, dm, nk), out_shape=results, in_spe...]
    ppermute x1, waiting for transfers between devices: 0.99 us -> 0.01 us  [on_device(): swap_b = lax.ppermute(swap_a, 'field', [(i, i ^ 1) for i in range(fields)])]
    ppermute x1 -> x2, starting transfers between devices: 0.68 us -> 1.35 us  [the longest x1 0.67 us: on_device(): rest_a = lax.ppermute(to_rest, 'slab', outward[0::4] + outward[1::4])]
  transfers between devices with their start and end apart: 5 -> 6, of which waited for: 2 -> 1; matrix products, arithmetic and copies ran while one was open for 0% -> 0% of each run, Pallas kernels for 28% -> 32%
where the time goes in v5:
time: 48.1 us; the launch traced here: 47.8 us
  Pallas kernels  20.6 us (43%)
  blocking collectives  17.2 us (36%)
  starting transfers between devices  6.18 us (13%)
  waiting for transfers between devices  2.02 us (4%)
  other arithmetic  1.39 us (3%)
    all_to_all x1, blocking collectives, on_device(): gathered = lax.all_to_all(everywhere, 'slab', 0, 0)  17.2 us
    pallas_call x6, Pallas kernels, call(): pl.pallas_call(functools.partial(body, dm, nk), out_shape=results, in_spe...  17 us
    ppermute x1, starting transfers between devices, on_device(): swap_b = lax.ppermute(swap_a, 'field', [(i, i ^ 1) for i in range(fields)])  2.96 us
    pallas_call x1, Pallas kernels, on_device(): pl.pallas_call(functools.partial(combine_body, dm, nk), out_shape=jax.Sha...  2.17 us
    ppermute x1, waiting for transfers between devices, on_device(): from_in = lax.ppermute(to_in, 'slab', [(i, i ^ 1) for i in range(count)])  2.01 us
    pallas_call x1, Pallas kernels, on_device(): pl.pallas_call(functools.partial(pack_body, dm, nk), out_shape=(shape(dm....  1.43 us
    another operation x1, other arithmetic, on_device(): jnp.stack([cond_x, cond_y])  1.39 us
  transfers between devices with their start and end apart: 6, of which 1 were waited for; matrix products, arithmetic and copies ran while one was open for 0% of the time, Pallas kernels for 32%

profile of v5, /device:TPU:0, one launch (start us, length us, event | category | flops | bytes accessed | tf_op | source)
XLA Modules:
  0.0 47.8 jit_solution(10305560862719989220)
XLA Ops:
  0.0 0.0 copy-start.3
  0.0 0.0 copy-start.4
  0.0 0.0 copy-start
  0.0 0.0 copy-start.1
  0.0 0.0 copy-start.2
  0.0 1.4 %pad_maximum_fusion.conds = f32[2,4,64,512]{3,2,1,0:T(8,128)S(1)} fusion(f32[1,4,64,512]{3,2,1,0:T(8,128)} %bitcast.8, f32[1,4,64,512]{3,2,1,0:T(8,128)} %bitcast.9), kind=kLoop, calls=%fused_computation | loop fusion | flops 262144 | bytes 2097152 | tf_op jit(solution)/shard_map/stack | solution.py:694
  1.4 0.0 copy-done.3
  1.4 0.0 copy-done.4
  1.4 0.0 copy-done
  1.4 0.1 copy-done.1
  1.5 0.2 copy-done.2
  1.7 1.4 %pack.1 = (f32[800,128]{1,0:T(8,128)S(1)}, f32[768,128]{1,0:T(8,128)S(1)}, f32[416,128]{1,0:T(8,128)S(1)}, f32[2600,128]{1,0:T(8,128)S(1)}, f32[5,1064,128]{2,1,0:T(8,128)S(1)}, /*index=5*/f32[72,128]{1,0:T(8,128)S(1)}) custom-call(f32[2,4,64,512]{3,2,1,0:T(8,128)S(1)} %pad_maximum_fusion.conds, f32[4,64,512]{2,1,0:T(8,128)S(1)} %copy-done, ...), custom_call_target="tpu_custom_call" | custom-call | tf_op jit(solution)/shard_map/pack/pallas_call | solution.py:681
  3.1 0.5 %collective-permute-start = (f32[2600,128]{1,0:T(8,128)S(1)}, f32[2600,128]{1,0:T(8,128)S(1)}, u32[]{:S(2)}, u32[]{:S(2)}) collective-permute-start(f32[2600,128]{1,0:T(8,128)S(1)} %get-tuple-element.51), channel_id=1, source_target_pairs={{0,1},{1,0},{2,3},{3,2},{4,5},{5,4},{6,7},{7,6},{8,9},{9,8},{10,11... | collective-permute-start | bytes 3993608 | tf_op jit(solution)/shard_map/ppermute | solution.py:698
  3.7 0.7 %collective-permute-start.1 = (f32[800,128]{1,0:T(8,128)S(1)}, f32[800,128]{1,0:T(8,128)S(1)}, u32[]{:S(2)}, u32[]{:S(2)}) collective-permute-start(f32[800,128]{1,0:T(8,128)S(1)} %get-tuple-element.64), channel_id=1, source_target_pairs={{1,2},{2,1},{3,4},{4,3},{5,6},{6,5},{7,8},{8,7},{9,10},{10,9},{11,... | collective-permute-start | bytes 1228808 | tf_op jit(solution)/shard_map/ppermute | solution.py:697
  4.3 2.0 %collective-permute-done.from_in = f32[2600,128]{1,0:T(8,128)S(1)} collective-permute-done((f32[2600,128]{1,0:T(8,128)S(1)}, f32[2600,128]{1,0:T(8,128)S(1)}, u32[]{:S(2)}, u32[]{:S(2)}) %collective-permute-start) | collective-permute-done | bytes 1331232 | tf_op jit(solution)/shard_map/ppermute | solution.py:698
  6.3 5.0 %near_a.1 = (f32[8,800,128]{2,1,0:T(8,128)S(1)}, f32[8,536,128]{2,1,0:T(8,128)S(1)}, f32[8,536,128]{2,1,0:T(8,128)S(1)}, f32[8,256,128]{2,1,0:T(8,128)S(1)}, f32...) custom-call(f32[5,1064,128]{2,1,0:T(8,128)S(1)} %get-tuple-element.50.fl, ...), custom_call_target="tpu_custom_call" | custom-call | flops 1000000 | bytes 18000000 | tf_op jit(solution)/shard_map/near_a/pallas_call | solution.py:702
  11.4 0.7 %collective-permute-start.2 = (f32[768,128]{1,0:T(8,128)S(1)}, f32[768,128]{1,0:T(8,128)S(1)}, u32[]{:S(2)}, u32[]{:S(2)}) collective-permute-start(f32[768,128]{1,0:T(8,128)S(1)} %get-tuple-element.79), channel_id=1, source_target_pairs={{1,2},{2,1},{3,4},{4,3},{5,6},{6,5},{7,8},{8,7},{9,10},{10,9},{11,... | collective-permute-start | bytes 1179656 | tf_op jit(solution)/shard_map/ppermute | solution.py:728
  12.1 2.7 %near_b.1 = (f32[8,272,128]{2,1,0:T(8,128)S(1)}, f32[8,256,128]{2,1,0:T(8,128)S(1)}, f32[384,128]{1,0:T(8,128)S(1)}) custom-call(f32[5,1064,128]{2,1,0:T(8,128)S(1)} %get-tuple-element.50.flats, f32[1064,128]{1,0:T(8,128)S(1)} %get-tuple-element.53.coef, f32[8,536,128]{2,1,0:T(8,128)S(1)} %get-tuple-element.55.w1a, ...), custom_call_target="tpu_custom_call" | custom-call | flops 1000000 | bytes 9000000 | tf_op jit(solution)/shard_map/near_b/pallas_call | solution.py:702
  14.8 0.0 collective-permute-done.1.from_first
  14.8 3.0 %collective-permute-start.3 = (f32[544,128]{1,0:T(8,128)S(1)}, f32[544,128]{1,0:T(8,128)S(1)}, u32[]{:S(2)}, u32[]{:S(2)}) collective-permute-start(f32[544,128]{1,0:T(8,128)S(1)} %slice.3.swap_a), channel_id=1, source_target_pairs={{0,16},{16,0},{1,17},{17,1},{2,18},{18,2},{3,19},{19,3},{4,20},{20... | collective-permute-start | bytes 835592 | tf_op jit(solution)/shard_map/ppermute | solution.py:737
  17.8 3.1 %far_0.1 = (f32[8,272,128]{2,1,0:T(8,128)S(1)}, f32[8,272,128]{2,1,0:T(8,128)S(1)}, f32[8,272,128]{2,1,0:T(8,128)S(1)}, f32[384,128]{1,0:T(8,128)S(1)}, f32[2,25...) custom-call(f32[5,1064,128]{2,1,0:T(8,128)S(1)} %get-tuple-element.50., ...), custom_call_target="tpu_custom_call" | custom-call | flops 1000000 | bytes 6000000 | tf_op jit(solution)/shard_map/far_0/pallas_call | solution.py:702
  20.9 0.7 %collective-permute-start.4 = (f32[416,128]{1,0:T(8,128)S(1)}, f32[416,128]{1,0:T(8,128)S(1)}, u32[]{:S(2)}, u32[]{:S(2)}) collective-permute-start(f32[416,128]{1,0:T(8,128)S(1)} %get-tuple-element.92), channel_id=1, source_target_pairs={{1,2},{5,6},{9,10},{13,14},{2,1},{6,5},{10,9},{14,13},{17,18},{21,... | collective-permute-start | bytes 638984 | tf_op jit(solution)/shard_map/ppermute | solution.py:745
  21.5 0.0 collective-permute-done.2.from_edge
  21.5 0.7 %collective-permute-start.5 = (f32[416,128]{1,0:T(8,128)S(1)}, f32[416,128]{1,0:T(8,128)S(1)}, u32[]{:S(2)}, u32[]{:S(2)}) collective-permute-start(f32[416,128]{1,0:T(8,128)S(1)} %get-tuple-element.92), channel_id=1, source_target_pairs={{3,4},{7,8},{11,12},{4,3},{8,7},{12,11},{19,20},{23,24},{27,28},{2... | collective-permute-start | bytes 638984 | tf_op jit(solution)/shard_map/ppermute | solution.py:753
  22.2 2.3 %far_a.1 = (f32[8,272,128]{2,1,0:T(8,128)S(1)}, f32[8,272,128]{2,1,0:T(8,128)S(1)}, f32[8,272,128]{2,1,0:T(8,128)S(1)}, f32[8,256,128]{2,1,0:T(8,128)S(1)}, f32[...) custom-call(f32[5,1064,128]{2,1,0:T(8,128)S(1)} %get-tuple-element.50.flats, f32[1064,128]{1,0:T(8,128)S(1)} %get-tuple-element.53.coef, ...), custom_call_target="tpu_custom_call" | custom-call | flops 1000000 | bytes 12000000 | tf_op jit(solution)/shard_map/far_a/pallas_call | solution.py:702
  24.5 0.0 collective-permute-done.3.swap_b
  24.6 2.0 %far_b.1 = (f32[8,272,128]{2,1,0:T(8,128)S(1)}, f32[384,128]{1,0:T(8,128)S(1)}, f32[8,272,128]{2,1,0:T(8,128)S(1)}, f32[8,272,128]{2,1,0:T(8,128)S(1)}, f32[1088,128]{1,0:T(8,128)S(1)}) custom-call(f32[5,1064,128]{2,1,0:T(8,128)S(1)} %get-tuple-element.50.flats, f32[1064,128]{1,0:T(8,128)S(1)} %get-tuple-element.53.coef, ...), custom_call_target="tpu_custom_call" | custom-call | flops 1000000 | bytes 9000000 | tf_op jit(solution)/shard_map/far_b/pallas_call | solution.py:702
  26.6 0.0 collective-permute-done.4.rest_a
  26.6 0.0 collective-permute-done.5.rest_b
  26.6 1.9 %far_c.1 = (f32[1,128]{1,0:T(1,128)S(1)}, f32[384,128]{1,0:T(8,128)}) custom-call(f32[8,272,128]{2,1,0:T(8,128)S(1)} %get-tuple-element.80.w0h, f32[8,272,128]{2,1,0:T(8,128)S(1)} %get-tuple-element.81.w1c, f32[8,272,128]{2,1,0:T(8,128)S(1)} %get-tuple-element.88.w1h, f32[8,272,128]{2,1,0:T(8,128)S(1)} %get-tuple-element.89.w2d, ...), custom_call_target="tpu_custom_call" | custom-call | flops 1000000 | bytes 6000000 | tf_op jit(solution)/shard_map/far_c/pallas_call | solution.py:702
  28.5 17.2 %all_to_all.5.moments = f32[16,1,128]{2,1,0:T(1,128)S(1)} all-to-all(f32[16,1,128]{2,1,0:T(1,128)S(1)} %broadcast_in_dim.17), channel_id=1, replica_groups=mesh['field'=2,'slab'=16] {'slab'}, dimensions={0} | all-to-all | bytes 16384 | tf_op jit(solution)/shard_map/all_to_all | solution.py:769
  45.7 2.2 %combine.1 = f32[4,64,512]{2,1,0:T(8,128)} custom-call(f32[16,1,128]{2,1,0:T(1,128)S(1)} %all_to_all.5.moments, f32[72,128]{1,0:T(8,128)S(1)} %get-tuple-element.52.shifts.scalars, f32[8,800,128]{2,1,0:T(8,128)S(1)} %get-tuple-element.54.w0a, f32[8,272,128]{2,1,0:T(8,128)S(1)} %get-tuple-element.69.w0b, f32[8,536,128]{2,1,0:T(8,128)S(1)} %get-tuple-element.55.w1a, ...), custom_call_target="tpu_custom_call" | custom-call | tf_op jit(solution)/shard_map/combine/pallas_call | solution.py:771
  (2 shorter events, 0.0 us)
Async XLA Ops:
  0.0 1.4 %copy-start.3 = (f32[8]{0:T(128)S(1)}, f32[8]{0:T(128)}, u32[]{:S(2)}) copy-start(f32[8]{0:T(128)} %param.12) | copy-start | bytes 100
  0.0 1.4 %copy-start.4 = (f32[8]{0:T(128)S(1)}, f32[8]{0:T(128)}, u32[]{:S(2)}) copy-start(f32[8]{0:T(128)} %param.13) | copy-start | bytes 100
  0.0 1.4 %copy-start = (f32[4,64,512]{2,1,0:T(8,128)S(1)}, f32[4,64,512]{2,1,0:T(8,128)}, u32[]{:S(2)}) copy-start(f32[4,64,512]{2,1,0:T(8,128)} %cz.1) | copy-start | bytes 1572868
  0.0 1.5 %copy-start.1 = (f32[4,64,512]{2,1,0:T(8,128)S(1)}, f32[4,64,512]{2,1,0:T(8,128)}, u32[]{:S(2)}) copy-start(f32[4,64,512]{2,1,0:T(8,128)} %kappa.1) | copy-start | bytes 1572868
  0.0 1.7 %copy-start.2 = (f32[4,64,512]{2,1,0:T(8,128)S(1)}, f32[4,64,512]{2,1,0:T(8,128)}, u32[]{:S(2)}) copy-start(f32[4,64,512]{2,1,0:T(8,128)} %b.1) | copy-start | bytes 1572868
  3.1 3.2 %collective-permute-start = (f32[2600,128]{1,0:T(8,128)S(1)}, f32[2600,128]{1,0:T(8,128)S(1)}, u32[]{:S(2)}, u32[]{:S(2)}) collective-permute-start(f32[2600,128]{1,0:T(8,128)S(1)} %get-tuple-element.51), channel_id=1, source_target_pairs={{0,1},{1,0},{2,3},{3,2},{4,5},{5,4},{6,7},{7,6},{8,9},{9,8},{10,11... | collective-permute-start | bytes 3993608 | tf_op jit(solution)/shard_map/ppermute | solution.py:698
  3.7 11.1 %collective-permute-start.1 = (f32[800,128]{1,0:T(8,128)S(1)}, f32[800,128]{1,0:T(8,128)S(1)}, u32[]{:S(2)}, u32[]{:S(2)}) collective-permute-start(f32[800,128]{1,0:T(8,128)S(1)} %get-tuple-element.64), channel_id=1, source_target_pairs={{1,2},{2,1},{3,4},{4,3},{5,6},{6,5},{7,8},{8,7},{9,10},{10,9},{11,... | collective-permute-start | bytes 1228808 | tf_op jit(solution)/shard_map/ppermute | solution.py:697
  11.4 10.2 %collective-permute-start.2 = (f32[768,128]{1,0:T(8,128)S(1)}, f32[768,128]{1,0:T(8,128)S(1)}, u32[]{:S(2)}, u32[]{:S(2)}) collective-permute-start(f32[768,128]{1,0:T(8,128)S(1)} %get-tuple-element.79), channel_id=1, source_target_pairs={{1,2},{2,1},{3,4},{4,3},{5,6},{6,5},{7,8},{8,7},{9,10},{10,9},{11,... | collective-permute-start | bytes 1179656 | tf_op jit(solution)/shard_map/ppermute | solution.py:728
  14.8 9.8 %collective-permute-start.3 = (f32[544,128]{1,0:T(8,128)S(1)}, f32[544,128]{1,0:T(8,128)S(1)}, u32[]{:S(2)}, u32[]{:S(2)}) collective-permute-start(f32[544,128]{1,0:T(8,128)S(1)} %slice.3.swap_a), channel_id=1, source_target_pairs={{0,16},{16,0},{1,17},{17,1},{2,18},{18,2},{3,19},{19,3},{4,20},{20... | collective-permute-start | bytes 835592 | tf_op jit(solution)/shard_map/ppermute | solution.py:737
  20.9 5.8 %collective-permute-start.4 = (f32[416,128]{1,0:T(8,128)S(1)}, f32[416,128]{1,0:T(8,128)S(1)}, u32[]{:S(2)}, u32[]{:S(2)}) collective-permute-start(f32[416,128]{1,0:T(8,128)S(1)} %get-tuple-element.92), channel_id=1, source_target_pairs={{1,2},{5,6},{9,10},{13,14},{2,1},{6,5},{10,9},{14,13},{17,18},{21,... | collective-permute-start | bytes 638984 | tf_op jit(solution)/shard_map/ppermute | solution.py:745
  21.5 5.1 %collective-permute-start.5 = (f32[416,128]{1,0:T(8,128)S(1)}, f32[416,128]{1,0:T(8,128)S(1)}, u32[]{:S(2)}, u32[]{:S(2)}) collective-permute-start(f32[416,128]{1,0:T(8,128)S(1)} %get-tuple-element.92), channel_id=1, source_target_pairs={{3,4},{7,8},{11,12},{4,3},{8,7},{12,11},{19,20},{23,24},{27,28},{2... | collective-permute-start | bytes 638984 | tf_op jit(solution)/shard_map/ppermute | solution.py:753

commit v6 on v5

--- a/solution.py
+++ b/solution.py
@@ -104,17 +104,17 @@
     return [Plane(ref, PAD + p * dm.slot, dm.nz) for p in range(dm.nl)]
 
 
-def prepare(dm, par, cx, cy, cz, kappa, b, flats):
+def prepare(dm, par, cx, cy, cz, kappa, flats):
     nc, nz, nl = dm.nc, dm.nz, dm.nl
-    bf, df, xf, yf, zf, tf = [own_planes(dm, ref) for ref in flats]
-    for ref in (flats[4], flats[5]):
+    df, xf, yf, zf, tf = [own_planes(dm, ref) for ref in flats]
+    for ref in (flats[3], flats[4]):
         for p in range(nl + 1):
             ref[p * dm.slot : p * dm.slot + PAD, :] = jnp.zeros((PAD, LANES), jnp.float32)
     layers = [jnp.where(par == 0, p, nl - 1 - p) for p in range(nl)]
 
     def copy(z):
         for p in range(nl):
-            for src, dst in ((b, bf), (cx, xf), (cz, tf)):
+            for src, dst in ((cx, xf), (cz, tf)):
                 block = src[layers[p], pl.ds(z, 8), :]
                 for c in range(nc):
                     dst[p].put(c, z, block[:, c * LANES : (c + 1) * LANES])
@@ -152,72 +152,90 @@
     blocks(0, nz, all_faces)
 
 
-def pack_body(
-    dm, nk, conds, cz, kappa, b, shifts, weights, to_swap, to_edge, to_rest, to_in, coef, scalars, temp,
-):
+class Packer:
+    def __init__(self, dm, par):
+        self.dm = dm
+        self.zs = pl.multiple_of((1 - par) * dm.half, 8)
+        self.zm = pl.multiple_of((1 - par) * (dm.nz - dm.more), 8)
+
+    def fill(self, out, at, z_count, sources):
+        def body(n):
+            for name, value in sources:
+                for c in range(self.dm.nc):
+                    out[pl.ds(pl.multiple_of(n, 8) + (at[name] + c * z_count), 8), :] = value(c, n)
+
+        blocks(0, z_count, body, min(4, z_count // 8) if z_count % 32 == 0 else 1)
+
+    def yz(self, out, at, yf, zf, one):
+        out[at["pad"] : at["pad"] + PAD, :] = jnp.zeros((PAD, LANES), jnp.float32)
+        self.fill(out, at, self.dm.nz, [
+            ("fz1", lambda c, n: zf[one].get(c, n)),
+            ("fy1", lambda c, n: yf[one].get(c, n)),
+        ])
+
+    def third(self, out, at, df, three):
+        self.fill(out, at, self.dm.half, [("d3", lambda c, n: df[three].get(c, self.zs + n))])
+
+
+def x_face_of(xf):
+    return lambda c, z, one, two: 0.5 * (xf[one].get(c, z) + xf[two].get(c, z))
+
+
+def pack_faces_body(dm, nk, conds, cz, kappa, shifts, weights, to_swap, coef, scalars, temp):
     par = lax.rem(lax.axis_index("slab"), 2)
     side_field = lax.rem(lax.axis_index("field"), 2)
-    nc, nz, nl = dm.nc, dm.nz, dm.nl
+    prepare(dm, par, conds.at[0], conds.at[1], cz, kappa, [coef.at[n] for n in range(4)] + [temp])
+    df, xf, yf, zf = [own_planes(dm, coef.at[n]) for n in range(4)]
+    x_face = x_face_of(xf)
+    to = Packer(dm, par)
+
+    @pl.when(side_field == 0)
+    def _():
+        to.yz(to_swap, dm.at_yz, yf, zf, 0)
+        if dm.rows_swap > dm.rows_yz:
+            to_swap[dm.rows_yz : dm.rows_swap, :] = jnp.zeros((dm.rows_swap - dm.rows_yz, LANES), jnp.float32)
+
+    @pl.when(side_field == 1)
+    def _():
+        to.fill(to_swap, dm.at_x, dm.more, [("fx2h", lambda c, n: x_face(c, to.zm + n, 0, 1))])
+        to.fill(to_swap, dm.at_x, dm.nz, [("d2", lambda c, n: df[1].get(c, n))])
+        to.third(to_swap, dm.at_x, df, 2)
+
+    to.fill(to_swap, dm.at_first, dm.nz, [("x1", lambda c, n: xf[0].get(c, n))])
     for k in range(nk):
         scalars[k * 8 : k * 8 + 8, :] = jnp.broadcast_to(shifts[:, k : k + 1], (8, LANES))
     scalars[nk * 8 :, :] = jnp.zeros((8, LANES), jnp.float32)
     scalars[nk * 8 : nk * 8 + 1, 0:nk] = weights[...]
-    raw = [conds.at[0], conds.at[1], cz, kappa, b]
-    prepare(dm, par, *raw, [coef.at[n] for n in range(5)] + [temp])
-    bf, df, xf, yf, zf = [own_planes(dm, coef.at[n]) for n in range(5)]
-    zs = pl.multiple_of((1 - par) * dm.half, 8)
-    zm = pl.multiple_of((1 - par) * (nz - dm.more), 8)
-
-    def x_face(c, z, one, two):
-        return 0.5 * (xf[one].get(c, z) + xf[two].get(c, z))
-
-    def fill(out, at, z_count, sources):
-        def body(n):
-            for name, value in sources:
-                for c in range(nc):
-                    out[pl.ds(pl.multiple_of(n, 8) + (at[name] + c * z_count), 8), :] = value(c, n)
-
-        blocks(0, z_count, body, min(4, z_count // 8) if z_count % 32 == 0 else 1)
-
-    def yz(out, at, one):
-        out[at["pad"] : at["pad"] + PAD, :] = jnp.zeros((PAD, LANES), jnp.float32)
-        fill(out, at, nz, [
-            ("fz1", lambda c, n: zf[one].get(c, n)),
-            ("fy1", lambda c, n: yf[one].get(c, n)),
-        ])
+
+
+def pack_body(dm, b, coef, to_edge, to_rest, to_in, rhs):
+    par = lax.rem(lax.axis_index("slab"), 2)
+    nc, nz, nl = dm.nc, dm.nz, dm.nl
+    df, xf, yf, zf = [own_planes(dm, coef.at[n]) for n in range(4)]
+    bf = own_planes(dm, rhs)
+    layers = [jnp.where(par == 0, p, nl - 1 - p) for p in range(nl)]
+
+    def copy(z):
+        for p in range(nl):
+            block = b[layers[p], pl.ds(z, 8), :]
+            for c in range(nc):
+                bf[p].put(c, z, block[:, c * LANES : (c + 1) * LANES])
+
+    blocks(0, nz, copy)
+    x_face = x_face_of(xf)
+    to = Packer(dm, par)
+    zs, zm = to.zs, to.zm
 
     def rest(out, at, two, three):
-        fill(out, at, dm.half, [
+        to.fill(out, at, dm.half, [
             ("fy2", lambda c, n: yf[two].get(c, zs + n)),
             ("g3", lambda c, n: x_face(c, zs + n, two, three) * bf[three].get(c, zs + n)),
         ])
-        fill(out, at, dm.more, [("fz2", lambda c, n: zf[two].get(c, zm + n))])
-
-    def third(out, at, three):
-        fill(out, at, dm.half, [("d3", lambda c, n: df[three].get(c, zs + n))])
-
-    @pl.when(side_field == 0)
-    def _():
-        yz(to_swap, dm.at_yz, 0)
-        if dm.rows_swap > dm.rows_yz:
-            to_swap[dm.rows_yz : dm.rows_swap, :] = jnp.zeros((dm.rows_swap - dm.rows_yz, LANES), jnp.float32)
-
-    @pl.when(side_field == 1)
-    def _():
-        fill(to_swap, dm.at_x, dm.more, [("fx2h", lambda c, n: x_face(c, zm + n, 0, 1))])
-        fill(to_swap, dm.at_x, nz, [("d2", lambda c, n: df[1].get(c, n))])
-        third(to_swap, dm.at_x, 2)
-
-    fill(to_swap, dm.at_first, nz, [("x1", lambda c, n: xf[0].get(c, n))])
-    fill(to_edge, dm.at_edge, nz, [
-        ("d1", lambda c, n: df[0].get(c, n)),
-        ("b1", lambda c, n: bf[0].get(c, n)),
-        ("g2", lambda c, n: x_face(c, n, 0, 1) * bf[1].get(c, n)),
-    ])
-    rest(to_rest, dm.at_rest, 1, 2)
+        to.fill(out, at, dm.more, [("fz2", lambda c, n: zf[two].get(c, zm + n))])
+
     one, two, three = nl - 1, nl - 2, nl - 3
-    yz(to_in, dm.at_all, one)
-    fill(to_in, dm.at_all, nz, [
+    to.yz(to_in, dm.at_all, yf, zf, one)
+    to.fill(to_in, dm.at_all, nz, [
         ("fx2", lambda c, n: x_face(c, n, one, two)),
         ("d2", lambda c, n: df[two].get(c, n)),
         ("x1", lambda c, n: xf[one].get(c, n)),
@@ -225,8 +243,14 @@
         ("b1", lambda c, n: bf[one].get(c, n)),
         ("b2", lambda c, n: bf[two].get(c, n)),
     ])
-    third(to_in, dm.at_all, three)
+    to.third(to_in, dm.at_all, df, three)
     rest(to_in, dm.at_all, two, three)
+    to.fill(to_edge, dm.at_edge, nz, [
+        ("d1", lambda c, n: df[0].get(c, n)),
+        ("b1", lambda c, n: bf[0].get(c, n)),
+        ("g2", lambda c, n: x_face(c, n, 0, 1) * bf[1].get(c, n)),
+    ])
+    rest(to_rest, dm.at_rest, 1, 2)
 
 
 class Steps:
@@ -251,7 +275,14 @@
     def tiles(self, plane, z, k=None, d=0):
         return [plane.get(c, z, k, d) for c in range(self.dm.nc)]
 
-    def start(self, d, b, w, r=None, half=False, own=False):
+    def fused(self, *bodies, unroll=4):
+        def body(z):
+            for one in bodies:
+                one(z)
+
+        self.sweep(False, body, unroll)
+
+    def start(self, d, b, w, r=None, half=False, own=False, run=True):
         def body(z):
             diagonal, rhs = self.tiles(d, z), self.tiles(b, z)
             for k in range(self.nk):
@@ -265,9 +296,11 @@
                 if own:
                     self.add(0, k, self.total(rhs, value))
 
+        if not run:
+            return body
         self.sweep(half, body, 2)
 
-    def apply(self, v, sides, out, r=None, yz=None, base=None, half=False, moment=None):
+    def apply(self, v, sides, out, r=None, yz=None, base=None, half=False, moment=None, run=True):
         nc = self.dm.nc
 
         def body(z):
@@ -308,9 +341,11 @@
                     self.add(moment, k, self.total(value, image))
                     self.add(moment + 1, k, self.total(result, image))
 
+        if not run:
+            return body
         self.sweep(half, body)
 
-    def face_sum(self, v, side=None, yz=None, half=False):
+    def face_sum(self, v, side=None, yz=None, half=False, run=True):
         nc = self.dm.nc
 
         def body(z):
@@ -331,6 +366,8 @@
                     image = [p + q for p, q in zip(*parts)]
                 self.add(5, k, 2.0 * self.total(value, image))
 
+        if not run:
+            return body
         self.sweep(half, body)
 
 
@@ -358,14 +395,15 @@
 
 
 def near_a_body(
-    dm, nk, flats, from_in, shifts, w0a, w1a, w1h, part1, acc, coef, inv12, inv34,
+    dm, nk, flats, rhs, from_in, shifts, w0a, w1a, w1h, part1, acc, coef, inv12, inv34,
     extra, w0h, inv5,
 ):
     par = lax.rem(lax.axis_index("slab"), 2)
     nl, nc, nz = dm.nl, dm.nc, dm.nz
     last = nl - 1
-    bf, df, raw_x, yf, zf = [own_planes(dm, flats.at[n]) for n in range(5)]
+    df, raw_x, yf, zf = [own_planes(dm, flats.at[n]) for n in range(4)]
     xf = own_planes(dm, coef)
+    bf = own_planes(dm, rhs)
     st = Steps(dm, nk, par, acc, shifts)
     hp = halo_planes(dm, st, (from_in, dm.at_all))
     acc[...] = jnp.zeros(acc.shape, jnp.float32)
@@ -416,7 +454,7 @@
     par = lax.rem(lax.axis_index("slab"), 2)
     nl, nz = dm.nl, dm.nz
     last = nl - 1
-    bf, df, raw_x, yf, zf = [own_planes(dm, flats.at[n]) for n in range(5)]
+    df, raw_x, yf, zf = [own_planes(dm, flats.at[n]) for n in range(4)]
     xf = own_planes(dm, coef)
     st = Steps(dm, nk, par, acc, shifts)
     hp = halo_planes(dm, st, (from_in, dm.at_all))
@@ -442,14 +480,14 @@
 
 
 def far_0_body(
-    dm, nk, flats, coef, w0a, w1a, w2a, part1, part2, acc_in, inv, from_first, shifts,
+    dm, nk, flats, rhs, coef, w0a, w1a, w2a, part1, part2, acc_in, inv, from_first, shifts,
     w0b, w1b, w2b, acc, edge, inv_out, part0, part3,
 ):
     index = lax.axis_index("slab")
     par = lax.rem(index, 2)
     has_off = jnp.where(jnp.logical_and(index > 0, index < lax.axis_size("slab") - 1), 0.5, 0.0)
     nl, nc, nz = dm.nl, dm.nc, dm.nz
-    bf, df, raw_x, yf, zf = [own_planes(dm, flats.at[n]) for n in range(5)]
+    df, raw_x, yf, zf = [own_planes(dm, flats.at[n]) for n in range(4)]
     xf = own_planes(dm, coef)
     st = Steps(dm, nk, par, acc, shifts)
     x1 = Plane(from_first, dm.at_first["x1"], nz)
@@ -472,7 +510,7 @@
     R = stack(dm, inv_out, (0,)) | stack(dm, inv, (1, 2))
     I1, I2 = Plane(part1, 0, nz), Plane(part2, 0, nz)
 
-    st.start(d_here, bf[0], W0[0], R[0], own=True)
+    st.start(d_here, own_planes(dm, rhs)[0], W0[0], R[0], own=True)
     st.apply(W0[1], [(xf[0], W0[0])], W1[1], R[1], base=I1, moment=1)
     st.apply(W1[2], [(xf[1], W1[1])], W2[2], R[2], base=I2, moment=3)
     st.apply(W0[0], [(xf[0], W0[1])], Plane(part0, 0, nz), yz=(yf[0], zf[0]))
@@ -486,7 +524,7 @@
 ):
     par = lax.rem(lax.axis_index("slab"), 2)
     nl, nc, nz = dm.nl, dm.nc, dm.nz
-    bf, df, raw_x, yf, zf = [own_planes(dm, flats.at[n]) for n in range(5)]
+    df, raw_x, yf, zf = [own_planes(dm, flats.at[n]) for n in range(4)]
     xf = own_planes(dm, coef)
     st = Steps(dm, nk, par, acc, shifts)
     hp = halo_planes(dm, st, (from_edge, dm.at_edge))
@@ -506,10 +544,16 @@
     W2 = stack(dm, w2b, (2,)) | stack(dm, w2c, (1,))
     R = stack(dm, inv_out, (-1,)) | stack(dm, inv0, (0,)) | stack(dm, inv, (1, 2))
 
-    st.start(d_next, hp["b1"], W0[-1], R[-1])
-    st.apply(W0[0], [(x_edge, W0[-1])], W1[0], R[0], base=Plane(part0, 0, nz), moment=1)
-    st.apply(W1[1], [(xf[0], W1[0])], W2[1], R[1], base=Plane(part3, 0, nz), moment=3)
-    st.apply(W1[0], [(xf[0], W1[1])], Plane(part4, 0, nz), yz=(yf[0], zf[0]))
+    st.fused(
+        st.start(d_next, hp["b1"], W0[-1], R[-1], run=False),
+        st.apply(W0[0], [(x_edge, W0[-1])], W1[0], R[0], base=Plane(part0, 0, nz), moment=1, run=False),
+    )
+    st.fused(
+        st.apply(W1[0], [(xf[0], W1[1])], Plane(part4, 0, nz), yz=(yf[0], zf[0]), run=False),
+        st.apply(
+            W1[1], [(xf[0], W1[0])], W2[1], R[1], base=Plane(part3, 0, nz), moment=3, run=False
+        ),
+    )
     st.face_sum(W2[1], (xf[1], W2[2]), (yf[1], zf[1]))
 
 
@@ -520,7 +564,7 @@
     par = lax.rem(lax.axis_index("slab"), 2)
     side_field = lax.rem(lax.axis_index("field"), 2)
     nl, nc, nz = dm.nl, dm.nc, dm.nz
-    bf, df, raw_x, yf, zf = [own_planes(dm, flats.at[n]) for n in range(5)]
+    df, raw_x, yf, zf = [own_planes(dm, flats.at[n]) for n in range(4)]
     xf = own_planes(dm, coef)
     st = Steps(dm, nk, par, acc, shifts)
 
@@ -546,19 +590,22 @@
     W2 = stack(dm, w2c, (1,)) | stack(dm, w2d, (0,))
     R = stack(dm, inv0, (0,)) | stack(dm, inv1, (-1,)) | stack(dm, inv_out, (-2,))
     st.start(hp["d2"], hp["g2"], behind, R[-2])
-    st.apply(W0[-1], [(None, behind), (x_edge, W0[0])], W1[-1], R[-1], (hp["fy1"], hp["fz1"]))
-    st.apply(W1[0], [(x_edge, W1[-1])], W2[0], R[0], base=Plane(part4, 0, nz), moment=3)
+    st.fused(
+        st.apply(
+            W0[-1], [(None, behind), (x_edge, W0[0])], W1[-1], R[-1], (hp["fy1"], hp["fz1"]), run=False
+        ),
+        st.apply(W1[0], [(x_edge, W1[-1])], W2[0], R[0], base=Plane(part4, 0, nz), moment=3, run=False),
+    )
     st.face_sum(W2[0], (xf[0], W2[1]), (yf[0], zf[0]))
 
 
 def far_c_body(
-    dm, nk, w0h, w1c, w1h, w2d, acc_in, edge, inv1, inv2, from_edge, rest_a, rest_b, shared, shifts,
-    moments, acc, w0g, w1g, w2g, w0m, rest,
+    dm, nk, w0h, w1c, w1h, w2d, acc_in, edge, inv1, inv2, from_edge, rest, shared, shifts,
+    moments, acc, w0g, w1g, w2g, w0m,
 ):
     par = lax.rem(lax.axis_index("slab"), 2)
     nz, nc = dm.nz, dm.nc
     st = Steps(dm, nk, par, acc, shifts)
-    rest[...] = rest_a[...] + rest_b[...]
     at_x = {name: row + dm.rows_swap for name, row in dm.at_x.items()}
     hp = halo_planes(dm, st, (from_edge, dm.at_edge), (rest, dm.at_rest), (shared, dm.at_yz), (shared, at_x))
     acc[...] = acc_in[...]
@@ -579,7 +626,7 @@
             for k in range(nk):
                 behind.put(c, z, rhs * R[-2].get(c, z, k), k)
 
-    blocks(st.zm, dm.more, right_side)
+    blocks(st.zm, dm.more, right_side, 5 if dm.more % 40 == 0 else 1)
     st.start(hp["d3"], hp["g3"], far, half=True)
     st.apply(
         behind, [(None, far), (hp["fx2h"], W0[-1])], near, R[-2], (hp["fy2"], hp["fz2"]), half=True
@@ -647,7 +694,7 @@
                     terms = [sum(terms[n : n + 2][1:], terms[n]) for n in range(0, len(terms), 2)]
                 made[p, pl.ds(z, 8), c * LANES : (c + 1) * LANES] = terms[0]
 
-        blocks(0, nz, body)
+        blocks(0, nz, body, 2)
         layer = jnp.where(par == 0, p, nl - 1 - p)
         copy = pltpu.make_async_copy(made.at[p], out.at[layer], sems.at[p])
         copy.start()
@@ -678,20 +725,25 @@
     plane_stack = shape(nk, dm.plane, LANES)
     sums = shape(6 * nk * 8, LANES)
 
-    to_swap, to_edge, to_rest, to_in, flats, scalars = pl.pallas_call(
-        functools.partial(pack_body, dm, nk),
+    to_swap, flats, scalars = pl.pallas_call(
+        functools.partial(pack_faces_body, dm, nk),
+        out_shape=(shape(dm.rows_first, LANES), shape(4, *own), shape(nk * 8 + 8, LANES)),
+        in_specs=[vmem] * 5,
+        out_specs=(vmem,) * 3,
+        scratch_shapes=[pltpu.VMEM(own, f32)],
+        compiler_params=params(20),
+        name="pack_faces",
+    )(jnp.stack([cond_x, cond_y]), cond_z, kappa_sq, shifts[None], weights[None])
+    to_edge, to_rest, to_in, rhs = pl.pallas_call(
+        functools.partial(pack_body, dm),
         out_shape=(
-            shape(dm.rows_first, LANES), shape(dm.rows_edge, LANES), shape(dm.rows_rest, LANES),
-            shape(dm.rows_all, LANES), shape(5, *own), shape(nk * 8 + 8, LANES),
+            shape(dm.rows_edge, LANES), shape(dm.rows_rest, LANES), shape(dm.rows_all, LANES), shape(*own),
         ),
-        in_specs=[vmem] * 6,
-        out_specs=(vmem,) * 6,
-        scratch_shapes=[
-            pltpu.VMEM(own, f32),
-        ],
+        in_specs=[vmem] * 2,
+        out_specs=(vmem,) * 4,
         compiler_params=params(20),
         name="pack",
-    )(jnp.stack([cond_x, cond_y]), cond_z, kappa_sq, right_side, shifts[None], weights[None])
+    )(right_side, flats)
 
     outward = [pair for i in range(1, count - 1, 2) for pair in ((i, i + 1), (i + 1, i))]
     from_first = lax.ppermute(to_swap, "slab", outward)
@@ -722,7 +774,7 @@
         near_a_body, "near_a", 20,
         (wide(nl - 1), wide(nl - 2), wide(2), plane_stack, sums, shape(*own), wide(2), wide(nl - 2)),
         [pltpu.VMEM((2, dm.plane, LANES), f32), held(3), held(1)],
-        (flats, from_in), 6,
+        (flats, rhs, from_in), 6,
     )
     to_edge, acc = lax.optimization_barrier((to_edge, acc))
     from_edge = lax.ppermute(to_edge, "slab", outward)
@@ -739,18 +791,16 @@
         far_0_body, "far_0", 20,
         (wide(1), wide(1), wide(1), sums, shape(2, dm.plane, LANES), wide(1), plane_stack, plane_stack),
         [],
-        (flats, coef, w0a, w1a, w2a, part1, part2, acc, inv12, from_first), 2,
+        (flats, rhs, coef, w0a, w1a, w2a, part1, part2, acc, inv12, from_first), 2,
     )
     to_rest, acc = lax.optimization_barrier((to_rest, acc))
-    rest_a = lax.ppermute(to_rest, "slab", outward[0::4] + outward[1::4])
+    from_rest = lax.ppermute(to_rest, "slab", outward)
     w0h, w1c, w2c, part4, acc, inv1 = call(
         far_a_body, "far_a", 20,
         (wide(1), wide(1), wide(1), plane_stack, sums, wide(1)),
         [pltpu.VMEM((dm.plane, LANES), f32)],
         (flats, coef, w0b, w1b, w2b, part0, part3, acc, inv12, inv0, edge, from_edge), 4,
     )
-    to_rest, from_edge = lax.optimization_barrier((to_rest, from_edge))
-    rest_b = lax.ppermute(to_rest, "slab", outward[2::4] + outward[3::4])
     w2d, acc, w1h, inv2, shared = call(
         far_b_body, "far_b", 20,
         (wide(1), sums, wide(1), wide(1), shape(2 * dm.rows_swap, LANES)),
@@ -761,8 +811,8 @@
         far_c_body, "far_c", 20,
         (shape(1, LANES), sums),
         [half_stack] * 3
-        + [pltpu.VMEM((nk, dm.nc * dm.more + 2 * PAD, LANES), f32), pltpu.VMEM((dm.rows_rest, LANES), f32)],
-        (w0h, w1c, w1h, w2d, acc, edge, inv1, inv2, from_edge, rest_a, rest_b, shared), 2,
+        + [pltpu.VMEM((nk, dm.nc * dm.more + 2 * PAD, LANES), f32)],
+        (w0h, w1c, w1h, w2d, acc, edge, inv1, inv2, from_edge, from_rest, shared), 2,
     )
 
     everywhere = jnp.broadcast_to(moments[None], (count, 1, LANES))

time: 48.1 us -> 47.6 us (0.990)
  blocking collectives: 17.2 us -> 18 us
  starting transfers between devices: 6.18 us -> 5.51 us
    all_to_all x1, blocking collectives: 17.2 us -> 18 us  [on_device(): gathered = lax.all_to_all(everywhere, 'slab', 0, 0)]
    ppermute x2 -> x1, starting transfers between devices: 1.35 us -> 0.67 us  [on_device(): from_rest = lax.ppermute(to_rest, 'slab', outward)]
    pallas_call x1 -> x2, Pallas kernels: 1.43 us -> 1.46 us  [the longest x1 1.13 us: on_device(): pl.pallas_call(functools.partial(pack_faces_body, dm, nk), out_shape=(sha...]
  transfers between devices with their start and end apart: 6 -> 5, of which waited for: 1 -> 1; matrix products, arithmetic and copies ran while one was open for 0% -> 0% of each run, Pallas kernels for 32% -> 31%
where the time goes in v6:
time: 47.6 us; the launch traced here: 47.4 us
  Pallas kernels  20.2 us (42%)
  blocking collectives  18 us (38%)
  starting transfers between devices  5.51 us (12%)
  waiting for transfers between devices  2.02 us (4%)
  other arithmetic  1.36 us (3%)
    all_to_all x1, blocking collectives, on_device(): gathered = lax.all_to_all(everywhere, 'slab', 0, 0)  18 us
    pallas_call x6, Pallas kernels, call(): pl.pallas_call(functools.partial(body, dm, nk), out_shape=results, in_spe...  16.7 us
    ppermute x1, starting transfers between devices, on_device(): swap_b = lax.ppermute(swap_a, 'field', [(i, i ^ 1) for i in range(fields)])  2.96 us
    ppermute x1, waiting for transfers between devices, on_device(): from_in = lax.ppermute(to_in, 'slab', [(i, i ^ 1) for i in range(count)])  2.01 us
    pallas_call x1, Pallas kernels, on_device(): pl.pallas_call(functools.partial(combine_body, dm, nk), out_shape=jax.Sha...  1.97 us
    another operation x1, other arithmetic, on_device(): jnp.stack([cond_x, cond_y])  1.36 us
    pallas_call x1, Pallas kernels, on_device(): pl.pallas_call(functools.partial(pack_faces_body, dm, nk), out_shape=(sha...  1.13 us
  transfers between devices with their start and end apart: 5, of which 1 were waited for; matrix products, arithmetic and copies ran while one was open for 0% of the time, Pallas kernels for 31%

profile of v6, /device:TPU:0, one launch (start us, length us, event | category | flops | bytes accessed | tf_op | source)
XLA Modules:
  0.0 47.4 jit_solution(10702688431944331575)
XLA Ops:
  0.0 0.0 copy-start.3
  0.0 0.0 copy-start.4
  0.0 0.0 copy-start
  0.0 0.0 copy-start.1
  0.0 1.4 %pad_maximum_fusion.conds = f32[2,4,64,512]{3,2,1,0:T(8,128)S(1)} fusion(f32[1,4,64,512]{3,2,1,0:T(8,128)} %bitcast.8, f32[1,4,64,512]{3,2,1,0:T(8,128)} %bitcast.9), kind=kLoop, calls=%fused_computation | loop fusion | flops 262144 | bytes 2097152 | tf_op jit(solution)/shard_map/stack | solution.py:736
  1.4 0.0 copy-start.2
  1.4 0.0 copy-done.3
  1.4 0.0 copy-done.4
  1.4 0.0 copy-done
  1.4 0.1 copy-done.1
  1.5 1.1 %pack_faces.1 = (f32[800,128]{1,0:T(8,128)S(1)}, f32[4,1064,128]{2,1,0:T(8,128)S(1)}, f32[72,128]{1,0:T(8,128)S(1)}) custom-call(f32[2,4,64,512]{3,2,1,0:T(8,128)S(1)} %pad_maximum_fusion.conds, f32[4,64,512]{2,1,0:T(8,128)S(1)} %copy-done, f32[4,64,512]{2,1,0:T(8,128)S(1)} %copy-done.1, f32[1,8]{1,0:T(1,128)S(1)} %bitcast.6, f32[1,8]{1,0:T(1,128)S(1)} %bitcast.7), custom_call_target="tpu_custom_call" | custom-call | tf_op jit(solution)/shard_map/pack_faces/pallas_call | solution.py:728
  2.7 0.0 copy-done.2
  2.7 0.3 pack.1
  3.0 0.5 %collective-permute-start = (f32[2600,128]{1,0:T(8,128)S(1)}, f32[2600,128]{1,0:T(8,128)S(1)}, u32[]{:S(2)}, u32[]{:S(2)}) collective-permute-start(f32[2600,128]{1,0:T(8,128)S(1)} %get-tuple-element.51), channel_id=1, source_target_pairs={{0,1},{1,0},{2,3},{3,2},{4,5},{5,4},{6,7},{7,6},{8,9},{9,8},{10,11... | collective-permute-start | bytes 3993608 | tf_op jit(solution)/shard_map/ppermute | solution.py:750
  3.5 0.7 %collective-permute-start.1 = (f32[800,128]{1,0:T(8,128)S(1)}, f32[800,128]{1,0:T(8,128)S(1)}, u32[]{:S(2)}, u32[]{:S(2)}) collective-permute-start(f32[800,128]{1,0:T(8,128)S(1)} %get-tuple-element.64), channel_id=1, source_target_pairs={{1,2},{2,1},{3,4},{4,3},{5,6},{6,5},{7,8},{8,7},{9,10},{10,9},{11,... | collective-permute-start | bytes 1228808 | tf_op jit(solution)/shard_map/ppermute | solution.py:749
  4.2 2.0 %collective-permute-done.from_in = f32[2600,128]{1,0:T(8,128)S(1)} collective-permute-done((f32[2600,128]{1,0:T(8,128)S(1)}, f32[2600,128]{1,0:T(8,128)S(1)}, u32[]{:S(2)}, u32[]{:S(2)}) %collective-permute-start) | collective-permute-done | bytes 1331232 | tf_op jit(solution)/shard_map/ppermute | solution.py:750
  6.2 5.3 %near_a.1 = (f32[8,800,128]{2,1,0:T(8,128)S(1)}, f32[8,536,128]{2,1,0:T(8,128)S(1)}, f32[8,536,128]{2,1,0:T(8,128)S(1)}, f32[8,256,128]{2,1,0:T(8,128)S(1)}, f32...) custom-call(f32[4,1064,128]{2,1,0:T(8,128)S(1)} %get-tuple-element.49.co, ...), custom_call_target="tpu_custom_call" | custom-call | flops 1000000 | bytes 18000000 | tf_op jit(solution)/shard_map/near_a/pallas_call | solution.py:754
  11.5 0.7 %collective-permute-start.2 = (f32[768,128]{1,0:T(8,128)S(1)}, f32[768,128]{1,0:T(8,128)S(1)}, u32[]{:S(2)}, u32[]{:S(2)}) collective-permute-start(f32[768,128]{1,0:T(8,128)S(1)} %get-tuple-element.79), channel_id=1, source_target_pairs={{1,2},{2,1},{3,4},{4,3},{5,6},{6,5},{7,8},{8,7},{9,10},{10,9},{11,... | collective-permute-start | bytes 1179656 | tf_op jit(solution)/shard_map/ppermute | solution.py:780
  12.2 2.7 %near_b.1 = (f32[8,272,128]{2,1,0:T(8,128)S(1)}, f32[8,256,128]{2,1,0:T(8,128)S(1)}, f32[384,128]{1,0:T(8,128)S(1)}) custom-call(f32[4,1064,128]{2,1,0:T(8,128)S(1)} %get-tuple-element.49.coef.flats, f32[1064,128]{1,0:T(8,128)S(1)} %get-tuple-element.53.coef, f32[8,536,128]{2,1,0:T(8,128)S(1)} %get-tuple-element.55.w1a, ...), custom_call_target="tpu_custom_call" | custom-call | flops 1000000 | bytes 9000000 | tf_op jit(solution)/shard_map/near_b/pallas_call | solution.py:754
  14.9 0.0 collective-permute-done.1.from_first
  14.9 3.0 %collective-permute-start.3 = (f32[544,128]{1,0:T(8,128)S(1)}, f32[544,128]{1,0:T(8,128)S(1)}, u32[]{:S(2)}, u32[]{:S(2)}) collective-permute-start(f32[544,128]{1,0:T(8,128)S(1)} %slice.3.swap_a), channel_id=1, source_target_pairs={{0,16},{16,0},{1,17},{17,1},{2,18},{18,2},{3,19},{19,3},{4,20},{20... | collective-permute-start | bytes 835592 | tf_op jit(solution)/shard_map/ppermute | solution.py:789
  17.9 2.9 %far_0.1 = (f32[8,272,128]{2,1,0:T(8,128)S(1)}, f32[8,272,128]{2,1,0:T(8,128)S(1)}, f32[8,272,128]{2,1,0:T(8,128)S(1)}, f32[384,128]{1,0:T(8,128)S(1)}, f32[2,25...) custom-call(f32[4,1064,128]{2,1,0:T(8,128)S(1)} %get-tuple-element.49., ...), custom_call_target="tpu_custom_call" | custom-call | flops 1000000 | bytes 6000000 | tf_op jit(solution)/shard_map/far_0/pallas_call | solution.py:754
  20.8 0.7 %collective-permute-start.4 = (f32[416,128]{1,0:T(8,128)S(1)}, f32[416,128]{1,0:T(8,128)S(1)}, u32[]{:S(2)}, u32[]{:S(2)}) collective-permute-start(f32[416,128]{1,0:T(8,128)S(1)} %get-tuple-element.90), channel_id=1, source_target_pairs={{1,2},{2,1},{3,4},{4,3},{5,6},{6,5},{7,8},{8,7},{9,10},{10,9},{11,... | collective-permute-start | bytes 638984 | tf_op jit(solution)/shard_map/ppermute | solution.py:797
  21.4 0.0 collective-permute-done.2.from_edge
  21.5 2.2 %far_a.1 = (f32[8,272,128]{2,1,0:T(8,128)S(1)}, f32[8,272,128]{2,1,0:T(8,128)S(1)}, f32[8,272,128]{2,1,0:T(8,128)S(1)}, f32[8,256,128]{2,1,0:T(8,128)S(1)}, f32[...) custom-call(f32[4,1064,128]{2,1,0:T(8,128)S(1)} %get-tuple-element.49.coef.flats, f32[1064,128]{1,0:T(8,128)S(1)} %get-tuple-element.53.coef, ...), custom_call_target="tpu_custom_call" | custom-call | flops 1000000 | bytes 12000000 | tf_op jit(solution)/shard_map/far_a/pallas_call | solution.py:754
  23.6 0.0 collective-permute-done.3.swap_b
  23.6 1.9 %far_b.1 = (f32[8,272,128]{2,1,0:T(8,128)S(1)}, f32[384,128]{1,0:T(8,128)S(1)}, f32[8,272,128]{2,1,0:T(8,128)S(1)}, f32[8,272,128]{2,1,0:T(8,128)S(1)}, f32[1088,128]{1,0:T(8,128)S(1)}) custom-call(f32[4,1064,128]{2,1,0:T(8,128)S(1)} %get-tuple-element.49.coef.flats, f32[1064,128]{1,0:T(8,128)S(1)} %get-tuple-element.53.coef, ...), custom_call_target="tpu_custom_call" | custom-call | flops 1000000 | bytes 9000000 | tf_op jit(solution)/shard_map/far_b/pallas_call | solution.py:754
  25.6 0.0 collective-permute-done.4.rest
  25.6 1.8 %far_c.1 = (f32[1,128]{1,0:T(1,128)S(1)}, f32[384,128]{1,0:T(8,128)}) custom-call(f32[8,272,128]{2,1,0:T(8,128)S(1)} %get-tuple-element.80.w0h, f32[8,272,128]{2,1,0:T(8,128)S(1)} %get-tuple-element.81.w1c, f32[8,272,128]{2,1,0:T(8,128)S(1)} %get-tuple-element.86.w1h, f32[8,272,128]{2,1,0:T(8,128)S(1)} %get-tuple-element.87.w2d, ...), custom_call_target="tpu_custom_call" | custom-call | flops 1000000 | bytes 6000000 | tf_op jit(solution)/shard_map/far_c/pallas_call | solution.py:754
  27.4 18.0 %all_to_all.5.moments = f32[16,1,128]{2,1,0:T(1,128)S(1)} all-to-all(f32[16,1,128]{2,1,0:T(1,128)S(1)} %broadcast_in_dim.17), channel_id=1, replica_groups=mesh['field'=2,'slab'=16] {'slab'}, dimensions={0} | all-to-all | bytes 16384 | tf_op jit(solution)/shard_map/all_to_all | solution.py:819
  45.4 2.0 %combine.1 = f32[4,64,512]{2,1,0:T(8,128)} custom-call(f32[16,1,128]{2,1,0:T(1,128)S(1)} %all_to_all.5.moments, f32[72,128]{1,0:T(8,128)S(1)} %get-tuple-element.52.shifts.scalars, f32[8,800,128]{2,1,0:T(8,128)S(1)} %get-tuple-element.54.w0a, f32[8,272,128]{2,1,0:T(8,128)S(1)} %get-tuple-element.69.w0b, f32[8,536,128]{2,1,0:T(8,128)S(1)} %get-tuple-element.55.w1a, ...), custom_call_target="tpu_custom_call" | custom-call | tf_op jit(solution)/shard_map/combine/pallas_call | solution.py:821
  (2 shorter events, 0.0 us)
Async XLA Ops:
  0.0 1.4 %copy-start.3 = (f32[8]{0:T(128)S(1)}, f32[8]{0:T(128)}, u32[]{:S(2)}) copy-start(f32[8]{0:T(128)} %param.12) | copy-start | bytes 100
  0.0 1.4 %copy-start.4 = (f32[8]{0:T(128)S(1)}, f32[8]{0:T(128)}, u32[]{:S(2)}) copy-start(f32[8]{0:T(128)} %param.13) | copy-start | bytes 100
  0.0 1.4 %copy-start = (f32[4,64,512]{2,1,0:T(8,128)S(1)}, f32[4,64,512]{2,1,0:T(8,128)}, u32[]{:S(2)}) copy-start(f32[4,64,512]{2,1,0:T(8,128)} %cz.1) | copy-start | bytes 1572868
  0.0 1.5 %copy-start.1 = (f32[4,64,512]{2,1,0:T(8,128)S(1)}, f32[4,64,512]{2,1,0:T(8,128)}, u32[]{:S(2)}) copy-start(f32[4,64,512]{2,1,0:T(8,128)} %kappa.1) | copy-start | bytes 1572868
  1.4 1.3 %copy-start.2 = (f32[4,64,512]{2,1,0:T(8,128)S(1)}, f32[4,64,512]{2,1,0:T(8,128)}, u32[]{:S(2)}) copy-start(f32[4,64,512]{2,1,0:T(8,128)} %b.1) | copy-start | bytes 1572868
  3.0 3.2 %collective-permute-start = (f32[2600,128]{1,0:T(8,128)S(1)}, f32[2600,128]{1,0:T(8,128)S(1)}, u32[]{:S(2)}, u32[]{:S(2)}) collective-permute-start(f32[2600,128]{1,0:T(8,128)S(1)} %get-tuple-element.51), channel_id=1, source_target_pairs={{0,1},{1,0},{2,3},{3,2},{4,5},{5,4},{6,7},{7,6},{8,9},{9,8},{10,11... | collective-permute-start | bytes 3993608 | tf_op jit(solution)/shard_map/ppermute | solution.py:750
  3.5 11.3 %collective-permute-start.1 = (f32[800,128]{1,0:T(8,128)S(1)}, f32[800,128]{1,0:T(8,128)S(1)}, u32[]{:S(2)}, u32[]{:S(2)}) collective-permute-start(f32[800,128]{1,0:T(8,128)S(1)} %get-tuple-element.64), channel_id=1, source_target_pairs={{1,2},{2,1},{3,4},{4,3},{5,6},{6,5},{7,8},{8,7},{9,10},{10,9},{11,... | collective-permute-start | bytes 1228808 | tf_op jit(solution)/shard_map/ppermute | solution.py:749
  11.5 10.0 %collective-permute-start.2 = (f32[768,128]{1,0:T(8,128)S(1)}, f32[768,128]{1,0:T(8,128)S(1)}, u32[]{:S(2)}, u32[]{:S(2)}) collective-permute-start(f32[768,128]{1,0:T(8,128)S(1)} %get-tuple-element.79), channel_id=1, source_target_pairs={{1,2},{2,1},{3,4},{4,3},{5,6},{6,5},{7,8},{8,7},{9,10},{10,9},{11,... | collective-permute-start | bytes 1179656 | tf_op jit(solution)/shard_map/ppermute | solution.py:780
  14.9 8.7 %collective-permute-start.3 = (f32[544,128]{1,0:T(8,128)S(1)}, f32[544,128]{1,0:T(8,128)S(1)}, u32[]{:S(2)}, u32[]{:S(2)}) collective-permute-start(f32[544,128]{1,0:T(8,128)S(1)} %slice.3.swap_a), channel_id=1, source_target_pairs={{0,16},{16,0},{1,17},{17,1},{2,18},{18,2},{3,19},{19,3},{4,20},{20... | collective-permute-start | bytes 835592 | tf_op jit(solution)/shard_map/ppermute | solution.py:789
  20.8 4.8 %collective-permute-start.4 = (f32[416,128]{1,0:T(8,128)S(1)}, f32[416,128]{1,0:T(8,128)S(1)}, u32[]{:S(2)}, u32[]{:S(2)}) collective-permute-start(f32[416,128]{1,0:T(8,128)S(1)} %get-tuple-element.90), channel_id=1, source_target_pairs={{1,2},{2,1},{3,4},{4,3},{5,6},{6,5},{7,8},{8,7},{9,10},{10,9},{11,... | collective-permute-start | bytes 638984 | tf_op jit(solution)/shard_map/ppermute | solution.py:797

commit v7 on v6

--- a/solution.py
+++ b/solution.py
@@ -254,14 +254,16 @@
 
 
 class Steps:
-    def __init__(self, dm, nk, par, acc, shifts):
+    def __init__(self, dm, nk, par, acc, shifts, unroll=4):
+        self.unroll = unroll
         self.dm, self.nk, self.acc, self.shifts = dm, nk, acc, shifts
         self.zs = pl.multiple_of(par * dm.half, 8)
         self.zm = pl.multiple_of(par * (dm.nz - dm.more), 8)
 
-    def sweep(self, half, body, unroll=4):
+    def sweep(self, half, body, unroll=None):
+        unroll = unroll or self.unroll
         if half:
-            blocks(self.zs, self.dm.half, body, unroll)
+            blocks(self.zs, self.dm.half, body, min(unroll, 4))
         else:
             blocks(0, self.dm.nz, body, unroll)
 
@@ -275,7 +277,7 @@
     def tiles(self, plane, z, k=None, d=0):
         return [plane.get(c, z, k, d) for c in range(self.dm.nc)]
 
-    def fused(self, *bodies, unroll=4):
+    def fused(self, *bodies, unroll=None):
         def body(z):
             for one in bodies:
                 one(z)
@@ -298,7 +300,7 @@
 
         if not run:
             return body
-        self.sweep(half, body, 2)
+        self.sweep(half, body, 4)
 
     def apply(self, v, sides, out, r=None, yz=None, base=None, half=False, moment=None, run=True):
         nc = self.dm.nc
@@ -489,7 +491,7 @@
     nl, nc, nz = dm.nl, dm.nc, dm.nz
     df, raw_x, yf, zf = [own_planes(dm, flats.at[n]) for n in range(4)]
     xf = own_planes(dm, coef)
-    st = Steps(dm, nk, par, acc, shifts)
+    st = Steps(dm, nk, par, acc, shifts, 8)
     x1 = Plane(from_first, dm.at_first["x1"], nz)
     acc[...] = acc_in[...]
     for ref in (w0b, w1b, w2b):
@@ -526,7 +528,7 @@
     nl, nc, nz = dm.nl, dm.nc, dm.nz
     df, raw_x, yf, zf = [own_planes(dm, flats.at[n]) for n in range(4)]
     xf = own_planes(dm, coef)
-    st = Steps(dm, nk, par, acc, shifts)
+    st = Steps(dm, nk, par, acc, shifts, 8)
     hp = halo_planes(dm, st, (from_edge, dm.at_edge))
     acc[...] = acc_in[...]
     for ref in (w0h, w1c, w2c):

time: 47.6 us -> 47.1 us (0.989)
  Pallas kernels: 20.2 us -> 19.5 us
    pallas_call x6, Pallas kernels: 16.7 us -> 16 us  [call(): pl.pallas_call(functools.partial(body, dm, nk), out_shape=results, in_spe...]
  transfers between devices with their start and end apart: 5 -> 5, of which waited for: 1 -> 1; matrix products, arithmetic and copies ran while one was open for 0% -> 0% of each run, Pallas kernels for 31% -> 30%
where the time goes in v7:
time: 47.1 us; the launch traced here: 46.9 us
  Pallas kernels  19.5 us (41%)
  blocking collectives  18.2 us (39%)
  starting transfers between devices  5.51 us (12%)
  waiting for transfers between devices  2.02 us (4%)
  other arithmetic  1.36 us (3%)
    all_to_all x1, blocking collectives, on_device(): gathered = lax.all_to_all(everywhere, 'slab', 0, 0)  18.2 us
    pallas_call x6, Pallas kernels, call(): pl.pallas_call(functools.partial(body, dm, nk), out_shape=results, in_spe...  16 us
    ppermute x1, starting transfers between devices, on_device(): swap_b = lax.ppermute(swap_a, 'field', [(i, i ^ 1) for i in range(fields)])  2.96 us
    ppermute x1, waiting for transfers between devices, on_device(): from_in = lax.ppermute(to_in, 'slab', [(i, i ^ 1) for i in range(count)])  2.01 us
    pallas_call x1, Pallas kernels, on_device(): pl.pallas_call(functools.partial(combine_body, dm, nk), out_shape=jax.Sha...  1.97 us
    another operation x1, other arithmetic, on_device(): jnp.stack([cond_x, cond_y])  1.36 us
    pallas_call x1, Pallas kernels, on_device(): pl.pallas_call(functools.partial(pack_faces_body, dm, nk), out_shape=(sha...  1.13 us
  transfers between devices with their start and end apart: 5, of which 1 were waited for; matrix products, arithmetic and copies ran while one was open for 0% of the time, Pallas kernels for 30%

profile of v7, /device:TPU:0, one launch (start us, length us, event | category | flops | bytes accessed | tf_op | source)
XLA Modules:
  0.0 46.9 jit_solution(15129503379390232807)
XLA Ops:
  0.0 0.0 copy-start.3
  0.0 0.0 copy-start.4
  0.0 0.0 copy-start
  0.0 0.0 copy-start.1
  0.0 1.4 %pad_maximum_fusion.conds = f32[2,4,64,512]{3,2,1,0:T(8,128)S(1)} fusion(f32[1,4,64,512]{3,2,1,0:T(8,128)} %bitcast.8, f32[1,4,64,512]{3,2,1,0:T(8,128)} %bitcast.9), kind=kLoop, calls=%fused_computation | loop fusion | flops 262144 | bytes 2097152 | tf_op jit(solution)/shard_map/stack | solution.py:738
  1.4 0.0 copy-start.2
  1.4 0.0 copy-done.3
  1.4 0.0 copy-done.4
  1.4 0.0 copy-done
  1.4 0.1 copy-done.1
  1.5 1.1 %pack_faces.1 = (f32[800,128]{1,0:T(8,128)S(1)}, f32[4,1064,128]{2,1,0:T(8,128)S(1)}, f32[72,128]{1,0:T(8,128)S(1)}) custom-call(f32[2,4,64,512]{3,2,1,0:T(8,128)S(1)} %pad_maximum_fusion.conds, f32[4,64,512]{2,1,0:T(8,128)S(1)} %copy-done, f32[4,64,512]{2,1,0:T(8,128)S(1)} %copy-done.1, f32[1,8]{1,0:T(1,128)S(1)} %bitcast.6, f32[1,8]{1,0:T(1,128)S(1)} %bitcast.7), custom_call_target="tpu_custom_call" | custom-call | tf_op jit(solution)/shard_map/pack_faces/pallas_call | solution.py:730
  2.7 0.0 copy-done.2
  2.7 0.3 pack.1
  3.0 0.5 %collective-permute-start = (f32[2600,128]{1,0:T(8,128)S(1)}, f32[2600,128]{1,0:T(8,128)S(1)}, u32[]{:S(2)}, u32[]{:S(2)}) collective-permute-start(f32[2600,128]{1,0:T(8,128)S(1)} %get-tuple-element.51), channel_id=1, source_target_pairs={{0,1},{1,0},{2,3},{3,2},{4,5},{5,4},{6,7},{7,6},{8,9},{9,8},{10,11... | collective-permute-start | bytes 3993608 | tf_op jit(solution)/shard_map/ppermute | solution.py:752
  3.5 0.7 %collective-permute-start.1 = (f32[800,128]{1,0:T(8,128)S(1)}, f32[800,128]{1,0:T(8,128)S(1)}, u32[]{:S(2)}, u32[]{:S(2)}) collective-permute-start(f32[800,128]{1,0:T(8,128)S(1)} %get-tuple-element.64), channel_id=1, source_target_pairs={{1,2},{2,1},{3,4},{4,3},{5,6},{6,5},{7,8},{8,7},{9,10},{10,9},{11,... | collective-permute-start | bytes 1228808 | tf_op jit(solution)/shard_map/ppermute | solution.py:751
  4.2 2.0 %collective-permute-done.from_in = f32[2600,128]{1,0:T(8,128)S(1)} collective-permute-done((f32[2600,128]{1,0:T(8,128)S(1)}, f32[2600,128]{1,0:T(8,128)S(1)}, u32[]{:S(2)}, u32[]{:S(2)}) %collective-permute-start) | collective-permute-done | bytes 1331232 | tf_op jit(solution)/shard_map/ppermute | solution.py:752
  6.2 5.1 %near_a.1 = (f32[8,800,128]{2,1,0:T(8,128)S(1)}, f32[8,536,128]{2,1,0:T(8,128)S(1)}, f32[8,536,128]{2,1,0:T(8,128)S(1)}, f32[8,256,128]{2,1,0:T(8,128)S(1)}, f32...) custom-call(f32[4,1064,128]{2,1,0:T(8,128)S(1)} %get-tuple-element.49.co, ...), custom_call_target="tpu_custom_call" | custom-call | flops 1000000 | bytes 18000000 | tf_op jit(solution)/shard_map/near_a/pallas_call | solution.py:756
  11.4 0.7 %collective-permute-start.2 = (f32[768,128]{1,0:T(8,128)S(1)}, f32[768,128]{1,0:T(8,128)S(1)}, u32[]{:S(2)}, u32[]{:S(2)}) collective-permute-start(f32[768,128]{1,0:T(8,128)S(1)} %get-tuple-element.79), channel_id=1, source_target_pairs={{1,2},{2,1},{3,4},{4,3},{5,6},{6,5},{7,8},{8,7},{9,10},{10,9},{11,... | collective-permute-start | bytes 1179656 | tf_op jit(solution)/shard_map/ppermute | solution.py:782
  12.1 2.7 %near_b.1 = (f32[8,272,128]{2,1,0:T(8,128)S(1)}, f32[8,256,128]{2,1,0:T(8,128)S(1)}, f32[384,128]{1,0:T(8,128)S(1)}) custom-call(f32[4,1064,128]{2,1,0:T(8,128)S(1)} %get-tuple-element.49.coef.flats, f32[1064,128]{1,0:T(8,128)S(1)} %get-tuple-element.53.coef, f32[8,536,128]{2,1,0:T(8,128)S(1)} %get-tuple-element.55.w1a, ...), custom_call_target="tpu_custom_call" | custom-call | flops 1000000 | bytes 9000000 | tf_op jit(solution)/shard_map/near_b/pallas_call | solution.py:756
  14.8 0.0 collective-permute-done.1.from_first
  14.8 3.0 %collective-permute-start.3 = (f32[544,128]{1,0:T(8,128)S(1)}, f32[544,128]{1,0:T(8,128)S(1)}, u32[]{:S(2)}, u32[]{:S(2)}) collective-permute-start(f32[544,128]{1,0:T(8,128)S(1)} %slice.3.swap_a), channel_id=1, source_target_pairs={{0,16},{16,0},{1,17},{17,1},{2,18},{18,2},{3,19},{19,3},{4,20},{20... | collective-permute-start | bytes 835592 | tf_op jit(solution)/shard_map/ppermute | solution.py:791
  17.8 2.6 %far_0.1 = (f32[8,272,128]{2,1,0:T(8,128)S(1)}, f32[8,272,128]{2,1,0:T(8,128)S(1)}, f32[8,272,128]{2,1,0:T(8,128)S(1)}, f32[384,128]{1,0:T(8,128)S(1)}, f32[2,25...) custom-call(f32[4,1064,128]{2,1,0:T(8,128)S(1)} %get-tuple-element.49., ...), custom_call_target="tpu_custom_call" | custom-call | flops 1000000 | bytes 6000000 | tf_op jit(solution)/shard_map/far_0/pallas_call | solution.py:756
  20.3 0.7 %collective-permute-start.4 = (f32[416,128]{1,0:T(8,128)S(1)}, f32[416,128]{1,0:T(8,128)S(1)}, u32[]{:S(2)}, u32[]{:S(2)}) collective-permute-start(f32[416,128]{1,0:T(8,128)S(1)} %get-tuple-element.90), channel_id=1, source_target_pairs={{1,2},{2,1},{3,4},{4,3},{5,6},{6,5},{7,8},{8,7},{9,10},{10,9},{11,... | collective-permute-start | bytes 638984 | tf_op jit(solution)/shard_map/ppermute | solution.py:799
  21.0 0.0 collective-permute-done.2.from_edge
  21.0 2.0 %far_a.1 = (f32[8,272,128]{2,1,0:T(8,128)S(1)}, f32[8,272,128]{2,1,0:T(8,128)S(1)}, f32[8,272,128]{2,1,0:T(8,128)S(1)}, f32[8,256,128]{2,1,0:T(8,128)S(1)}, f32[...) custom-call(f32[4,1064,128]{2,1,0:T(8,128)S(1)} %get-tuple-element.49.coef.flats, f32[1064,128]{1,0:T(8,128)S(1)} %get-tuple-element.53.coef, ...), custom_call_target="tpu_custom_call" | custom-call | flops 1000000 | bytes 12000000 | tf_op jit(solution)/shard_map/far_a/pallas_call | solution.py:756
  23.0 0.0 collective-permute-done.3.swap_b
  23.0 1.9 %far_b.1 = (f32[8,272,128]{2,1,0:T(8,128)S(1)}, f32[384,128]{1,0:T(8,128)S(1)}, f32[8,272,128]{2,1,0:T(8,128)S(1)}, f32[8,272,128]{2,1,0:T(8,128)S(1)}, f32[1088,128]{1,0:T(8,128)S(1)}) custom-call(f32[4,1064,128]{2,1,0:T(8,128)S(1)} %get-tuple-element.49.coef.flats, f32[1064,128]{1,0:T(8,128)S(1)} %get-tuple-element.53.coef, ...), custom_call_target="tpu_custom_call" | custom-call | flops 1000000 | bytes 9000000 | tf_op jit(solution)/shard_map/far_b/pallas_call | solution.py:756
  24.9 0.0 collective-permute-done.4.rest
  24.9 1.8 %far_c.1 = (f32[1,128]{1,0:T(1,128)S(1)}, f32[384,128]{1,0:T(8,128)}) custom-call(f32[8,272,128]{2,1,0:T(8,128)S(1)} %get-tuple-element.80.w0h, f32[8,272,128]{2,1,0:T(8,128)S(1)} %get-tuple-element.81.w1c, f32[8,272,128]{2,1,0:T(8,128)S(1)} %get-tuple-element.86.w1h, f32[8,272,128]{2,1,0:T(8,128)S(1)} %get-tuple-element.87.w2d, ...), custom_call_target="tpu_custom_call" | custom-call | flops 1000000 | bytes 6000000 | tf_op jit(solution)/shard_map/far_c/pallas_call | solution.py:756
  26.7 18.2 %all_to_all.5.moments = f32[16,1,128]{2,1,0:T(1,128)S(1)} all-to-all(f32[16,1,128]{2,1,0:T(1,128)S(1)} %broadcast_in_dim.17), channel_id=1, replica_groups=mesh['field'=2,'slab'=16] {'slab'}, dimensions={0} | all-to-all | bytes 16384 | tf_op jit(solution)/shard_map/all_to_all | solution.py:821
  44.9 2.0 %combine.1 = f32[4,64,512]{2,1,0:T(8,128)} custom-call(f32[16,1,128]{2,1,0:T(1,128)S(1)} %all_to_all.5.moments, f32[72,128]{1,0:T(8,128)S(1)} %get-tuple-element.52.shifts.scalars, f32[8,800,128]{2,1,0:T(8,128)S(1)} %get-tuple-element.54.w0a, f32[8,272,128]{2,1,0:T(8,128)S(1)} %get-tuple-element.69.w0b, f32[8,536,128]{2,1,0:T(8,128)S(1)} %get-tuple-element.55.w1a, ...), custom_call_target="tpu_custom_call" | custom-call | tf_op jit(solution)/shard_map/combine/pallas_call | solution.py:823
  (2 shorter events, 0.0 us)
Async XLA Ops:
  0.0 1.4 %copy-start.3 = (f32[8]{0:T(128)S(1)}, f32[8]{0:T(128)}, u32[]{:S(2)}) copy-start(f32[8]{0:T(128)} %param.12) | copy-start | bytes 100
  0.0 1.4 %copy-start.4 = (f32[8]{0:T(128)S(1)}, f32[8]{0:T(128)}, u32[]{:S(2)}) copy-start(f32[8]{0:T(128)} %param.13) | copy-start | bytes 100
  0.0 1.4 %copy-start = (f32[4,64,512]{2,1,0:T(8,128)S(1)}, f32[4,64,512]{2,1,0:T(8,128)}, u32[]{:S(2)}) copy-start(f32[4,64,512]{2,1,0:T(8,128)} %cz.1) | copy-start | bytes 1572868
  0.0 1.5 %copy-start.1 = (f32[4,64,512]{2,1,0:T(8,128)S(1)}, f32[4,64,512]{2,1,0:T(8,128)}, u32[]{:S(2)}) copy-start(f32[4,64,512]{2,1,0:T(8,128)} %kappa.1) | copy-start | bytes 1572868
  1.4 1.3 %copy-start.2 = (f32[4,64,512]{2,1,0:T(8,128)S(1)}, f32[4,64,512]{2,1,0:T(8,128)}, u32[]{:S(2)}) copy-start(f32[4,64,512]{2,1,0:T(8,128)} %b.1) | copy-start | bytes 1572868
  3.0 3.2 %collective-permute-start = (f32[2600,128]{1,0:T(8,128)S(1)}, f32[2600,128]{1,0:T(8,128)S(1)}, u32[]{:S(2)}, u32[]{:S(2)}) collective-permute-start(f32[2600,128]{1,0:T(8,128)S(1)} %get-tuple-element.51), channel_id=1, source_target_pairs={{0,1},{1,0},{2,3},{3,2},{4,5},{5,4},{6,7},{7,6},{8,9},{9,8},{10,11... | collective-permute-start | bytes 3993608 | tf_op jit(solution)/shard_map/ppermute | solution.py:752
  3.5 11.2 %collective-permute-start.1 = (f32[800,128]{1,0:T(8,128)S(1)}, f32[800,128]{1,0:T(8,128)S(1)}, u32[]{:S(2)}, u32[]{:S(2)}) collective-permute-start(f32[800,128]{1,0:T(8,128)S(1)} %get-tuple-element.64), channel_id=1, source_target_pairs={{1,2},{2,1},{3,4},{4,3},{5,6},{6,5},{7,8},{8,7},{9,10},{10,9},{11,... | collective-permute-start | bytes 1228808 | tf_op jit(solution)/shard_map/ppermute | solution.py:751
  11.4 9.6 %collective-permute-start.2 = (f32[768,128]{1,0:T(8,128)S(1)}, f32[768,128]{1,0:T(8,128)S(1)}, u32[]{:S(2)}, u32[]{:S(2)}) collective-permute-start(f32[768,128]{1,0:T(8,128)S(1)} %get-tuple-element.79), channel_id=1, source_target_pairs={{1,2},{2,1},{3,4},{4,3},{5,6},{6,5},{7,8},{8,7},{9,10},{10,9},{11,... | collective-permute-start | bytes 1179656 | tf_op jit(solution)/shard_map/ppermute | solution.py:782
  14.8 8.2 %collective-permute-start.3 = (f32[544,128]{1,0:T(8,128)S(1)}, f32[544,128]{1,0:T(8,128)S(1)}, u32[]{:S(2)}, u32[]{:S(2)}) collective-permute-start(f32[544,128]{1,0:T(8,128)S(1)} %slice.3.swap_a), channel_id=1, source_target_pairs={{0,16},{16,0},{1,17},{17,1},{2,18},{18,2},{3,19},{19,3},{4,20},{20... | collective-permute-start | bytes 835592 | tf_op jit(solution)/shard_map/ppermute | solution.py:791
  20.3 4.6 %collective-permute-start.4 = (f32[416,128]{1,0:T(8,128)S(1)}, f32[416,128]{1,0:T(8,128)S(1)}, u32[]{:S(2)}, u32[]{:S(2)}) collective-permute-start(f32[416,128]{1,0:T(8,128)S(1)} %get-tuple-element.90), channel_id=1, source_target_pairs={{1,2},{2,1},{3,4},{4,3},{5,6},{6,5},{7,8},{8,7},{9,10},{10,9},{11,... | collective-permute-start | bytes 638984 | tf_op jit(solution)/shard_map/ppermute | solution.py:799
